TPU v7x, 512 devices: a whole 4x8x8 slice. The times are simulated.
512 devices in a mesh: rows: 64 (over y, z_lo, core), cols: 8 (over x, z_hi).
Axes of the slice: x: 4, y: 8, z: 8 (z_hi: 2, z_lo: 4; z = z_hi * 4 + z_lo), core: 2. Of those that a mesh axis runs over, the one named last changes fastest.
Arguments:
- grad_out: bfloat16 [65536, 256], P(('rows', 'cols')), may hold values from -6 to 6
- mask_top: int32 [65536, 256], P(('rows', 'cols')), may hold values 0 or 1
- mask_mid: int32 [65536, 256], P(('rows', 'cols')), may hold values 0 or 1
- feats_in: bfloat16 [65536, 256], P(('rows', 'cols')), may hold values from -6 to 6
- feats_mid: bfloat16 [65536, 256], P(('rows', 'cols')), may hold values from -6 to 6
- weight_first: bfloat16 [256, 256], replicated, may hold values from -0.375 to 0.375
- weight_second: bfloat16 [256, 256], replicated, may hold values from -0.375 to 0.375
- adj_blocks: bfloat16 [512, 8, 12, 128, 128], P('rows', 'cols'), may hold values from -0.3125 to 0.3125
- block_cols: int32 [512, 8, 12], P('rows', 'cols'), may hold values from 0 to 63
- block_counts: int32 [512, 8], P('rows', 'cols'), may hold values from 1 to 12, as said below
Outputs:
- grad_in: bfloat16 [65536, 256], P(('rows', 'cols'))
- grad_first: float32 [256, 256], replicated
- grad_second: float32 [256, 256], replicated
Inputs may be any that keep to these rules, and one draw needn't show every extreme that they name: `block_counts`: in some row group (the 8 row blocks held by one device index along rows) the counts run higher than in others; some entry equals 12.
All inputs are finite; a program needn't handle non-finite values. No bound on the sum of `mask_top` or of `mask_mid` on one device may be relied on, other than what follows from the above.
Results may differ from a plain program's by a relative error of at most 0.0075.
Values may be sent and summed in bfloat16 or wider, within the bound.
No kernel may reach another device: no remote copies, remote signals or barrier semaphores. Data moves between devices by JAX's collectives and lax.ppermute only.
A program may use at most 64 MiB of HBM per device.

v0:
```python
import jax
import jax.numpy as jnp
from jax import lax
from jax.sharding import PartitionSpec as P


def apply_blocks(values, adj_blocks, block_cols, block_counts):
    block_size = adj_blocks.shape[-1]
    features = values.shape[1]
    slots = adj_blocks.shape[2]
    node_blocks = values.reshape(-1, block_size, features)
    targets = block_cols[:, 0, :]
    live_slot = jnp.arange(slots, dtype=jnp.int32)[None, :] < block_counts
    local_adj = adj_blocks[:, 0]
    gathered = lax.all_gather(node_blocks, "rows", axis=0, tiled=True)
    chosen = gathered[targets]
    chosen = jnp.where(live_slot[:, :, None, None], chosen, jnp.zeros_like(chosen))
    partial_value = jnp.einsum(
        "ikab,ikbf->iaf", local_adj, chosen, preferred_element_type=jnp.float32
    )
    summed = lax.psum_scatter(
        partial_value.reshape(-1, features), "cols", scatter_dimension=0, tiled=True
    )
    return summed.astype(jnp.bfloat16)


def weight_term(features_rows, aggregated):
    return lax.dot_general(
        features_rows, aggregated, (((0,), (0,)), ((), ())), preferred_element_type=jnp.float32
    )


def times_transpose(aggregated, weight):
    return lax.dot_general(
        aggregated, weight, (((1,), (1,)), ((), ())), preferred_element_type=jnp.float32
    )


def total_weight(term):
    return lax.psum(term, ("rows", "cols"))


def local(
    grad_out,
    mask_top,
    mask_mid,
    feats_in,
    feats_mid,
    weight_first,
    weight_second,
    adj_blocks,
    block_cols,
    block_counts,
):
    node_count = grad_out.shape[0] * lax.axis_size("rows") * lax.axis_size("cols")
    norm_scale = 1.0 / jnp.sqrt(jnp.float32(node_count))
    grad_top = jnp.where(mask_top > 0, grad_out, jnp.zeros_like(grad_out))
    agg_top = apply_blocks(grad_top, adj_blocks, block_cols, block_counts)
    term_second = weight_term(feats_mid, agg_top)
    grad_second = total_weight(term_second) * norm_scale
    hidden_grad = times_transpose(agg_top, weight_second)
    grad_mid = jnp.where(mask_mid > 0, hidden_grad, jnp.zeros_like(hidden_grad)).astype(
        jnp.bfloat16
    )
    agg_mid = apply_blocks(grad_mid, adj_blocks, block_cols, block_counts)
    term_first = weight_term(feats_in, agg_mid)
    grad_first = total_weight(term_first) * norm_scale
    grad_in = times_transpose(agg_mid, weight_first).astype(jnp.bfloat16)
    return (grad_in, grad_first, grad_second)


def solution(mesh):
    return jax.shard_map(
        local,
        mesh=mesh,
        in_specs=(
            P(("rows", "cols"), None),
            P(("rows", "cols"), None),
            P(("rows", "cols"), None),
            P(("rows", "cols"), None),
            P(("rows", "cols"), None),
            P(),
            P(),
            P("rows", "cols", None, None, None),
            P("rows", "cols", None),
            P("rows", "cols"),
        ),
        out_specs=(P(("rows", "cols"), None), P(), P()),
        check_vma=False,
    )
```

profile of v0, /device:TPU:1, one launch (start us, length us, event | category | flops | bytes accessed | tf_op | source)
XLA Modules:
  0.0 745.3 jit_solution(1772348487100562795)
XLA Ops:
  7.2 1.7 compare_select_fusion
  9.0 0.0 reduce-scatter.3.cloned.1.call-start
  9.0 0.7 compare_select_fusion.1
  9.7 0.1 reshape.74
  9.8 0.7 iota_compare_fusion
  10.5 126.6 %all-gather.5.cloned.1.call-done = bf16[8192,256]{1,0:T(8,128)(2,1)} async-done(((bf16[128,256]{1,0:T(8,128)(2,1)}), bf16[8192,256]{1,0:T(8,128)(2,1)}) %all-gather.5.cloned.1.call-update) | async-done | bytes 4194320 | tf_op jit(solution)/shard_map/all_gather | solution.py:15
  137.2 8.2 %gather_fusion = bf16[96,128,256]{2,1,0:T(8,128)(2,1)} fusion(bf16[64,128,256]{2,1,0:T(8,128)(2,1)} %bitcast.33, s32[1024]{0:T(1024)S(1)} %pad_clamp_fusion), kind=kCustom, calls=%fused_computation | custom fusion | bytes 12583296 | tf_op jit(solution)/shard_map/gather | solution.py:16
  145.4 5.0 fusion.2
  150.5 0.0 all-gather.7.cloned.1.call-start
  150.5 88.5 %reduce-scatter.3.cloned.1.call-done = f32[128,256]{1,0:T(8,128)} async-done(((f32[1024,256]{1,0:T(8,128)}), f32[128,256]{1,0:T(8,128)}) %reduce-scatter.3.cloned.1.call-update) | async-done | bytes 131088 | tf_op jit(solution)/shard_map/reduce_scatter | solution.py:21
  239.0 1.7 fusion.10
  240.8 0.0 reduce-scatter.5.cloned.1.call-start
  240.8 119.1 %all-gather.7.cloned.1.call-done = bf16[8192,256]{1,0:T(8,128)(2,1)} async-done(((bf16[128,256]{1,0:T(8,128)(2,1)}), bf16[8192,256]{1,0:T(8,128)(2,1)}) %all-gather.7.cloned.1.call-update) | async-done | bytes 4194320 | tf_op jit(solution)/shard_map/all_gather | solution.py:15
  359.9 8.2 %gather_fusion.1 = bf16[96,128,256]{2,1,0:T(8,128)(2,1)} fusion(bf16[64,128,256]{2,1,0:T(8,128)(2,1)} %bitcast.34, s32[1024]{0:T(1024)S(1)} %pad_clamp_fusion), kind=kCustom, calls=%fused_computation.1 | custom fusion | bytes 12583296 | tf_op jit(solution)/shard_map/gather | solution.py:16
  368.1 5.0 fusion
  373.2 0.0 all-reduce.3.cloned.1.call-start
  373.3 0.9 convolution_bitcast_fusion
  374.2 87.6 %reduce-scatter.5.cloned.1.call-done = f32[128,256]{1,0:T(8,128)} async-done(((f32[1024,256]{1,0:T(8,128)}), f32[128,256]{1,0:T(8,128)}) %reduce-scatter.5.cloned.1.call-update) | async-done | bytes 131088 | tf_op jit(solution)/shard_map/reduce_scatter | solution.py:21
  461.8 1.8 convolution_bitcast_fusion.1
  463.7 1.7 convolution_convert_fusion
  465.4 269.0 %all-reduce.3.cloned.1.call-done = (f32[256,256]{0,1:T(8,128)}, f32[256,256]{0,1:T(8,128)}) async-done(((f32[256,256]{0,1:T(8,128)}, f32[256,256]{0,1:T(8,128)}), (f32[256,256]{0,1:T(8,128)}, f32[256,256]{0,1:T(8,128)})) %all-reduce.3.cloned.1.call-update) | async-done | bytes 524304 | tf_op jit(solution)/shard_map/psum | solution.py:40
  734.4 1.8 broadcast_multiply_fusion
  736.1 1.8 copy.13
  737.9 0.8 copy.14
  (21 shorter events, 0.2 us)
Async XLA Ops:
  7.2 138.2 %copy-start = (bf16[8,1,12,128,128]{4,3,2,1,0:T(8,128)(2,1)S(1)}, bf16[8,1,12,128,128]{4,3,2,1,0:T(8,128)(2,1)}, u32[]{:S(2)}) copy-start(bf16[8,1,12,128,128]{4,3,2,1,0:T(8,128)(2,1)} %param.17) | copy-start | bytes 9437188
  7.2 130.0 %all-gather.5.cloned.1.call-start = ((), (), s32[]{:S(2)}) async-start(), calls=%async_computation.4 | async-start | bytes 4259840 | tf_op jit(solution)/shard_map/all_gather | solution.py:15
  9.0 230.0 %reduce-scatter.3.cloned.1.call-start = ((), (), s32[]{:S(2)}) async-start(), calls=%async_computation.2 | async-start | bytes 1179648 | tf_op jit(solution)/shard_map/reduce_scatter | solution.py:21
  145.4 93.6 %copy-start.2 = (bf16[256,256]{1,0:T(8,128)(2,1)S(1)}, bf16[256,256]{1,0:T(8,128)(2,1)}, u32[]{:S(2)}) copy-start(bf16[256,256]{1,0:T(8,128)(2,1)} %param.16) | copy-start | bytes 393220
  145.4 93.6 %copy-start.3 = (s32[128,256]{1,0:T(8,128)S(1)}, s32[128,256]{1,0:T(8,128)}, u32[]{:S(2)}) copy-start(s32[128,256]{1,0:T(8,128)} %param.12) | copy-start | bytes 393220
  150.5 209.4 %all-gather.7.cloned.1.call-start = ((), (), s32[]{:S(2)}) async-start(), calls=%async_computation.5 | async-start | bytes 4259840 | tf_op jit(solution)/shard_map/all_gather | solution.py:15
  240.8 221.1 %reduce-scatter.5.cloned.1.call-start = ((), (), s32[]{:S(2)}) async-start(), calls=%async_computation.3 | async-start | bytes 1179648 | tf_op jit(solution)/shard_map/reduce_scatter | solution.py:21
  368.1 5.1 copy-start.1
  368.1 5.1 copy-start.5
  368.1 93.7 %copy-start.6 = (bf16[128,256]{1,0:T(8,128)(2,1)S(1)}, bf16[128,256]{1,0:T(8,128)(2,1)}, u32[]{:S(2)}) copy-start(bf16[128,256]{1,0:T(8,128)(2,1)} %param.13) | copy-start | bytes 196612
  368.1 95.5 %copy-start.4 = (bf16[256,256]{1,0:T(8,128)(2,1)S(1)}, bf16[256,256]{1,0:T(8,128)(2,1)}, u32[]{:S(2)}) copy-start(bf16[256,256]{1,0:T(8,128)(2,1)} %param.15) | copy-start | bytes 393220
  373.2 361.2 %all-reduce.3.cloned.1.call-start = ((), (), s32[]{:S(2)}) async-start(), calls=%async_computation.6 | async-start | bytes 1048576 | tf_op jit(solution)/shard_map/psum | solution.py:40
Sparse Core Ops, SparseCore 0:
  10.7 126.4 all-gather.4
  150.6 88.3 reduce-scatter.2
  241.9 117.9 all-gather.6
  373.3 88.4 reduce-scatter.4
  467.4 266.9 all-reduce.2
where the time goes:
time: 746 us; the launch traced here: 745 us
  waiting for transfers between devices  691 us (93%)
  local copies, waits for them, and re-layouts  19.2 us (3%)
  matrix products  16.3 us (2%)
  between operations  13.8 us (2%)
    psum x1, waiting for transfers between devices, total_weight(): return lax.psum(term, ('rows', 'cols'))  269 us
    all_gather x2, waiting for transfers between devices, apply_blocks(): gathered = lax.all_gather(node_blocks, 'rows', axis=0, tiled=True)  246 us
    reduce_scatter x2, waiting for transfers between devices, apply_blocks(): lax.psum_scatter(partial_value.reshape(-1, features), 'cols', scatter_dim...  176 us
    gather x2, local copies, waits for them, and re-layouts, apply_blocks(): chosen = gathered[targets]  16.4 us
  transfers between devices with their start and end apart: 5, of which 5 were waited for; matrix products, arithmetic and copies ran while one was open for 1% of the time, Pallas kernels for 0%

commit v1 on v0

v1 whole, which is shorter than its diff:
```python
import jax
import jax.numpy as jnp
import numpy as np
from jax import lax
from jax.experimental import pallas as pl
from jax.experimental.pallas import tpu as pltpu
from jax.sharding import Mesh, PartitionSpec as P

Y, ZL, CORE, X, ZH = 8, 4, 2, 4, 2
AXES = ("y", "zl", "core", "x", "zh")
ROWS = ("y", "zl", "core")
COLS = ("x", "zh")
NCOL = X * ZH
BF16, F32 = jnp.bfloat16, jnp.float32


def everyone(value, axes, count):
    return lax.all_to_all(
        jnp.broadcast_to(value[None], (count,) + value.shape), axes, 0, 0, tiled=True
    )


def spmm_kernel(meta_ref, core_ref, x_ref, own_ref, other_ref, out_ref):
    core = core_ref[0]
    slots = own_ref.shape[1]
    group = 4
    for side, adj_ref in ((0, own_ref), (1, other_ref)):
        j = jnp.bitwise_xor(core, side)
        for i in range(own_ref.shape[0]):
            base = (j * own_ref.shape[0] + i) * 16
            count = meta_ref[base + slots]

            def step(s, acc, base=base, count=count, i=i, adj_ref=adj_ref):
                for t in range(group):
                    k = s * group + t
                    block = x_ref[meta_ref[base + k]]
                    block = jnp.where(k < count, block, jnp.zeros_like(block))
                    acc = acc + jnp.dot(adj_ref[i, k], block, preferred_element_type=F32)
                return acc

            acc = lax.fori_loop(
                0, (count + group - 1) // group, step, jnp.zeros(out_ref.shape[2:], F32)
            )
            out_ref[i, j] = acc.astype(out_ref.dtype)


def spmm(meta, core, gathered, own, other):
    vmem = pl.BlockSpec(memory_space=pltpu.VMEM)
    smem = pl.BlockSpec(memory_space=pltpu.SMEM)
    return pl.pallas_call(
        spmm_kernel,
        out_shape=jax.ShapeDtypeStruct((NCOL, CORE) + gathered.shape[1:], BF16),
        in_specs=[smem, smem, vmem, vmem, vmem],
        out_specs=vmem,
        compiler_params=pltpu.CompilerParams(vmem_limit_bytes=40 * 1024 * 1024),
    )(meta, core, gathered, own, other)


def contract_rows(a, b):
    return lax.dot_general(a, b, (((0,), (0,)), ((), ())), preferred_element_type=F32)


def times_transpose(a, b):
    return lax.dot_general(a, b, (((1,), (1,)), ((), ())), preferred_element_type=F32)


def local(
    grad_out, mask_top, mask_mid, feats_in, feats_mid, weight_first, weight_second,
    adj_blocks, block_cols, block_counts,
):
    bs, feats = grad_out.shape
    half = feats // CORE
    core = lax.axis_index("core")
    nodes = bs * Y * ZL * CORE * X * ZH
    norm_scale = 1.0 / jnp.sqrt(F32(nodes))

    def my_half(v):
        return lax.dynamic_slice_in_dim(v, core * half, half, axis=v.ndim - 1)

    adj = adj_blocks[:, 0]
    other_adj = lax.ppermute(adj, "core", [(0, 1), (1, 0)])
    meta = jnp.concatenate(
        [block_cols[:, 0], block_counts, jnp.zeros((NCOL, 16 - 13), jnp.int32)], axis=1
    )
    meta = lax.all_gather(meta, "core", axis=0, tiled=True).reshape(-1)
    core_id = core.astype(jnp.int32).reshape(1)

    with jax.named_scope("pair_inputs"):
        grad_top = jnp.where(mask_top > 0, grad_out, jnp.zeros_like(grad_out))
        pair = lax.all_gather(
            jnp.stack([grad_top, mask_mid.astype(BF16), feats_mid]), "core", axis=0
        )
        unit_top = my_half(pair[:, 0]).reshape(CORE * bs, half)
        mask_pair = my_half(pair[:, 1]).reshape(CORE * bs, half)
        feats_mid_pair = pair[:, 2].reshape(CORE * bs, feats)
    with jax.named_scope("group_feats"):
        feats_in_group = lax.all_gather(feats_in, ("x", "zh", "core"), axis=0, tiled=True)

    def gather_units(unit):
        return everyone(unit, ("y", "zl"), Y * ZL).reshape(-1, bs, half)

    with jax.named_scope("section_top"):
        partial_top = spmm(meta, core_id, gather_units(unit_top), adj, other_adj)
        parts = lax.all_to_all(
            partial_top.reshape(NCOL, CORE * bs, half), COLS, 0, 0, tiled=True
        )
        agg_top = jnp.sum(parts.astype(F32), axis=0).astype(BF16)
        agg_top_both = lax.all_gather(agg_top, "core", axis=1, tiled=True)
        term_second = contract_rows(feats_mid_pair, agg_top)
        weight_half = lax.dynamic_slice_in_dim(weight_second, core * half, half, axis=0)
        hidden = times_transpose(agg_top_both, weight_half)
        grad_mid = jnp.where(mask_pair > 0, hidden, jnp.zeros_like(hidden)).astype(BF16)
    with jax.named_scope("section_mid"):
        partial_mid = spmm(meta, core_id, gather_units(grad_mid), adj, other_adj)
        term_first = contract_rows(feats_in_group, partial_mid.reshape(-1, half))
        terms = jnp.stack([term_first, term_second]).astype(BF16)
        terms = terms.reshape(2, NCOL, feats // NCOL, half).transpose(1, 0, 2, 3)
        sent = jnp.concatenate(
            [partial_mid.reshape(NCOL, CORE * bs, half), terms.reshape(NCOL, -1, half)], axis=1
        )
        parts = lax.all_to_all(sent, COLS, 0, 0, tiled=True)
        summed = jnp.sum(parts.astype(F32), axis=0)
        agg_mid = summed[: CORE * bs].astype(BF16)
        own_nodes = lax.all_gather(agg_mid, "core", axis=1, tiled=True)
        own_nodes = lax.dynamic_slice_in_dim(own_nodes, core * bs, bs, axis=0)
        grad_in = times_transpose(own_nodes, weight_first).astype(BF16)
    with jax.named_scope("weight_sums"):
        piece = summed[CORE * bs :]
        over_z = everyone(piece.astype(BF16), ("zh", "zl"), ZH * ZL)
        piece = jnp.sum(over_z.reshape((ZH, ZL) + piece.shape).astype(F32), axis=1)
        over_y = everyone(piece.astype(BF16), "y", Y)
        piece = jnp.sum(over_y.reshape((Y,) + piece.shape).astype(F32), axis=0)
        over_x = everyone(piece, "x", X).reshape(NCOL, 2, feats // NCOL, half)
        whole = lax.all_gather(over_x * norm_scale, "core", axis=3, tiled=True)
        whole = whole.transpose(1, 0, 2, 3).reshape(2, feats, feats)
    return (grad_in, whole[0], whole[1])


def solution(mesh):
    parts = Mesh(mesh.devices.reshape(Y, ZL, CORE, X, ZH), AXES)
    nodes = P(AXES, None)
    return jax.shard_map(
        local,
        mesh=parts,
        in_specs=(
            nodes, nodes, nodes, nodes, nodes, P(), P(),
            P(ROWS, COLS, None, None, None),
            P(ROWS, COLS, None),
            P(ROWS, COLS),
        ),
        out_specs=(nodes, P(), P()),
        check_vma=False,
    )
```

time: 746 us -> 287 us (0.38)
  waiting for transfers between devices: 691 us -> 135 us
  blocking collectives: 0 us -> 67.2 us
  starting transfers between devices: 0.21 us -> 42.2 us
  matrix products: 16.3 us -> 3 us
  Pallas kernels: 0 us -> 11.3 us
  local copies, waits for them, and re-layouts: 19.2 us -> 9.66 us
    psum x1 -> x0, waiting for transfers between devices: 269 us -> none  [total_weight(): return lax.psum(term, ('rows', 'cols'))]
    all_gather x2 -> x1, waiting for transfers between devices: 246 us -> 25.4 us  [local(): lax.all_gather(feats_in, ('x', 'zh', 'core'), axis=0, tiled=True)]
    reduce_scatter x2 -> x0, waiting for transfers between devices: 176 us -> none  [apply_blocks(): lax.psum_scatter(partial_value.reshape(-1, features), 'cols', scatter_dim...]
    all_to_all x0 -> x5, waiting for transfers between devices: none -> 109 us  [the longest x4 97.1 us: everyone(): lax.all_to_all(jnp.broadcast_to(value[None], (count,) + value.shape), axe...]
    all_to_all x0 -> x5, starting transfers between devices: none -> 39.6 us  [the longest x4 29.9 us: everyone(): lax.all_to_all(jnp.broadcast_to(value[None], (count,) + value.shape), axe...]
    all_to_all x0 -> x2, blocking collectives: none -> 35.9 us  [the longest x1 19 us: local(): parts = lax.all_to_all(sent, COLS, 0, 0, tiled=True)]
    all_gather x0 -> x5, blocking collectives: none -> 31.2 us  [the longest x1 8.6 us: local(): lax.all_gather(jnp.stack([grad_top, mask_mid.astype(BF16), feats_mid]), '...]
    gather x2 -> x0, local copies, waits for them, and re-layouts: 16.4 us -> none  [apply_blocks(): chosen = gathered[targets]]
  transfers between devices with their start and end apart: 5 -> 7, of which waited for: 5 -> 6; matrix products, arithmetic and copies ran while one was open for 1% -> 1% of each run, Pallas kernels for 0% -> 2%
where the time goes in v1:
time: 287 us
  waiting for transfers between devices  135 us (47%)
  blocking collectives  67.2 us (23%)
  starting transfers between devices  42.2 us (15%)
  between operations  14.3 us (5%)
  Pallas kernels  11.3 us (4%)
  local copies, waits for them, and re-layouts  9.66 us (3%)
  other arithmetic  4.23 us (1%)
  matrix products  3 us (1%)
    all_to_all x4, waiting for transfers between devices, everyone(): lax.all_to_all(jnp.broadcast_to(value[None], (count,) + value.shape), axe...  97.1 us
    all_to_all x4, starting transfers between devices, everyone(): lax.all_to_all(jnp.broadcast_to(value[None], (count,) + value.shape), axe...  29.9 us
    all_gather x1, waiting for transfers between devices, local(): lax.all_gather(feats_in, ('x', 'zh', 'core'), axis=0, tiled=True)  25.4 us
    all_to_all x1, blocking collectives, local(): parts = lax.all_to_all(sent, COLS, 0, 0, tiled=True)  19 us
    all_to_all x1, blocking collectives, everyone(): lax.all_to_all(jnp.broadcast_to(value[None], (count,) + value.shape), axe...  16.9 us
    all_to_all x1, waiting for transfers between devices, local(): lax.all_to_all(partial_top.reshape(NCOL, CORE * bs, half), COLS, 0, 0, ti...  11.5 us
    pallas_call x2, Pallas kernels, spmm(): pl.pallas_call(spmm_kernel, out_shape=jax.ShapeDtypeStruct((NCOL, CORE) +...  11.3 us
    all_to_all x1, starting transfers between devices, local(): lax.all_to_all(partial_top.reshape(NCOL, CORE * bs, half), COLS, 0, 0, ti...  9.77 us
  transfers between devices with their start and end apart: 7, of which 6 were waited for; matrix products, arithmetic and copies ran while one was open for 1% of the time, Pallas kernels for 2%

profile of v1, /device:TPU:1, one launch (start us, length us, event | category | flops | bytes accessed | tf_op | source)
XLA Modules:
  0.0 286.6 jit_solution(11429448420682365258)
XLA Ops:
  10.0 8.6 %all-gather = bf16[6,128,256]{2,1,0:T(8,128)(2,1)S(1)} all-gather(bf16[3,128,256]{2,1,0:T(8,128)(2,1)S(1)} %pad_maximum_fusion.1), channel_id=2, replica_groups=mesh['y'=8,'zl'=4,'core'=2,'x'=4,'zh'=2] {'core'}, dimensions={0}, use_global_device_ids=true | all-gather | bytes 589824 | tf_op jit(solution)/shard_map/pair_inputs/all_gather | solution.py:90
  19.3 1.8 broadcast_in_dim.18
  21.1 7.7 %all-to-all-start = ((bf16[32,256,128]{2,1,0:T(8,128)(2,1)}), bf16[32,256,128]{2,1,0:T(8,128)(2,1)}, u32[]{:S(2)}, u32[]{:S(2)}) async-start(bf16[32,256,128]{2,1,0:T(8,128)(2,1)} %broadcast_in_dim.18), calls=%async_computation | async-start | bytes 4194304 | tf_op jit(solution)/shard_map/section_top/all_to_all | solution.py:18
  28.8 2.6 collective-permute-start
  31.6 5.0 %all_gather.21 = s32[16,16]{1,0:T(8,128)S(1)} all-gather(s32[8,16]{1,0:T(8,128)S(1)} %add_add_fusion), channel_id=1, replica_groups=mesh['y'=8,'zl'=4,'core'=2,'x'=4,'zh'=2] {'core'}, dimensions={0}, use_global_device_ids=true | all-gather | bytes 1536 | tf_op jit(solution)/shard_map/all_gather | solution.py:85
  36.7 40.8 %all-to-all-done = bf16[32,256,128]{2,1,0:T(8,128)(2,1)} async-done(((bf16[32,256,128]{2,1,0:T(8,128)(2,1)}), bf16[32,256,128]{2,1,0:T(8,128)(2,1)}, u32[]{:S(2)}, u32[]{:S(2)}) %all-to-all-start) | async-done | bytes 2097184 | tf_op jit(solution)/shard_map/section_top/all_to_all | solution.py:18
  77.6 5.6 %section_top.1 = bf16[8,2,128,128]{3,2,1,0:T(8,128)(2,1)S(1)} custom-call(s32[256]{0:T(256)S(1)} %reshape.67.meta_ref, s32[1]{0:T(128)} %bitcast.1.core_ref, bf16[64,128,128]{2,1,0:T(8,128)(2,1)} %bitcast.8.x_ref, bf16[8,12,128,128]{3,2,1,0:T(8,128)(2,1)S(1)} %bitcast.46, bf16[8,12,128,128]{3,2,1,0:T(8,128)(2,1)} %collective-permute-done.other_ref), custom_call_target="tpu_custom_call" | custom-call | tf_op jit(solution)/shard_map/section_top/pallas_call | solution.py:50
  84.0 9.8 %all-to-all-start.1 = ((bf16[8,256,128]{2,1,0:T(8,128)(2,1)}), bf16[8,256,128]{2,1,0:T(8,128)(2,1)}, u32[]{:S(2)}, u32[]{:S(2)}) async-start(bf16[8,256,128]{2,1,0:T(8,128)(2,1)} %bitcast.50), calls=%async_computation.1 | async-start | bytes 1048576 | tf_op jit(solution)/shard_map/section_top/all_to_all | solution.py:104
  93.8 11.5 %all-to-all-done.1 = bf16[8,256,128]{2,1,0:T(8,128)(2,1)} async-done(((bf16[8,256,128]{2,1,0:T(8,128)(2,1)}), bf16[8,256,128]{2,1,0:T(8,128)(2,1)}, u32[]{:S(2)}, u32[]{:S(2)}) %all-to-all-start.1) | async-done | bytes 524320 | tf_op jit(solution)/shard_map/section_top/all_to_all | solution.py:104
  106.4 6.2 %all_gather.24 = bf16[256,256]{1,0:T(8,128)(2,1)S(1)} all-gather(bf16[256,128]{1,0:T(8,128)(2,1)S(1)} %reduce_sum.42), channel_id=1, replica_groups=mesh['y'=8,'zl'=4,'core'=2,'x'=4,'zh'=2] {'core'}, dimensions={1}, use_global_device_ids=true | all-gather | bytes 196608 | tf_op jit(solution)/shard_map/section_top/all_gather | solution.py:108
  112.8 1.8 broadcast_in_dim.20
  114.7 12.3 %all-to-all-start.2 = ((bf16[32,256,128]{2,1,0:T(8,128)(2,1)}), bf16[32,256,128]{2,1,0:T(8,128)(2,1)}, u32[]{:S(2)}, u32[]{:S(2)}) async-start(bf16[32,256,128]{2,1,0:T(8,128)(2,1)} %broadcast_in_dim.20), calls=%async_computation.2 | async-start | bytes 4194304 | tf_op jit(solution)/shard_map/section_mid/all_to_all | solution.py:18
  129.0 46.7 %all-to-all-done.2 = bf16[32,256,128]{2,1,0:T(8,128)(2,1)} async-done(((bf16[32,256,128]{2,1,0:T(8,128)(2,1)}), bf16[32,256,128]{2,1,0:T(8,128)(2,1)}, u32[]{:S(2)}, u32[]{:S(2)}) %all-to-all-start.2) | async-done | bytes 2097184 | tf_op jit(solution)/shard_map/section_mid/all_to_all | solution.py:18
  175.7 5.6 %section_mid.1 = bf16[8,2,128,128]{3,2,1,0:T(8,128)(2,1)S(1)} custom-call(s32[256]{0:T(256)S(1)} %reshape.67.meta_ref, s32[1]{0:T(128)} %bitcast.1.core_ref, bf16[64,128,128]{2,1,0:T(8,128)(2,1)} %bitcast.11.x_ref, bf16[8,12,128,128]{3,2,1,0:T(8,128)(2,1)S(1)} %bitcast.47, bf16[8,12,128,128]{3,2,1,0:T(8,128)(2,1)} %collective-permute-done.other_ref), custom_call_target="tpu_custom_call" | custom-call | tf_op jit(solution)/shard_map/section_mid/pallas_call | solution.py:50
  182.1 25.4 %all-gather.3.cloned.1.call-done = bf16[2048,256]{1,0:T(8,128)(2,1)} async-done(((bf16[128,256]{1,0:T(8,128)(2,1)}), bf16[2048,256]{1,0:T(8,128)(2,1)}) %all-gather.3.cloned.1.call-update) | async-done | bytes 1048592 | tf_op jit(solution)/shard_map/group_feats/all_gather | solution.py:97
  207.5 1.8 fusion.1
  209.6 19.0 %all_to_all.35 = bf16[8,320,128]{2,1,0:T(8,128)(2,1)S(1)} all-to-all(bf16[8,320,128]{2,1,0:T(8,128)(2,1)S(1)} %pad_maximum_fusion), channel_id=1, replica_groups=mesh['y'=8,'zl'=4,'core'=2,'x'=4,'zh'=2] {'x','zh'}, dimensions={0} | all-to-all | bytes 1310720 | tf_op jit(solution)/shard_map/section_mid/all_to_all | solution.py:121
  228.7 16.9 %all_to_all.36 = bf16[8,64,128]{2,1,0:T(8,128)(2,1)S(1)} all-to-all(bf16[8,64,128]{2,1,0:T(8,128)(2,1)S(1)} %broadcast_in_dim.42), channel_id=1, replica_groups=mesh['y'=8,'zl'=4,'core'=2,'x'=4,'zh'=2] {'zh','zl'}, dimensions={0} | all-to-all | bytes 262144 | tf_op jit(solution)/shard_map/weight_sums/all_to_all | solution.py:18
  246.4 6.5 %all-to-all-start.5 = ((bf16[8,2,64,128]{3,2,1,0:T(8,128)(2,1)}), bf16[8,2,64,128]{3,2,1,0:T(8,128)(2,1)S(1)}, u32[]{:S(2)}, u32[]{:S(2)}) async-start(bf16[8,2,64,128]{3,2,1,0:T(8,128)(2,1)} %broadcast_in_dim.43), calls=%async_computation.5 | async-start | bytes 524288 | tf_op jit(solution)/shard_map/weight_sums/all_to_all | solution.py:18
  252.9 4.4 %all_gather.26 = bf16[256,256]{1,0:T(8,128)(2,1)S(1)} all-gather(bf16[256,128]{1,0:T(8,128)(2,1)S(1)} %slice.35), channel_id=1, replica_groups=mesh['y'=8,'zl'=4,'core'=2,'x'=4,'zh'=2] {'core'}, dimensions={1}, use_global_device_ids=true | all-gather | bytes 196608 | tf_op jit(solution)/shard_map/section_mid/all_gather | solution.py:124
  257.3 4.9 %all-to-all-done.5 = bf16[8,2,64,128]{3,2,1,0:T(8,128)(2,1)S(1)} async-done(((bf16[8,2,64,128]{3,2,1,0:T(8,128)(2,1)}), bf16[8,2,64,128]{3,2,1,0:T(8,128)(2,1)S(1)}, u32[]{:S(2)}, u32[]{:S(2)}) %all-to-all-start.5) | async-done | bytes 262176 | tf_op jit(solution)/shard_map/weight_sums/all_to_all | solution.py:18
  263.0 3.4 %all-to-all-start.6 = ((f32[4,2,64,128]{3,2,1,0:T(8,128)}), f32[4,2,64,128]{3,2,1,0:T(8,128)S(1)}, u32[]{:S(2)}, u32[]{:S(2)}) async-start(f32[4,2,64,128]{3,2,1,0:T(8,128)} %broadcast_in_dim.44), calls=%async_computation.6 | async-start | bytes 524288 | tf_op jit(solution)/shard_map/weight_sums/all_to_all | solution.py:18
  267.3 4.7 %all-to-all-done.6 = f32[4,2,64,128]{3,2,1,0:T(8,128)S(1)} async-done(((f32[4,2,64,128]{3,2,1,0:T(8,128)}), f32[4,2,64,128]{3,2,1,0:T(8,128)S(1)}, u32[]{:S(2)}, u32[]{:S(2)}) %all-to-all-start.6) | async-done | bytes 262176 | tf_op jit(solution)/shard_map/weight_sums/all_to_all | solution.py:18
  272.0 6.9 %all_gather.27 = f32[8,2,32,256]{3,2,1,0:T(8,128)S(1)} all-gather(f32[8,2,32,128]{3,2,1,0:T(8,128)S(1)} %bitcast.53), channel_id=1, replica_groups=mesh['y'=8,'zl'=4,'core'=2,'x'=4,'zh'=2] {'core'}, dimensions={3}, use_global_device_ids=true | all-gather | bytes 786432 | tf_op jit(solution)/shard_map/weight_sums/all_gather | solution.py:134
  (49 shorter events, 12.2 us)
Async XLA Ops:
  7.2 105.5 %copy-start = (bf16[256,256]{1,0:T(8,128)(2,1)S(1)}, bf16[256,256]{1,0:T(8,128)(2,1)}, u32[]{:S(2)}) copy-start(bf16[256,256]{1,0:T(8,128)(2,1)} %param.16) | copy-start | bytes 393220
  21.1 7.7 %copy-start.1 = (bf16[8,1,12,128,128]{4,3,2,1,0:T(8,128)(2,1)S(1)}, bf16[8,1,12,128,128]{4,3,2,1,0:T(8,128)(2,1)}, u32[]{:S(2)}) copy-start(bf16[8,1,12,128,128]{4,3,2,1,0:T(8,128)(2,1)} %param.17) | copy-start | bytes 9437188
  21.1 10.2 %copy-start.7 = (s32[8,1]{0,1:T(1,128)S(1)}, s32[8,1]{0,1:T(1,128)}, u32[]{:S(2)}) copy-start(s32[8,1]{0,1:T(1,128)} %param.19) | copy-start | bytes 100
  21.1 10.4 %copy-start.6 = (s32[8,1,12]{2,1,0:T(1,128)S(1)}, s32[8,1,12]{2,1,0:T(1,128)}, u32[]{:S(2)}) copy-start(s32[8,1,12]{2,1,0:T(1,128)} %param.18) | copy-start | bytes 1156
  21.1 56.5 %all-to-all-start = ((bf16[32,256,128]{2,1,0:T(8,128)(2,1)}), bf16[32,256,128]{2,1,0:T(8,128)(2,1)}, u32[]{:S(2)}, u32[]{:S(2)}) async-start(bf16[32,256,128]{2,1,0:T(8,128)(2,1)} %broadcast_in_dim.18), calls=%async_computation | async-start | bytes 4194304 | tf_op jit(solution)/shard_map/section_top/all_to_all | solution.py:18
  28.8 8.0 %collective-permute-start = (bf16[8,12,128,128]{3,2,1,0:T(8,128)(2,1)S(1)}, bf16[8,12,128,128]{3,2,1,0:T(8,128)(2,1)}, u32[]{:S(2)}, u32[]{:S(2)}) collective-permute-start(bf16[8,12,128,128]{3,2,1,0:T(8,128)(2,1)S(1)} %bitcast.45), channel_id=1, source_target_pairs={{0,8},{8,0},{1,9},{9,1},{2,10},{10,2},{3,11},{11,3},{4,12},{12,4},... | collective-permute-start | bytes 9437192 | tf_op jit(solution)/shard_map/ppermute | solution.py:81
  83.2 0.8 copy-start.4
  84.0 21.3 %all-to-all-start.1 = ((bf16[8,256,128]{2,1,0:T(8,128)(2,1)}), bf16[8,256,128]{2,1,0:T(8,128)(2,1)}, u32[]{:S(2)}, u32[]{:S(2)}) async-start(bf16[8,256,128]{2,1,0:T(8,128)(2,1)} %bitcast.50), calls=%async_computation.1 | async-start | bytes 1048576 | tf_op jit(solution)/shard_map/section_top/all_to_all | solution.py:104
  114.7 61.0 %all-to-all-start.2 = ((bf16[32,256,128]{2,1,0:T(8,128)(2,1)}), bf16[32,256,128]{2,1,0:T(8,128)(2,1)}, u32[]{:S(2)}, u32[]{:S(2)}) async-start(bf16[32,256,128]{2,1,0:T(8,128)(2,1)} %broadcast_in_dim.20), calls=%async_computation.2 | async-start | bytes 4194304 | tf_op jit(solution)/shard_map/section_mid/all_to_all | solution.py:18
  127.0 80.5 %all-gather.3.cloned.1.call-start = ((), (), s32[]{:S(2)}) async-start(), calls=%async_computation.7 | async-start | bytes 1114112 | tf_op jit(solution)/shard_map/group_feats/all_gather | solution.py:97
  181.3 0.8 copy-start.2
  207.5 2.0 copy-start.3
  228.6 37.8 %copy-start.5 = (bf16[256,256]{1,0:T(8,128)(2,1)S(1)}, bf16[256,256]{1,0:T(8,128)(2,1)}, u32[]{:S(2)}) copy-start(bf16[256,256]{1,0:T(8,128)(2,1)} %param.15) | copy-start | bytes 393220
  246.4 15.8 %all-to-all-start.5 = ((bf16[8,2,64,128]{3,2,1,0:T(8,128)(2,1)}), bf16[8,2,64,128]{3,2,1,0:T(8,128)(2,1)S(1)}, u32[]{:S(2)}, u32[]{:S(2)}) async-start(bf16[8,2,64,128]{3,2,1,0:T(8,128)(2,1)} %broadcast_in_dim.43), calls=%async_computation.5 | async-start | bytes 524288 | tf_op jit(solution)/shard_map/weight_sums/all_to_all | solution.py:18
  263.0 8.9 %all-to-all-start.6 = ((f32[4,2,64,128]{3,2,1,0:T(8,128)}), f32[4,2,64,128]{3,2,1,0:T(8,128)S(1)}, u32[]{:S(2)}, u32[]{:S(2)}) async-start(f32[4,2,64,128]{3,2,1,0:T(8,128)} %broadcast_in_dim.44), calls=%async_computation.6 | async-start | bytes 524288 | tf_op jit(solution)/shard_map/weight_sums/all_to_all | solution.py:18
Sparse Core Ops, SparseCore 0:
  131.1 76.3 all-gather.2

commit v2 on v1

--- a/solution.py
+++ b/solution.py
@@ -20,40 +20,103 @@
     )
 
 
-def spmm_kernel(meta_ref, core_ref, x_ref, own_ref, other_ref, out_ref):
+def y_pairs(which):
+    pairs = []
+    for y in range(Y):
+        for core in range(CORE):
+            up = (y + core + which) % 2 == 0
+            pairs.append((y * CORE + core, (y + (1 if up else -1)) % Y * CORE + core))
+    return pairs
+
+
+def piece_table():
+    step = [dict(y_pairs(0)), dict(y_pairs(1))]
+    table = np.zeros((Y * CORE, Y), np.int32)
+    for me in range(Y * CORE):
+        for piece, hops in enumerate(
+            ((), (0,), (1,), (1, 0), (0, 1), (0, 1, 0), (1, 0, 1), (1, 0, 1, 0))
+        ):
+            at = me
+            for hop in hops:
+                at = step[hop][at]
+            table[me, at // CORE] = piece
+    return table
+
+
+def gather_y(mine):
+    def swap(value, which):
+        return lax.ppermute(value, ("y", "core"), y_pairs(which))
+
+    first, second = swap(mine, 0), swap(mine, 1)
+    third, fourth = swap(first, 1), swap(second, 0)
+    fifth, sixth = swap(third, 0), swap(fourth, 1)
+    last = swap(fifth, 1)
+    return mine, first, second, third, fourth, fifth, sixth, last
+
+
+def spmm_kernel(meta_ref, core_ref, *refs):
+    pieces, (own_ref, other_ref, out_ref, x_ref, adj_ref, x_sem, adj_sem) = refs[:Y], refs[Y:]
     core = core_ref[0]
-    slots = own_ref.shape[1]
+    per_side, slots = own_ref.shape[0], own_ref.shape[1]
+    per_piece = pieces[0].shape[0]
     group = 4
-    for side, adj_ref in ((0, own_ref), (1, other_ref)):
+    x_copies = [
+        pltpu.make_async_copy(ref, x_ref.at[pl.ds(p * per_piece, per_piece)], x_sem.at[p])
+        for p, ref in enumerate(pieces)
+    ]
+    adj_copies = [
+        pltpu.make_async_copy(ref.at[i], adj_ref.at[side * per_side + i], adj_sem.at[side * per_side + i])
+        for side, ref in enumerate((own_ref, other_ref))
+        for i in range(per_side)
+    ]
+    for copy in x_copies + adj_copies:
+        copy.start()
+    for copy in x_copies:
+        copy.wait()
+    for n, copy in enumerate(adj_copies):
+        side, i = divmod(n, per_side)
         j = jnp.bitwise_xor(core, side)
-        for i in range(own_ref.shape[0]):
-            base = (j * own_ref.shape[0] + i) * 16
-            count = meta_ref[base + slots]
-
-            def step(s, acc, base=base, count=count, i=i, adj_ref=adj_ref):
-                for t in range(group):
-                    k = s * group + t
-                    block = x_ref[meta_ref[base + k]]
-                    block = jnp.where(k < count, block, jnp.zeros_like(block))
-                    acc = acc + jnp.dot(adj_ref[i, k], block, preferred_element_type=F32)
-                return acc
-
-            acc = lax.fori_loop(
-                0, (count + group - 1) // group, step, jnp.zeros(out_ref.shape[2:], F32)
+        base = (j * per_side + i) * 16
+        count = meta_ref[base + slots]
+        copy.wait()
+
+        def step(s, acc, base=base, count=count, n=n):
+            blocks = []
+            for t in range(group):
+                k = s * group + t
+                block = x_ref[meta_ref[base + k]]
+                blocks.append(jnp.where(k < count, block, jnp.zeros_like(block)))
+            adj = [adj_ref[n, s * group + t] for t in range(group)]
+            return acc + jnp.dot(
+                jnp.concatenate(adj, axis=1),
+                jnp.concatenate(blocks, axis=0),
+                preferred_element_type=F32,
             )
-            out_ref[i, j] = acc.astype(out_ref.dtype)
-
-
-def spmm(meta, core, gathered, own, other):
-    vmem = pl.BlockSpec(memory_space=pltpu.VMEM)
+
+        acc = lax.fori_loop(
+            0, (count + group - 1) // group, step, jnp.zeros(out_ref.shape[2:], F32)
+        )
+        out_ref[i, j] = acc.astype(out_ref.dtype)
+
+
+def spmm(meta, core, pieces, own, other):
     smem = pl.BlockSpec(memory_space=pltpu.SMEM)
+    anywhere = pl.BlockSpec(memory_space=pl.ANY)
+    blocks, bs, half = pieces[0].shape
+    rows = own.shape[0] * CORE
     return pl.pallas_call(
         spmm_kernel,
-        out_shape=jax.ShapeDtypeStruct((NCOL, CORE) + gathered.shape[1:], BF16),
-        in_specs=[smem, smem, vmem, vmem, vmem],
-        out_specs=vmem,
-        compiler_params=pltpu.CompilerParams(vmem_limit_bytes=40 * 1024 * 1024),
-    )(meta, core, gathered, own, other)
+        out_shape=jax.ShapeDtypeStruct((NCOL, CORE, bs, half), BF16),
+        in_specs=[smem, smem] + [anywhere] * (Y + 2),
+        out_specs=pl.BlockSpec(memory_space=pltpu.VMEM),
+        scratch_shapes=[
+            pltpu.VMEM((blocks * Y, bs, half), BF16),
+            pltpu.VMEM((rows,) + own.shape[1:], BF16),
+            pltpu.SemaphoreType.DMA((Y,)),
+            pltpu.SemaphoreType.DMA((rows,)),
+        ],
+        compiler_params=pltpu.CompilerParams(vmem_limit_bytes=20 * 1024 * 1024),
+    )(meta, core, *pieces, own, other)
 
 
 def contract_rows(a, b):
@@ -83,27 +146,35 @@
         [block_cols[:, 0], block_counts, jnp.zeros((NCOL, 16 - 13), jnp.int32)], axis=1
     )
     meta = lax.all_gather(meta, "core", axis=0, tiled=True).reshape(-1)
+    row = lax.dynamic_slice_in_dim(
+        jnp.asarray(piece_table()), lax.axis_index("y") * CORE + core, 1, axis=0
+    )[0]
+    per_piece = ZL * CORE
+    place = sum(
+        jnp.where(meta // per_piece == y, row[y] * per_piece, 0) for y in range(Y)
+    ) + meta % per_piece
+    is_count = jnp.arange(meta.shape[0]) % 16 == 12
+    meta = jnp.where(is_count, meta, place)
     core_id = core.astype(jnp.int32).reshape(1)
 
     with jax.named_scope("pair_inputs"):
         grad_top = jnp.where(mask_top > 0, grad_out, jnp.zeros_like(grad_out))
-        pair = lax.all_gather(
-            jnp.stack([grad_top, mask_mid.astype(BF16), feats_mid]), "core", axis=0
-        )
-        unit_top = my_half(pair[:, 0]).reshape(CORE * bs, half)
-        mask_pair = my_half(pair[:, 1]).reshape(CORE * bs, half)
-        feats_mid_pair = pair[:, 2].reshape(CORE * bs, feats)
+        unit_top = my_half(lax.all_gather(grad_top, "core", axis=0, tiled=True))
+        pair = lax.all_gather(jnp.stack([mask_mid.astype(BF16), feats_mid]), "core", axis=1, tiled=True)
+        mask_pair = my_half(pair[0])
+        feats_mid_pair = pair[1]
     with jax.named_scope("group_feats"):
         feats_in_group = lax.all_gather(feats_in, ("x", "zh", "core"), axis=0, tiled=True)
 
     def gather_units(unit):
-        return everyone(unit, ("y", "zl"), Y * ZL).reshape(-1, bs, half)
+        return gather_y(everyone(unit, "zl", ZL).reshape(-1, bs, half))
 
     with jax.named_scope("section_top"):
         partial_top = spmm(meta, core_id, gather_units(unit_top), adj, other_adj)
         parts = lax.all_to_all(
             partial_top.reshape(NCOL, CORE * bs, half), COLS, 0, 0, tiled=True
         )
+        parts, feats_in_group = lax.optimization_barrier((parts, feats_in_group))
         agg_top = jnp.sum(parts.astype(F32), axis=0).astype(BF16)
         agg_top_both = lax.all_gather(agg_top, "core", axis=1, tiled=True)
         term_second = contract_rows(feats_mid_pair, agg_top)

time: 287 us -> 267 us (0.930)
  waiting for transfers between devices: 135 us -> 32.2 us
  blocking collectives: 67.2 us -> 99.5 us
  starting transfers between devices: 42.2 us -> 71.2 us
  local copies, waits for them, and re-layouts: 9.66 us -> 18.7 us
  Pallas kernels: 11.3 us -> 16.9 us
  between operations: 14.3 us -> 19.4 us
    all_to_all x4 -> x2, waiting for transfers between devices: 97.1 us -> 4.65 us  [everyone(): lax.all_to_all(jnp.broadcast_to(value[None], (count,) + value.shape), axe...]
    ppermute x0 -> x14, starting transfers between devices: none -> 39.5 us  [swap(): return lax.ppermute(value, ('y', 'core'), y_pairs(which))]
    all_gather x1, waiting for transfers between devices: 25.4 us -> 0.01 us  [local(): lax.all_gather(feats_in, ('x', 'zh', 'core'), axis=0, tiled=True)]
    all_to_all x4 -> x2, starting transfers between devices: 29.9 us -> 10.4 us  [everyone(): lax.all_to_all(jnp.broadcast_to(value[None], (count,) + value.shape), axe...]
    ppermute x0 -> x14, waiting for transfers between devices: none -> 19.1 us  [swap(): return lax.ppermute(value, ('y', 'core'), y_pairs(which))]
    all_to_all x1 -> x3, blocking collectives: 16.9 us -> 33.7 us  [everyone(): lax.all_to_all(jnp.broadcast_to(value[None], (count,) + value.shape), axe...]
    unnamed x17 -> x36, local copies, waits for them, and re-layouts: 1.69 us -> 12.4 us
    all_gather x1, blocking collectives: 4.45 us -> 14.9 us  [local(): own_nodes = lax.all_gather(agg_mid, 'core', axis=1, tiled=True)]
  transfers between devices with their start and end apart: 7 -> 19, of which waited for: 6 -> 10; matrix products, arithmetic and copies ran while one was open for 1% -> 4% of each run, Pallas kernels for 2% -> 3%
where the time goes in v2:
time: 267 us; the launch traced here: 265 us
  blocking collectives  99.5 us (37%)
  starting transfers between devices  71.2 us (27%)
  waiting for transfers between devices  32.2 us (12%)
  between operations  19.4 us (7%)
  local copies, waits for them, and re-layouts  18.7 us (7%)
  Pallas kernels  16.9 us (6%)
  other arithmetic  4.18 us (2%)
  matrix products  3.36 us (1%)
    ppermute x14, starting transfers between devices, swap(): return lax.ppermute(value, ('y', 'core'), y_pairs(which))  39.5 us
    all_to_all x3, blocking collectives, everyone(): lax.all_to_all(jnp.broadcast_to(value[None], (count,) + value.shape), axe...  33.7 us
    ppermute x14, waiting for transfers between devices, swap(): return lax.ppermute(value, ('y', 'core'), y_pairs(which))  19.1 us
    all_to_all x1, blocking collectives, local(): parts = lax.all_to_all(sent, COLS, 0, 0, tiled=True)  17.5 us
    pallas_call x2, Pallas kernels, spmm(): pl.pallas_call(spmm_kernel, out_shape=jax.ShapeDtypeStruct((NCOL, CORE, b...  16.9 us
    all_gather x1, blocking collectives, local(): own_nodes = lax.all_gather(agg_mid, 'core', axis=1, tiled=True)  14.9 us
    unnamed x36, local copies, waits for them, and re-layouts  12.4 us
    all_to_all x1, starting transfers between devices, local(): lax.all_to_all(partial_top.reshape(NCOL, CORE * bs, half), COLS, 0, 0, ti...  12.3 us
  transfers between devices with their start and end apart: 19, of which 10 were waited for; matrix products, arithmetic and copies ran while one was open for 4% of the time, Pallas kernels for 3%

profile of v2, /device:TPU:1, one launch (start us, length us, event | category | flops | bytes accessed | tf_op | source)
XLA Modules:
  0.0 265.4 jit_solution(17961854207235936739)
XLA Ops:
  7.2 8.9 %collective-permute-start.7 = (bf16[8,12,128,128]{3,2,1,0:T(8,128)(2,1)}, bf16[8,12,128,128]{3,2,1,0:T(8,128)(2,1)S(1)}, u32[]{:S(2)}, u32[]{:S(2)}) collective-permute-start(bf16[8,12,128,128]{3,2,1,0:T(8,128)(2,1)} %bitcast.52), channel_id=1, source_target_pairs={{0,8},{8,0},{1,9},{9,1},{2,10},{10,2},{3,11},{11,3},{4,12},{12,4},... | collective-permute-start | bytes 9437192 | tf_op jit(solution)/shard_map/ppermute | solution.py:144
  17.1 4.4 %all_gather.23 = bf16[256,256]{1,0:T(8,128)(2,1)S(1)} all-gather(bf16[128,256]{1,0:T(8,128)(2,1)S(1)} %compare_select_fusion), channel_id=1, replica_groups=mesh['y'=8,'zl'=4,'core'=2,'x'=4,'zh'=2] {'core'}, dimensions={0}, use_global_device_ids=true | all-gather | bytes 196608 | tf_op jit(solution)/shard_map/pair_inputs/all_gather | solution.py:162
  21.6 10.7 %all_to_all.35 = bf16[4,256,128]{2,1,0:T(8,128)(2,1)S(1)} all-to-all(bf16[4,256,128]{2,1,0:T(8,128)(2,1)S(1)} %broadcast_in_dim.79), channel_id=1, replica_groups=mesh['y'=8,'zl'=4,'core'=2,'x'=4,'zh'=2] {'zl'}, dimensions={0} | all-to-all | bytes 524288 | tf_op jit(solution)/shard_map/section_top/all_to_all | solution.py:18
  44.6 3.8 %collective-permute-start.3 = (bf16[8,128,128]{2,1,0:T(8,128)(2,1)}, bf16[8,128,128]{2,1,0:T(8,128)(2,1)}, u32[]{:S(2)}, u32[]{:S(2)}) collective-permute-start(bf16[8,128,128]{2,1,0:T(8,128)(2,1)} %collective-permute-done.1.refs_2_), channel_id=1, source_target_pairs={{0,64},{8,456},{64,0},{72,136},{128,192},{136,72},{192,128},{200,2... | collective-permute-start | bytes 786440 | tf_op jit(solution)/shard_map/section_top/ppermute | solution.py:48
  48.4 3.1 %collective-permute-start.4 = (bf16[8,128,128]{2,1,0:T(8,128)(2,1)}, bf16[8,128,128]{2,1,0:T(8,128)(2,1)}, u32[]{:S(2)}, u32[]{:S(2)}) collective-permute-start(bf16[8,128,128]{2,1,0:T(8,128)(2,1)} %collective-permute-done.2.refs_3_), channel_id=1, source_target_pairs={{0,64},{8,456},{64,0},{72,136},{128,192},{136,72},{192,128},{200,2... | collective-permute-start | bytes 786440 | tf_op jit(solution)/shard_map/section_top/ppermute | solution.py:48
  60.9 11.6 %all_gather.21 = s32[16,16]{1,0:T(8,128)S(1)} all-gather(s32[8,16]{1,0:T(8,128)S(1)} %add_add_fusion), channel_id=1, replica_groups=mesh['y'=8,'zl'=4,'core'=2,'x'=4,'zh'=2] {'core'}, dimensions={0}, use_global_device_ids=true | all-gather | bytes 1536 | tf_op jit(solution)/shard_map/all_gather | solution.py:148
  77.7 3.0 %copy-done.1 = bf16[8,1,12,128,128]{4,3,2,1,0:T(8,128)(2,1)S(1)} copy-done((bf16[8,1,12,128,128]{4,3,2,1,0:T(8,128)(2,1)S(1)}, bf16[8,1,12,128,128]{4,3,2,1,0:T(8,128)(2,1)}, u32[]{:S(2)}) %copy-start.1) | copy-done | bytes 3145752
  80.7 8.4 %section_top.1 = bf16[8,2,128,128]{3,2,1,0:T(8,128)(2,1)S(1)} custom-call(s32[256]{0:T(256)S(1)} %compare_select_fusion.9.meta_ref, s32[1]{0:T(128)} %bitcast.9.core_ref, bf16[8,128,128]{2,1,0:T(8,128)(2,1)S(1)} %bitcast.60, bf16[8,128,128]{2,1,0:T(8,128)(2,1)} %collective-permute-done.refs_1_, bf16[8,128,128]{2,1,0:T(8,128)(2,1)} %collective-permute-done.1.refs_2_, ...), custom_call_target="tpu_custom_call" | custom-call | tf_op jit(solution)/shard_map/section_top/pallas_call | solution.py:107
  89.9 12.3 %all-to-all-start.1 = ((bf16[8,256,128]{2,1,0:T(8,128)(2,1)}), bf16[8,256,128]{2,1,0:T(8,128)(2,1)}, u32[]{:S(2)}, u32[]{:S(2)}) async-start(bf16[8,256,128]{2,1,0:T(8,128)(2,1)} %bitcast.57), calls=%async_computation.1 | async-start | bytes 1048576 | tf_op jit(solution)/shard_map/section_top/all_to_all | solution.py:174
  107.1 8.5 %all-to-all-done.1 = bf16[8,256,128]{2,1,0:T(8,128)(2,1)} async-done(((bf16[8,256,128]{2,1,0:T(8,128)(2,1)}), bf16[8,256,128]{2,1,0:T(8,128)(2,1)}, u32[]{:S(2)}, u32[]{:S(2)}) %all-to-all-start.1) | async-done | bytes 524320 | tf_op jit(solution)/shard_map/section_top/all_to_all | solution.py:174
  116.7 3.3 %all_gather.25 = bf16[256,256]{1,0:T(8,128)(2,1)S(1)} all-gather(bf16[256,128]{1,0:T(8,128)(2,1)S(1)} %reduce_sum.42), channel_id=1, replica_groups=mesh['y'=8,'zl'=4,'core'=2,'x'=4,'zh'=2] {'core'}, dimensions={1}, use_global_device_ids=true | all-gather | bytes 196608 | tf_op jit(solution)/shard_map/section_top/all_gather | solution.py:179
  121.1 10.0 %all_to_all.36 = bf16[4,256,128]{2,1,0:T(8,128)(2,1)S(1)} all-to-all(bf16[4,256,128]{2,1,0:T(8,128)(2,1)S(1)} %broadcast_in_dim.81), channel_id=1, replica_groups=mesh['y'=8,'zl'=4,'core'=2,'x'=4,'zh'=2] {'zl'}, dimensions={0} | all-to-all | bytes 524288 | tf_op jit(solution)/shard_map/section_mid/all_to_all | solution.py:18
  134.9 4.5 %collective-permute-done.8.refs_1_ = bf16[8,128,128]{2,1,0:T(8,128)(2,1)S(1)} collective-permute-done((bf16[8,128,128]{2,1,0:T(8,128)(2,1)S(1)}, bf16[8,128,128]{2,1,0:T(8,128)(2,1)S(1)}, u32[]{:S(2)}, u32[]{:S(2)}) %collective-permute-start.8) | collective-permute-done | bytes 262176 | tf_op jit(solution)/shard_map/section_mid/ppermute | solution.py:48
  142.0 5.5 %collective-permute-start.11 = (bf16[8,128,128]{2,1,0:T(8,128)(2,1)S(1)}, bf16[8,128,128]{2,1,0:T(8,128)(2,1)}, u32[]{:S(2)}, u32[]{:S(2)}) collective-permute-start(bf16[8,128,128]{2,1,0:T(8,128)(2,1)S(1)} %collective-permute-done.9.refs_2_), channel_id=1, source_target_pairs={{0,64},{8,456},{64,0},{72,136},{128,192},{136,72},{192,128},{200,2... | collective-permute-start | bytes 786440 | tf_op jit(solution)/shard_map/section_mid/ppermute | solution.py:48
  153.3 5.8 %collective-permute-start.13 = (bf16[8,128,128]{2,1,0:T(8,128)(2,1)}, bf16[8,128,128]{2,1,0:T(8,128)(2,1)}, u32[]{:S(2)}, u32[]{:S(2)}) collective-permute-start(bf16[8,128,128]{2,1,0:T(8,128)(2,1)} %collective-permute-done.11.refs_4_), channel_id=1, source_target_pairs={{0,448},{8,72},{64,128},{72,8},{128,64},{136,200},{192,256},{200,1... | collective-permute-start | bytes 786440 | tf_op jit(solution)/shard_map/section_mid/ppermute | solution.py:48
  166.1 3.0 %collective-permute-done.14.refs_7_ = bf16[8,128,128]{2,1,0:T(8,128)(2,1)} collective-permute-done((bf16[8,128,128]{2,1,0:T(8,128)(2,1)}, bf16[8,128,128]{2,1,0:T(8,128)(2,1)}, u32[]{:S(2)}, u32[]{:S(2)}) %collective-permute-start.14) | collective-permute-done | bytes 262176 | tf_op jit(solution)/shard_map/section_mid/ppermute | solution.py:48
  173.9 8.5 %section_mid.1 = bf16[8,2,128,128]{3,2,1,0:T(8,128)(2,1)S(1)} custom-call(s32[256]{0:T(256)S(1)} %compare_select_fusion.9.meta_ref, s32[1]{0:T(128)} %bitcast.9.core_ref, bf16[8,128,128]{2,1,0:T(8,128)(2,1)S(1)} %bitcast.63, bf16[8,128,128]{2,1,0:T(8,128)(2,1)S(1)} %copy-done.7, bf16[8,128,128]{2,1,0:T(8,128)(2,1)S(1)} %copy-done.9, ...), custom_call_target="tpu_custom_call" | custom-call | tf_op jit(solution)/shard_map/section_mid/pallas_call | solution.py:107
  182.9 17.5 %all_to_all.37 = bf16[8,320,128]{2,1,0:T(8,128)(2,1)S(1)} all-to-all(bf16[8,320,128]{2,1,0:T(8,128)(2,1)S(1)} %pad_maximum_fusion), channel_id=1, replica_groups=mesh['y'=8,'zl'=4,'core'=2,'x'=4,'zh'=2] {'x','zh'}, dimensions={0} | all-to-all | bytes 1310720 | tf_op jit(solution)/shard_map/section_mid/all_to_all | solution.py:192
  200.5 13.0 %all_to_all.38 = bf16[8,64,128]{2,1,0:T(8,128)(2,1)S(1)} all-to-all(bf16[8,64,128]{2,1,0:T(8,128)(2,1)S(1)} %broadcast_in_dim.82), channel_id=1, replica_groups=mesh['y'=8,'zl'=4,'core'=2,'x'=4,'zh'=2] {'zh','zl'}, dimensions={0} | all-to-all | bytes 262144 | tf_op jit(solution)/shard_map/weight_sums/all_to_all | solution.py:18
  214.3 7.0 %all-to-all-start.5 = ((bf16[8,2,64,128]{3,2,1,0:T(8,128)(2,1)}), bf16[8,2,64,128]{3,2,1,0:T(8,128)(2,1)S(1)}, u32[]{:S(2)}, u32[]{:S(2)}) async-start(bf16[8,2,64,128]{3,2,1,0:T(8,128)(2,1)} %broadcast_in_dim.83), calls=%async_computation.5 | async-start | bytes 524288 | tf_op jit(solution)/shard_map/weight_sums/all_to_all | solution.py:18
  221.3 14.9 %all_gather.26 = bf16[256,256]{1,0:T(8,128)(2,1)S(1)} all-gather(bf16[256,128]{1,0:T(8,128)(2,1)S(1)} %slice.70), channel_id=1, replica_groups=mesh['y'=8,'zl'=4,'core'=2,'x'=4,'zh'=2] {'core'}, dimensions={1}, use_global_device_ids=true | all-gather | bytes 196608 | tf_op jit(solution)/shard_map/section_mid/all_gather | solution.py:195
  237.0 3.4 %all-to-all-start.6 = ((f32[4,2,64,128]{3,2,1,0:T(8,128)}), f32[4,2,64,128]{3,2,1,0:T(8,128)S(1)}, u32[]{:S(2)}, u32[]{:S(2)}) async-start(f32[4,2,64,128]{3,2,1,0:T(8,128)} %broadcast_in_dim.84), calls=%async_computation.6 | async-start | bytes 524288 | tf_op jit(solution)/shard_map/weight_sums/all_to_all | solution.py:18
  241.2 4.6 %all-to-all-done.6 = f32[4,2,64,128]{3,2,1,0:T(8,128)S(1)} async-done(((f32[4,2,64,128]{3,2,1,0:T(8,128)}), f32[4,2,64,128]{3,2,1,0:T(8,128)S(1)}, u32[]{:S(2)}, u32[]{:S(2)}) %all-to-all-start.6) | async-done | bytes 262176 | tf_op jit(solution)/shard_map/weight_sums/all_to_all | solution.py:18
  245.9 11.9 %all_gather.27 = f32[8,2,32,256]{3,2,1,0:T(8,128)S(1)} all-gather(f32[8,2,32,128]{3,2,1,0:T(8,128)S(1)} %bitcast.65), channel_id=1, replica_groups=mesh['y'=8,'zl'=4,'core'=2,'x'=4,'zh'=2] {'core'}, dimensions={3}, use_global_device_ids=true | all-gather | bytes 786432 | tf_op jit(solution)/shard_map/weight_sums/all_gather | solution.py:205
  (96 shorter events, 58.4 us)
Async XLA Ops:
  7.2 112.8 %copy-start = (bf16[256,256]{1,0:T(8,128)(2,1)S(1)}, bf16[256,256]{1,0:T(8,128)(2,1)}, u32[]{:S(2)}) copy-start(bf16[256,256]{1,0:T(8,128)(2,1)} %param.17) | copy-start | bytes 393220
  7.2 45.0 %copy-start.16 = (s32[8,1]{0,1:T(1,128)S(1)}, s32[8,1]{0,1:T(1,128)}, u32[]{:S(2)}) copy-start(s32[8,1]{0,1:T(1,128)} %param.20) | copy-start | bytes 100
  7.2 45.2 %copy-start.15 = (s32[8,1,12]{2,1,0:T(1,128)S(1)}, s32[8,1,12]{2,1,0:T(1,128)}, u32[]{:S(2)}) copy-start(s32[8,1,12]{2,1,0:T(1,128)} %param.19) | copy-start | bytes 1156
  7.2 99.9 %all-gather.2.cloned.1.call-start = ((), (), s32[]{:S(2)}) async-start(), calls=%async_computation.7 | async-start | bytes 1114112 | tf_op jit(solution)/shard_map/group_feats/all_gather | solution.py:167
  7.2 70.4 %collective-permute-start.7 = (bf16[8,12,128,128]{3,2,1,0:T(8,128)(2,1)}, bf16[8,12,128,128]{3,2,1,0:T(8,128)(2,1)S(1)}, u32[]{:S(2)}, u32[]{:S(2)}) collective-permute-start(bf16[8,12,128,128]{3,2,1,0:T(8,128)(2,1)} %bitcast.52), channel_id=1, source_target_pairs={{0,8},{8,0},{1,9},{9,1},{2,10},{10,2},{3,11},{11,3},{4,12},{12,4},... | collective-permute-start | bytes 9437192 | tf_op jit(solution)/shard_map/ppermute | solution.py:144
  32.2 8.4 %collective-permute-start = (bf16[8,128,128]{2,1,0:T(8,128)(2,1)S(1)}, bf16[8,128,128]{2,1,0:T(8,128)(2,1)}, u32[]{:S(2)}, u32[]{:S(2)}) collective-permute-start(bf16[8,128,128]{2,1,0:T(8,128)(2,1)S(1)} %bitcast.58), channel_id=1, source_target_pairs={{0,64},{8,456},{64,0},{72,136},{128,192},{136,72},{192,128},{200,2... | collective-permute-start | bytes 786440 | tf_op jit(solution)/shard_map/section_top/ppermute | solution.py:48
  36.7 7.9 %collective-permute-start.1 = (bf16[8,128,128]{2,1,0:T(8,128)(2,1)S(1)}, bf16[8,128,128]{2,1,0:T(8,128)(2,1)}, u32[]{:S(2)}, u32[]{:S(2)}) collective-permute-start(bf16[8,128,128]{2,1,0:T(8,128)(2,1)S(1)} %bitcast.59), channel_id=1, source_target_pairs={{0,448},{8,72},{64,128},{72,8},{128,64},{136,200},{192,256},{200,1... | collective-permute-start | bytes 786440 | tf_op jit(solution)/shard_map/section_top/ppermute | solution.py:48
  40.7 7.7 %collective-permute-start.2 = (bf16[8,128,128]{2,1,0:T(8,128)(2,1)}, bf16[8,128,128]{2,1,0:T(8,128)(2,1)}, u32[]{:S(2)}, u32[]{:S(2)}) collective-permute-start(bf16[8,128,128]{2,1,0:T(8,128)(2,1)} %collective-permute-done.refs_1_), channel_id=1, source_target_pairs={{0,448},{8,72},{64,128},{72,8},{128,64},{136,200},{192,256},{200,1... | collective-permute-start | bytes 786440 | tf_op jit(solution)/shard_map/section_top/ppermute | solution.py:48
  44.6 10.4 %collective-permute-start.3 = (bf16[8,128,128]{2,1,0:T(8,128)(2,1)}, bf16[8,128,128]{2,1,0:T(8,128)(2,1)}, u32[]{:S(2)}, u32[]{:S(2)}) collective-permute-start(bf16[8,128,128]{2,1,0:T(8,128)(2,1)} %collective-permute-done.1.refs_2_), channel_id=1, source_target_pairs={{0,64},{8,456},{64,0},{72,136},{128,192},{136,72},{192,128},{200,2... | collective-permute-start | bytes 786440 | tf_op jit(solution)/shard_map/section_top/ppermute | solution.py:48
  48.4 9.4 %collective-permute-start.4 = (bf16[8,128,128]{2,1,0:T(8,128)(2,1)}, bf16[8,128,128]{2,1,0:T(8,128)(2,1)}, u32[]{:S(2)}, u32[]{:S(2)}) collective-permute-start(bf16[8,128,128]{2,1,0:T(8,128)(2,1)} %collective-permute-done.2.refs_3_), channel_id=1, source_target_pairs={{0,64},{8,456},{64,0},{72,136},{128,192},{136,72},{192,128},{200,2... | collective-permute-start | bytes 786440 | tf_op jit(solution)/shard_map/section_top/ppermute | solution.py:48
  55.0 22.6 %collective-permute-start.5 = (bf16[8,128,128]{2,1,0:T(8,128)(2,1)}, bf16[8,128,128]{2,1,0:T(8,128)(2,1)}, u32[]{:S(2)}, u32[]{:S(2)}) collective-permute-start(bf16[8,128,128]{2,1,0:T(8,128)(2,1)} %collective-permute-done.3.refs_4_), channel_id=1, source_target_pairs={{0,448},{8,72},{64,128},{72,8},{128,64},{136,200},{192,256},{200,1... | collective-permute-start | bytes 786440 | tf_op jit(solution)/shard_map/section_top/ppermute | solution.py:48
  57.8 19.8 %collective-permute-start.6 = (bf16[8,128,128]{2,1,0:T(8,128)(2,1)}, bf16[8,128,128]{2,1,0:T(8,128)(2,1)}, u32[]{:S(2)}, u32[]{:S(2)}) collective-permute-start(bf16[8,128,128]{2,1,0:T(8,128)(2,1)} %collective-permute-done.4.refs_5_), channel_id=1, source_target_pairs={{0,448},{8,72},{64,128},{72,8},{128,64},{136,200},{192,256},{200,1... | collective-permute-start | bytes 786440 | tf_op jit(solution)/shard_map/section_top/ppermute | solution.py:48
  89.9 25.6 %all-to-all-start.1 = ((bf16[8,256,128]{2,1,0:T(8,128)(2,1)}), bf16[8,256,128]{2,1,0:T(8,128)(2,1)}, u32[]{:S(2)}, u32[]{:S(2)}) async-start(bf16[8,256,128]{2,1,0:T(8,128)(2,1)} %bitcast.57), calls=%async_computation.1 | async-start | bytes 1048576 | tf_op jit(solution)/shard_map/section_top/all_to_all | solution.py:174
  104.0 65.1 %copy-start.2 = (bf16[8,1,12,128,128]{4,3,2,1,0:T(8,128)(2,1)S(1)}, bf16[8,1,12,128,128]{4,3,2,1,0:T(8,128)(2,1)}, u32[]{:S(2)}) copy-start(bf16[8,1,12,128,128]{4,3,2,1,0:T(8,128)(2,1)} %param.18) | copy-start | bytes 9437188
  131.1 8.3 %collective-permute-start.8 = (bf16[8,128,128]{2,1,0:T(8,128)(2,1)S(1)}, bf16[8,128,128]{2,1,0:T(8,128)(2,1)S(1)}, u32[]{:S(2)}, u32[]{:S(2)}) collective-permute-start(bf16[8,128,128]{2,1,0:T(8,128)(2,1)S(1)} %bitcast.61), channel_id=1, source_target_pairs={{0,64},{8,456},{64,0},{72,136},{128,192},{136,72},{192,128},{200,2... | collective-permute-start | bytes 786440 | tf_op jit(solution)/shard_map/section_mid/ppermute | solution.py:48
  133.0 9.0 %collective-permute-start.9 = (bf16[8,128,128]{2,1,0:T(8,128)(2,1)S(1)}, bf16[8,128,128]{2,1,0:T(8,128)(2,1)S(1)}, u32[]{:S(2)}, u32[]{:S(2)}) collective-permute-start(bf16[8,128,128]{2,1,0:T(8,128)(2,1)S(1)} %bitcast.62), channel_id=1, source_target_pairs={{0,448},{8,72},{64,128},{72,8},{128,64},{136,200},{192,256},{200,1... | collective-permute-start | bytes 786440 | tf_op jit(solution)/shard_map/section_mid/ppermute | solution.py:48
  139.4 8.9 %collective-permute-start.10 = (bf16[8,128,128]{2,1,0:T(8,128)(2,1)S(1)}, bf16[8,128,128]{2,1,0:T(8,128)(2,1)S(1)}, u32[]{:S(2)}, u32[]{:S(2)}) collective-permute-start(bf16[8,128,128]{2,1,0:T(8,128)(2,1)S(1)} %collective-permute-done.8.refs_1_), channel_id=1, source_target_pairs={{0,448},{8,72},{64,128},{72,8},{128,64},{136,200},{192,256},{200,1... | collective-permute-start | bytes 786440 | tf_op jit(solution)/shard_map/section_mid/ppermute | solution.py:48
  142.0 11.3 %collective-permute-start.11 = (bf16[8,128,128]{2,1,0:T(8,128)(2,1)S(1)}, bf16[8,128,128]{2,1,0:T(8,128)(2,1)}, u32[]{:S(2)}, u32[]{:S(2)}) collective-permute-start(bf16[8,128,128]{2,1,0:T(8,128)(2,1)S(1)} %collective-permute-done.9.refs_2_), channel_id=1, source_target_pairs={{0,64},{8,456},{64,0},{72,136},{128,192},{136,72},{192,128},{200,2... | collective-permute-start | bytes 786440 | tf_op jit(solution)/shard_map/section_mid/ppermute | solution.py:48
  148.3 10.9 %collective-permute-start.12 = (bf16[8,128,128]{2,1,0:T(8,128)(2,1)S(1)}, bf16[8,128,128]{2,1,0:T(8,128)(2,1)}, u32[]{:S(2)}, u32[]{:S(2)}) collective-permute-start(bf16[8,128,128]{2,1,0:T(8,128)(2,1)S(1)} %collective-permute-done.10.refs_3_), channel_id=1, source_target_pairs={{0,64},{8,456},{64,0},{72,136},{128,192},{136,72},{192,128},{200,2... | collective-permute-start | bytes 786440 | tf_op jit(solution)/shard_map/section_mid/ppermute | solution.py:48
  153.3 12.8 %collective-permute-start.13 = (bf16[8,128,128]{2,1,0:T(8,128)(2,1)}, bf16[8,128,128]{2,1,0:T(8,128)(2,1)}, u32[]{:S(2)}, u32[]{:S(2)}) collective-permute-start(bf16[8,128,128]{2,1,0:T(8,128)(2,1)} %collective-permute-done.11.refs_4_), channel_id=1, source_target_pairs={{0,448},{8,72},{64,128},{72,8},{128,64},{136,200},{192,256},{200,1... | collective-permute-start | bytes 786440 | tf_op jit(solution)/shard_map/section_mid/ppermute | solution.py:48
  159.1 10.0 %collective-permute-start.14 = (bf16[8,128,128]{2,1,0:T(8,128)(2,1)}, bf16[8,128,128]{2,1,0:T(8,128)(2,1)}, u32[]{:S(2)}, u32[]{:S(2)}) collective-permute-start(bf16[8,128,128]{2,1,0:T(8,128)(2,1)} %collective-permute-done.12.refs_5_), channel_id=1, source_target_pairs={{0,448},{8,72},{64,128},{72,8},{128,64},{136,200},{192,256},{200,1... | collective-permute-start | bytes 786440 | tf_op jit(solution)/shard_map/section_mid/ppermute | solution.py:48
  200.5 39.9 %copy-start.14 = (bf16[256,256]{1,0:T(8,128)(2,1)S(1)}, bf16[256,256]{1,0:T(8,128)(2,1)}, u32[]{:S(2)}) copy-start(bf16[256,256]{1,0:T(8,128)(2,1)} %param.16) | copy-start | bytes 393220
  214.3 21.9 %all-to-all-start.5 = ((bf16[8,2,64,128]{3,2,1,0:T(8,128)(2,1)}), bf16[8,2,64,128]{3,2,1,0:T(8,128)(2,1)S(1)}, u32[]{:S(2)}, u32[]{:S(2)}) async-start(bf16[8,2,64,128]{3,2,1,0:T(8,128)(2,1)} %broadcast_in_dim.83), calls=%async_computation.5 | async-start | bytes 524288 | tf_op jit(solution)/shard_map/weight_sums/all_to_all | solution.py:18
  237.0 8.9 %all-to-all-start.6 = ((f32[4,2,64,128]{3,2,1,0:T(8,128)}), f32[4,2,64,128]{3,2,1,0:T(8,128)S(1)}, u32[]{:S(2)}, u32[]{:S(2)}) async-start(f32[4,2,64,128]{3,2,1,0:T(8,128)} %broadcast_in_dim.84), calls=%async_computation.6 | async-start | bytes 524288 | tf_op jit(solution)/shard_map/weight_sums/all_to_all | solution.py:18
  (12 other events, 35.0 us)
Sparse Core Ops, SparseCore 0:
  36.8 63.9 all-gather.1

commit v3 on v2

--- a/solution.py
+++ b/solution.py
@@ -59,44 +59,50 @@
     core = core_ref[0]
     per_side, slots = own_ref.shape[0], own_ref.shape[1]
     per_piece = pieces[0].shape[0]
-    group = 4
+    together = 4
+    groups = per_side // together
     x_copies = [
         pltpu.make_async_copy(ref, x_ref.at[pl.ds(p * per_piece, per_piece)], x_sem.at[p])
         for p, ref in enumerate(pieces)
     ]
-    adj_copies = [
-        pltpu.make_async_copy(ref.at[i], adj_ref.at[side * per_side + i], adj_sem.at[side * per_side + i])
-        for side, ref in enumerate((own_ref, other_ref))
-        for i in range(per_side)
-    ]
-    for copy in x_copies + adj_copies:
+
+    def adj_copy(ref, side, m):
+        return pltpu.make_async_copy(
+            ref.at[pl.ds(m * together, together)],
+            adj_ref.at[pl.ds(side * per_side + m * together, together)],
+            adj_sem.at[side * groups + m],
+        )
+
+    for copy in x_copies:
         copy.start()
+    for side, ref in enumerate((own_ref, other_ref)):
+        for m in range(groups):
+            adj_copy(ref, side, m).start()
     for copy in x_copies:
         copy.wait()
-    for n, copy in enumerate(adj_copies):
-        side, i = divmod(n, per_side)
+
+    for side, ref in enumerate((own_ref, other_ref)):
         j = jnp.bitwise_xor(core, side)
-        base = (j * per_side + i) * 16
-        count = meta_ref[base + slots]
-        copy.wait()
-
-        def step(s, acc, base=base, count=count, n=n):
-            blocks = []
-            for t in range(group):
-                k = s * group + t
-                block = x_ref[meta_ref[base + k]]
-                blocks.append(jnp.where(k < count, block, jnp.zeros_like(block)))
-            adj = [adj_ref[n, s * group + t] for t in range(group)]
-            return acc + jnp.dot(
-                jnp.concatenate(adj, axis=1),
-                jnp.concatenate(blocks, axis=0),
-                preferred_element_type=F32,
-            )
-
-        acc = lax.fori_loop(
-            0, (count + group - 1) // group, step, jnp.zeros(out_ref.shape[2:], F32)
-        )
-        out_ref[i, j] = acc.astype(out_ref.dtype)
+
+        def some_rows(m, carry, side=side, ref=ref, j=j):
+            adj_copy(ref, side, m).wait()
+            for t in range(together):
+                i = m * together + t
+                base = (j * per_side + i) * 16
+                count = meta_ref[base + slots]
+                blocks = []
+                for k in range(slots):
+                    block = x_ref[meta_ref[base + k]]
+                    blocks.append(jnp.where(k < count, block, jnp.zeros_like(block)))
+                adj = [adj_ref[side * per_side + i, k] for k in range(slots)]
+                out_ref[i, j] = jnp.dot(
+                    jnp.concatenate(adj, axis=1),
+                    jnp.concatenate(blocks, axis=0),
+                    preferred_element_type=F32,
+                ).astype(out_ref.dtype)
+            return carry
+
+        lax.fori_loop(0, groups, some_rows, 0)
 
 
 def spmm(meta, core, pieces, own, other):
@@ -113,9 +119,9 @@
             pltpu.VMEM((blocks * Y, bs, half), BF16),
             pltpu.VMEM((rows,) + own.shape[1:], BF16),
             pltpu.SemaphoreType.DMA((Y,)),
-            pltpu.SemaphoreType.DMA((rows,)),
+            pltpu.SemaphoreType.DMA((rows // 4,)),
         ],
-        compiler_params=pltpu.CompilerParams(vmem_limit_bytes=20 * 1024 * 1024),
+        compiler_params=pltpu.CompilerParams(vmem_limit_bytes=60 * 1024 * 1024),
     )(meta, core, *pieces, own, other)
 
 
@@ -141,7 +147,6 @@
         return lax.dynamic_slice_in_dim(v, core * half, half, axis=v.ndim - 1)
 
     adj = adj_blocks[:, 0]
-    other_adj = lax.ppermute(adj, "core", [(0, 1), (1, 0)])
     meta = jnp.concatenate(
         [block_cols[:, 0], block_counts, jnp.zeros((NCOL, 16 - 13), jnp.int32)], axis=1
     )
@@ -160,21 +165,25 @@
     with jax.named_scope("pair_inputs"):
         grad_top = jnp.where(mask_top > 0, grad_out, jnp.zeros_like(grad_out))
         unit_top = my_half(lax.all_gather(grad_top, "core", axis=0, tiled=True))
-        pair = lax.all_gather(jnp.stack([mask_mid.astype(BF16), feats_mid]), "core", axis=1, tiled=True)
+        pair = lax.all_gather(
+            jnp.stack([mask_mid.astype(BF16), feats_mid, feats_in]), "core", axis=1, tiled=True
+        )
         mask_pair = my_half(pair[0])
         feats_mid_pair = pair[1]
     with jax.named_scope("group_feats"):
-        feats_in_group = lax.all_gather(feats_in, ("x", "zh", "core"), axis=0, tiled=True)
-
-    def gather_units(unit):
-        return gather_y(everyone(unit, "zl", ZL).reshape(-1, bs, half))
+        feats_in_group = everyone(pair[2], COLS, NCOL).reshape(-1, feats)
+
+    def gather_z(unit):
+        return everyone(unit, "zl", ZL).reshape(-1, bs, half)
 
     with jax.named_scope("section_top"):
-        partial_top = spmm(meta, core_id, gather_units(unit_top), adj, other_adj)
+        units = gather_z(unit_top)
+        adj, units = lax.optimization_barrier((adj, units))
+        other_adj = lax.ppermute(adj, "core", [(0, 1), (1, 0)])
+        partial_top = spmm(meta, core_id, gather_y(units), adj, other_adj)
         parts = lax.all_to_all(
             partial_top.reshape(NCOL, CORE * bs, half), COLS, 0, 0, tiled=True
         )
-        parts, feats_in_group = lax.optimization_barrier((parts, feats_in_group))
         agg_top = jnp.sum(parts.astype(F32), axis=0).astype(BF16)
         agg_top_both = lax.all_gather(agg_top, "core", axis=1, tiled=True)
         term_second = contract_rows(feats_mid_pair, agg_top)
@@ -182,7 +191,7 @@
         hidden = times_transpose(agg_top_both, weight_half)
         grad_mid = jnp.where(mask_pair > 0, hidden, jnp.zeros_like(hidden)).astype(BF16)
     with jax.named_scope("section_mid"):
-        partial_mid = spmm(meta, core_id, gather_units(grad_mid), adj, other_adj)
+        partial_mid = spmm(meta, core_id, gather_y(gather_z(grad_mid)), adj, other_adj)
         term_first = contract_rows(feats_in_group, partial_mid.reshape(-1, half))
         terms = jnp.stack([term_first, term_second]).astype(BF16)
         terms = terms.reshape(2, NCOL, feats // NCOL, half).transpose(1, 0, 2, 3)
@@ -197,11 +206,11 @@
         grad_in = times_transpose(own_nodes, weight_first).astype(BF16)
     with jax.named_scope("weight_sums"):
         piece = summed[CORE * bs :]
-        over_z = everyone(piece.astype(BF16), ("zh", "zl"), ZH * ZL)
-        piece = jnp.sum(over_z.reshape((ZH, ZL) + piece.shape).astype(F32), axis=1)
         over_y = everyone(piece.astype(BF16), "y", Y)
         piece = jnp.sum(over_y.reshape((Y,) + piece.shape).astype(F32), axis=0)
-        over_x = everyone(piece, "x", X).reshape(NCOL, 2, feats // NCOL, half)
+        over_xz = everyone(piece.astype(BF16), ("x", "zh", "zl"), NCOL * ZL)
+        over_x = jnp.sum(over_xz.reshape((NCOL, ZL) + piece.shape).astype(F32), axis=1)
+        over_x = over_x.reshape(NCOL, 2, feats // NCOL, half)
         whole = lax.all_gather(over_x * norm_scale, "core", axis=3, tiled=True)
         whole = whole.transpose(1, 0, 2, 3).reshape(2, feats, feats)
     return (grad_in, whole[0], whole[1])

time: 267 us -> 237 us (0.89)
  between operations: 19.4 us -> 6.01 us
  local copies, waits for them, and re-layouts: 18.7 us -> 8.24 us
  waiting for transfers between devices: 32.2 us -> 40 us
  starting transfers between devices: 71.2 us -> 63.9 us
  Pallas kernels: 16.9 us -> 13.6 us
    unnamed x36 -> x23, local copies, waits for them, and re-layouts: 12.4 us -> 1.74 us
    all_to_all x3 -> x2, blocking collectives: 33.7 us -> 26.7 us  [everyone(): lax.all_to_all(jnp.broadcast_to(value[None], (count,) + value.shape), axe...]
    ppermute x1, starting transfers between devices: 8.92 us -> 3.43 us  [local(): other_adj = lax.ppermute(adj, 'core', [(0, 1), (1, 0)])]
    all_gather x1, blocking collectives: 4.39 us -> 8.43 us  [local(): unit_top = my_half(lax.all_gather(grad_top, 'core', axis=0, tiled=True))]
    all_to_all x1, blocking collectives: 17.5 us -> 21.3 us  [local(): parts = lax.all_to_all(sent, COLS, 0, 0, tiled=True)]
    pallas_call x2, Pallas kernels: 16.9 us -> 13.6 us  [spmm(): pl.pallas_call(spmm_kernel, out_shape=jax.ShapeDtypeStruct((NCOL, CORE, b...]
    all_to_all x1, waiting for transfers between devices: 8.46 us -> 11.7 us  [local(): lax.all_to_all(partial_top.reshape(NCOL, CORE * bs, half), COLS, 0, 0, ti...]
    all_to_all x2 -> x3, waiting for transfers between devices: 4.65 us -> 7.31 us  [everyone(): lax.all_to_all(jnp.broadcast_to(value[None], (count,) + value.shape), axe...]
  transfers between devices with their start and end apart: 19 -> 19, of which waited for: 10 -> 11; matrix products, arithmetic and copies ran while one was open for 4% -> 3% of each run, Pallas kernels for 3% -> 0%
where the time goes in v3:
time: 237 us; the launch traced here: 236 us
  blocking collectives  97.8 us (41%)
  starting transfers between devices  63.9 us (27%)
  waiting for transfers between devices  40 us (17%)
  Pallas kernels  13.6 us (6%)
  local copies, waits for them, and re-layouts  8.24 us (3%)
  between operations  6.01 us (3%)
  other arithmetic  3.8 us (2%)
  matrix products  2.71 us (1%)
    ppermute x14, starting transfers between devices, swap(): return lax.ppermute(value, ('y', 'core'), y_pairs(which))  38.4 us
    all_to_all x2, blocking collectives, everyone(): lax.all_to_all(jnp.broadcast_to(value[None], (count,) + value.shape), axe...  26.7 us
    all_to_all x1, blocking collectives, local(): parts = lax.all_to_all(sent, COLS, 0, 0, tiled=True)  21.3 us
    ppermute x14, waiting for transfers between devices, swap(): return lax.ppermute(value, ('y', 'core'), y_pairs(which))  21 us
    pallas_call x2, Pallas kernels, spmm(): pl.pallas_call(spmm_kernel, out_shape=jax.ShapeDtypeStruct((NCOL, CORE, b...  13.6 us
    all_gather x1, blocking collectives, local(): own_nodes = lax.all_gather(agg_mid, 'core', axis=1, tiled=True)  13.4 us
    all_to_all x3, starting transfers between devices, everyone(): lax.all_to_all(jnp.broadcast_to(value[None], (count,) + value.shape), axe...  12.3 us
    all_gather x1, blocking collectives, local(): whole = lax.all_gather(over_x * norm_scale, 'core', axis=3, tiled=True)  11.9 us
  transfers between devices with their start and end apart: 19, of which 11 were waited for; matrix products, arithmetic and copies ran while one was open for 3% of the time, Pallas kernels for 0%

profile of v3, /device:TPU:1, one launch (start us, length us, event | category | flops | bytes accessed | tf_op | source)
XLA Modules:
  0.0 236.0 jit_solution(3206154660769259079)
XLA Ops:
  1.7 8.4 %all_gather.20 = bf16[256,256]{1,0:T(8,128)(2,1)S(1)} all-gather(bf16[128,256]{1,0:T(8,128)(2,1)S(1)} %compare_select_fusion), channel_id=1, replica_groups=mesh['y'=8,'zl'=4,'core'=2,'x'=4,'zh'=2] {'core'}, dimensions={0}, use_global_device_ids=true | all-gather | bytes 196608 | tf_op jit(solution)/shard_map/pair_inputs/all_gather | solution.py:167
  10.1 10.7 %all_to_all.35 = bf16[4,256,128]{2,1,0:T(8,128)(2,1)S(1)} all-to-all(bf16[4,256,128]{2,1,0:T(8,128)(2,1)S(1)} %broadcast_in_dim.80), channel_id=1, replica_groups=mesh['y'=8,'zl'=4,'core'=2,'x'=4,'zh'=2] {'zl'}, dimensions={0} | all-to-all | bytes 524288 | tf_op jit(solution)/shard_map/section_top/all_to_all | solution.py:18
  20.8 3.4 %collective-permute-start.7 = (bf16[8,12,128,128]{3,2,1,0:T(8,128)(2,1)}, bf16[8,12,128,128]{3,2,1,0:T(8,128)(2,1)S(1)}, u32[]{:S(2)}, u32[]{:S(2)}) collective-permute-start(bf16[8,12,128,128]{3,2,1,0:T(8,128)(2,1)} %bitcast.57), channel_id=1, source_target_pairs={{0,8},{8,0},{1,9},{9,1},{2,10},{10,2},{3,11},{11,3},{4,12},{12,4},... | collective-permute-start | bytes 9437192 | tf_op jit(solution)/shard_map/section_top/ppermute | solution.py:182
  24.3 4.1 %collective-permute-start = (bf16[8,128,128]{2,1,0:T(8,128)(2,1)S(1)}, bf16[8,128,128]{2,1,0:T(8,128)(2,1)}, u32[]{:S(2)}, u32[]{:S(2)}) collective-permute-start(bf16[8,128,128]{2,1,0:T(8,128)(2,1)S(1)} %bitcast.66), channel_id=1, source_target_pairs={{0,64},{8,456},{64,0},{72,136},{128,192},{136,72},{192,128},{200,2... | collective-permute-start | bytes 786440 | tf_op jit(solution)/shard_map/section_top/ppermute | solution.py:48
  35.9 3.3 %collective-permute-start.3 = (bf16[8,128,128]{2,1,0:T(8,128)(2,1)}, bf16[8,128,128]{2,1,0:T(8,128)(2,1)}, u32[]{:S(2)}, u32[]{:S(2)}) collective-permute-start(bf16[8,128,128]{2,1,0:T(8,128)(2,1)} %collective-permute-done.1.refs_2_), channel_id=1, source_target_pairs={{0,64},{8,456},{64,0},{72,136},{128,192},{136,72},{192,128},{200,2... | collective-permute-start | bytes 786440 | tf_op jit(solution)/shard_map/section_top/ppermute | solution.py:48
  40.4 4.1 %collective-permute-start.4 = (bf16[8,128,128]{2,1,0:T(8,128)(2,1)}, bf16[8,128,128]{2,1,0:T(8,128)(2,1)}, u32[]{:S(2)}, u32[]{:S(2)}) collective-permute-start(bf16[8,128,128]{2,1,0:T(8,128)(2,1)} %collective-permute-done.2.refs_3_), channel_id=1, source_target_pairs={{0,64},{8,456},{64,0},{72,136},{128,192},{136,72},{192,128},{200,2... | collective-permute-start | bytes 786440 | tf_op jit(solution)/shard_map/section_top/ppermute | solution.py:48
  56.5 10.5 %all_gather.18 = s32[16,16]{1,0:T(8,128)S(1)} all-gather(s32[8,16]{1,0:T(8,128)S(1)} %add_add_fusion), channel_id=1, replica_groups=mesh['y'=8,'zl'=4,'core'=2,'x'=4,'zh'=2] {'core'}, dimensions={0}, use_global_device_ids=true | all-gather | bytes 1536 | tf_op jit(solution)/shard_map/all_gather | solution.py:153
  69.4 6.8 %section_top.1 = bf16[8,2,128,128]{3,2,1,0:T(8,128)(2,1)} custom-call(s32[256]{0:T(256)} %compare_select_fusion.9.meta_ref, s32[1]{0:T(128)} %bitcast.9.core_ref, bf16[8,128,128]{2,1,0:T(8,128)(2,1)} %bitcast.68, bf16[8,128,128]{2,1,0:T(8,128)(2,1)} %collective-permute-done.refs_1_, bf16[8,128,128]{2,1,0:T(8,128)(2,1)} %collective-permute-done.1.refs_2_, ...), custom_call_target="tpu_custom_call" | custom-call | tf_op jit(solution)/shard_map/section_top/pallas_call | solution.py:113
  76.2 9.8 %all-to-all-start.1 = ((bf16[8,256,128]{2,1,0:T(8,128)(2,1)}), bf16[8,256,128]{2,1,0:T(8,128)(2,1)S(1)}, u32[]{:S(2)}, u32[]{:S(2)}) async-start(bf16[8,256,128]{2,1,0:T(8,128)(2,1)} %bitcast.64), calls=%async_computation.1 | async-start | bytes 1048576 | tf_op jit(solution)/shard_map/section_top/all_to_all | solution.py:184
  90.1 11.7 %all-to-all-done.1 = bf16[8,256,128]{2,1,0:T(8,128)(2,1)S(1)} async-done(((bf16[8,256,128]{2,1,0:T(8,128)(2,1)}), bf16[8,256,128]{2,1,0:T(8,128)(2,1)S(1)}, u32[]{:S(2)}, u32[]{:S(2)}) %all-to-all-start.1) | async-done | bytes 524320 | tf_op jit(solution)/shard_map/section_top/all_to_all | solution.py:184
  101.9 3.2 %all_gather.21 = bf16[256,256]{1,0:T(8,128)(2,1)S(1)} all-gather(bf16[256,128]{1,0:T(8,128)(2,1)S(1)} %reduce_sum.42), channel_id=1, replica_groups=mesh['y'=8,'zl'=4,'core'=2,'x'=4,'zh'=2] {'core'}, dimensions={1}, use_global_device_ids=true | all-gather | bytes 196608 | tf_op jit(solution)/shard_map/section_top/all_gather | solution.py:188
  106.0 4.3 %all-to-all-start.2 = ((bf16[4,256,128]{2,1,0:T(8,128)(2,1)}), bf16[4,256,128]{2,1,0:T(8,128)(2,1)S(1)}, u32[]{:S(2)}, u32[]{:S(2)}) async-start(bf16[4,256,128]{2,1,0:T(8,128)(2,1)} %broadcast_in_dim.82), calls=%async_computation.2 | async-start | bytes 524288 | tf_op jit(solution)/shard_map/section_mid/all_to_all | solution.py:18
  110.4 7.3 %all-to-all-done.2 = bf16[4,256,128]{2,1,0:T(8,128)(2,1)S(1)} async-done(((bf16[4,256,128]{2,1,0:T(8,128)(2,1)}), bf16[4,256,128]{2,1,0:T(8,128)(2,1)S(1)}, u32[]{:S(2)}, u32[]{:S(2)}) %all-to-all-start.2) | async-done | bytes 262176 | tf_op jit(solution)/shard_map/section_mid/all_to_all | solution.py:18
  118.8 3.6 %all-to-all-start.3 = ((bf16[8,256,256]{1,2,0:T(8,128)(2,1)}), bf16[8,256,256]{1,2,0:T(8,128)(2,1)S(1)}, u32[]{:S(2)}, u32[]{:S(2)}) async-start(bf16[8,256,256]{1,2,0:T(8,128)(2,1)} %broadcast_in_dim.84), calls=%async_computation.3 | async-start | bytes 2097152 | tf_op jit(solution)/shard_map/group_feats/all_to_all | solution.py:18
  126.2 4.7 %collective-permute-done.8.refs_1_ = bf16[8,128,128]{2,1,0:T(8,128)(2,1)S(1)} collective-permute-done((bf16[8,128,128]{2,1,0:T(8,128)(2,1)S(1)}, bf16[8,128,128]{2,1,0:T(8,128)(2,1)S(1)}, u32[]{:S(2)}, u32[]{:S(2)}) %collective-permute-start.8) | collective-permute-done | bytes 262176 | tf_op jit(solution)/shard_map/section_mid/ppermute | solution.py:48
  133.5 4.9 %collective-permute-start.11 = (bf16[8,128,128]{2,1,0:T(8,128)(2,1)S(1)}, bf16[8,128,128]{2,1,0:T(8,128)(2,1)}, u32[]{:S(2)}, u32[]{:S(2)}) collective-permute-start(bf16[8,128,128]{2,1,0:T(8,128)(2,1)S(1)} %collective-permute-done.9.refs_2_), channel_id=1, source_target_pairs={{0,64},{8,456},{64,0},{72,136},{128,192},{136,72},{192,128},{200,2... | collective-permute-start | bytes 786440 | tf_op jit(solution)/shard_map/section_mid/ppermute | solution.py:48
  144.3 3.1 %collective-permute-start.13 = (bf16[8,128,128]{2,1,0:T(8,128)(2,1)}, bf16[8,128,128]{2,1,0:T(8,128)(2,1)}, u32[]{:S(2)}, u32[]{:S(2)}) collective-permute-start(bf16[8,128,128]{2,1,0:T(8,128)(2,1)} %collective-permute-done.11.refs_4_), channel_id=1, source_target_pairs={{0,448},{8,72},{64,128},{72,8},{128,64},{136,200},{192,256},{200,1... | collective-permute-start | bytes 786440 | tf_op jit(solution)/shard_map/section_mid/ppermute | solution.py:48
  152.2 5.4 %collective-permute-done.14.refs_7_ = bf16[8,128,128]{2,1,0:T(8,128)(2,1)} collective-permute-done((bf16[8,128,128]{2,1,0:T(8,128)(2,1)}, bf16[8,128,128]{2,1,0:T(8,128)(2,1)}, u32[]{:S(2)}, u32[]{:S(2)}) %collective-permute-start.14) | collective-permute-done | bytes 262176 | tf_op jit(solution)/shard_map/section_mid/ppermute | solution.py:48
  157.6 6.8 %section_mid.1 = bf16[8,2,128,128]{3,2,1,0:T(8,128)(2,1)} custom-call(s32[256]{0:T(256)} %compare_select_fusion.9.meta_ref, s32[1]{0:T(128)} %bitcast.9.core_ref, bf16[8,128,128]{2,1,0:T(8,128)(2,1)} %bitcast.71, bf16[8,128,128]{2,1,0:T(8,128)(2,1)} %copy-done.5, bf16[8,128,128]{2,1,0:T(8,128)(2,1)} %copy-done.6, bf16[8,128,128]{2,1,0:T(8,128)(2,1)} %copy-done.7, ...), custom_call_target="tpu_custom_call" | custom-call | tf_op jit(solution)/shard_map/section_mid/pallas_call | solution.py:113
  166.1 21.3 %all_to_all.36 = bf16[8,320,128]{2,1,0:T(8,128)(2,1)S(1)} all-to-all(bf16[8,320,128]{2,1,0:T(8,128)(2,1)S(1)} %pad_maximum_fusion), channel_id=1, replica_groups=mesh['y'=8,'zl'=4,'core'=2,'x'=4,'zh'=2] {'x','zh'}, dimensions={0} | all-to-all | bytes 1310720 | tf_op jit(solution)/shard_map/section_mid/all_to_all | solution.py:201
  187.5 16.0 %all_to_all.37 = bf16[8,64,128]{2,1,0:T(8,128)(2,1)S(1)} all-to-all(bf16[8,64,128]{2,1,0:T(8,128)(2,1)S(1)} %broadcast_in_dim.85), channel_id=1, replica_groups=mesh['y'=8,'zl'=4,'core'=2,'x'=4,'zh'=2] {'y'}, dimensions={0} | all-to-all | bytes 262144 | tf_op jit(solution)/shard_map/weight_sums/all_to_all | solution.py:18
  204.5 4.4 %all-to-all-start.6 = ((bf16[32,64,128]{2,1,0:T(8,128)(2,1)}), bf16[32,64,128]{2,1,0:T(8,128)(2,1)S(1)}, u32[]{:S(2)}, u32[]{:S(2)}) async-start(bf16[32,64,128]{2,1,0:T(8,128)(2,1)} %broadcast_in_dim.86), calls=%async_computation.6 | async-start | bytes 1048576 | tf_op jit(solution)/shard_map/weight_sums/all_to_all | solution.py:18
  208.9 13.4 %all_gather.22 = bf16[256,256]{1,0:T(8,128)(2,1)S(1)} all-gather(bf16[256,128]{1,0:T(8,128)(2,1)S(1)} %slice.75), channel_id=1, replica_groups=mesh['y'=8,'zl'=4,'core'=2,'x'=4,'zh'=2] {'core'}, dimensions={1}, use_global_device_ids=true | all-gather | bytes 196608 | tf_op jit(solution)/shard_map/section_mid/all_gather | solution.py:204
  223.3 11.9 %all_gather.23 = f32[8,2,32,256]{3,2,1,0:T(8,128)S(1)} all-gather(f32[8,2,32,128]{3,2,1,0:T(8,128)S(1)} %bitcast.72), channel_id=1, replica_groups=mesh['y'=8,'zl'=4,'core'=2,'x'=4,'zh'=2] {'core'}, dimensions={3}, use_global_device_ids=true | all-gather | bytes 786432 | tf_op jit(solution)/shard_map/weight_sums/all_gather | solution.py:214
  (84 shorter events, 46.8 us)
Async XLA Ops:
  0.6 104.4 %copy-start = (bf16[256,256]{1,0:T(8,128)(2,1)S(1)}, bf16[256,256]{1,0:T(8,128)(2,1)}, u32[]{:S(2)}) copy-start(bf16[256,256]{1,0:T(8,128)(2,1)} %param.17) | copy-start | bytes 393220
  0.6 44.6 %copy-start.10 = (s32[8,1]{0,1:T(1,128)S(1)}, s32[8,1]{0,1:T(1,128)}, u32[]{:S(2)}) copy-start(s32[8,1]{0,1:T(1,128)} %param.20) | copy-start | bytes 100
  0.7 44.7 %copy-start.9 = (s32[8,1,12]{2,1,0:T(1,128)S(1)}, s32[8,1,12]{2,1,0:T(1,128)}, u32[]{:S(2)}) copy-start(s32[8,1,12]{2,1,0:T(1,128)} %param.19) | copy-start | bytes 1156
  20.8 46.9 %copy-start.3 = (bf16[4,256,128]{2,1,0:T(8,128)(2,1)}, bf16[4,256,128]{2,1,0:T(8,128)(2,1)S(1)}, u32[]{:S(2)}) copy-start(bf16[4,256,128]{2,1,0:T(8,128)(2,1)S(1)} %all_to_all.35) | copy-start | bytes 786436
  20.8 46.9 %collective-permute-start.7 = (bf16[8,12,128,128]{3,2,1,0:T(8,128)(2,1)}, bf16[8,12,128,128]{3,2,1,0:T(8,128)(2,1)S(1)}, u32[]{:S(2)}, u32[]{:S(2)}) collective-permute-start(bf16[8,12,128,128]{3,2,1,0:T(8,128)(2,1)} %bitcast.57), channel_id=1, source_target_pairs={{0,8},{8,0},{1,9},{9,1},{2,10},{10,2},{3,11},{11,3},{4,12},{12,4},... | collective-permute-start | bytes 9437192 | tf_op jit(solution)/shard_map/section_top/ppermute | solution.py:182
  24.3 8.4 %collective-permute-start = (bf16[8,128,128]{2,1,0:T(8,128)(2,1)S(1)}, bf16[8,128,128]{2,1,0:T(8,128)(2,1)}, u32[]{:S(2)}, u32[]{:S(2)}) collective-permute-start(bf16[8,128,128]{2,1,0:T(8,128)(2,1)S(1)} %bitcast.66), channel_id=1, source_target_pairs={{0,64},{8,456},{64,0},{72,136},{128,192},{136,72},{192,128},{200,2... | collective-permute-start | bytes 786440 | tf_op jit(solution)/shard_map/section_top/ppermute | solution.py:48
  28.4 7.5 %collective-permute-start.1 = (bf16[8,128,128]{2,1,0:T(8,128)(2,1)S(1)}, bf16[8,128,128]{2,1,0:T(8,128)(2,1)}, u32[]{:S(2)}, u32[]{:S(2)}) collective-permute-start(bf16[8,128,128]{2,1,0:T(8,128)(2,1)S(1)} %bitcast.67), channel_id=1, source_target_pairs={{0,448},{8,72},{64,128},{72,8},{128,64},{136,200},{192,256},{200,1... | collective-permute-start | bytes 786440 | tf_op jit(solution)/shard_map/section_top/ppermute | solution.py:48
  32.7 7.7 %collective-permute-start.2 = (bf16[8,128,128]{2,1,0:T(8,128)(2,1)}, bf16[8,128,128]{2,1,0:T(8,128)(2,1)}, u32[]{:S(2)}, u32[]{:S(2)}) collective-permute-start(bf16[8,128,128]{2,1,0:T(8,128)(2,1)} %collective-permute-done.refs_1_), channel_id=1, source_target_pairs={{0,448},{8,72},{64,128},{72,8},{128,64},{136,200},{192,256},{200,1... | collective-permute-start | bytes 786440 | tf_op jit(solution)/shard_map/section_top/ppermute | solution.py:48
  35.9 9.6 %collective-permute-start.3 = (bf16[8,128,128]{2,1,0:T(8,128)(2,1)}, bf16[8,128,128]{2,1,0:T(8,128)(2,1)}, u32[]{:S(2)}, u32[]{:S(2)}) collective-permute-start(bf16[8,128,128]{2,1,0:T(8,128)(2,1)} %collective-permute-done.1.refs_2_), channel_id=1, source_target_pairs={{0,64},{8,456},{64,0},{72,136},{128,192},{136,72},{192,128},{200,2... | collective-permute-start | bytes 786440 | tf_op jit(solution)/shard_map/section_top/ppermute | solution.py:48
  40.4 8.6 %collective-permute-start.4 = (bf16[8,128,128]{2,1,0:T(8,128)(2,1)}, bf16[8,128,128]{2,1,0:T(8,128)(2,1)}, u32[]{:S(2)}, u32[]{:S(2)}) collective-permute-start(bf16[8,128,128]{2,1,0:T(8,128)(2,1)} %collective-permute-done.2.refs_3_), channel_id=1, source_target_pairs={{0,64},{8,456},{64,0},{72,136},{128,192},{136,72},{192,128},{200,2... | collective-permute-start | bytes 786440 | tf_op jit(solution)/shard_map/section_top/ppermute | solution.py:48
  45.5 22.3 %collective-permute-start.5 = (bf16[8,128,128]{2,1,0:T(8,128)(2,1)}, bf16[8,128,128]{2,1,0:T(8,128)(2,1)}, u32[]{:S(2)}, u32[]{:S(2)}) collective-permute-start(bf16[8,128,128]{2,1,0:T(8,128)(2,1)} %collective-permute-done.3.refs_4_), channel_id=1, source_target_pairs={{0,448},{8,72},{64,128},{72,8},{128,64},{136,200},{192,256},{200,1... | collective-permute-start | bytes 786440 | tf_op jit(solution)/shard_map/section_top/ppermute | solution.py:48
  49.0 18.7 %collective-permute-start.6 = (bf16[8,128,128]{2,1,0:T(8,128)(2,1)}, bf16[8,128,128]{2,1,0:T(8,128)(2,1)}, u32[]{:S(2)}, u32[]{:S(2)}) collective-permute-start(bf16[8,128,128]{2,1,0:T(8,128)(2,1)} %collective-permute-done.4.refs_5_), channel_id=1, source_target_pairs={{0,448},{8,72},{64,128},{72,8},{128,64},{136,200},{192,256},{200,1... | collective-permute-start | bytes 786440 | tf_op jit(solution)/shard_map/section_top/ppermute | solution.py:48
  76.2 25.6 %all-to-all-start.1 = ((bf16[8,256,128]{2,1,0:T(8,128)(2,1)}), bf16[8,256,128]{2,1,0:T(8,128)(2,1)S(1)}, u32[]{:S(2)}, u32[]{:S(2)}) async-start(bf16[8,256,128]{2,1,0:T(8,128)(2,1)} %bitcast.64), calls=%async_computation.1 | async-start | bytes 1048576 | tf_op jit(solution)/shard_map/section_top/all_to_all | solution.py:184
  106.0 11.7 %all-to-all-start.2 = ((bf16[4,256,128]{2,1,0:T(8,128)(2,1)}), bf16[4,256,128]{2,1,0:T(8,128)(2,1)S(1)}, u32[]{:S(2)}, u32[]{:S(2)}) async-start(bf16[4,256,128]{2,1,0:T(8,128)(2,1)} %broadcast_in_dim.82), calls=%async_computation.2 | async-start | bytes 524288 | tf_op jit(solution)/shard_map/section_mid/all_to_all | solution.py:18
  118.8 32.0 %all-to-all-start.3 = ((bf16[8,256,256]{1,2,0:T(8,128)(2,1)}), bf16[8,256,256]{1,2,0:T(8,128)(2,1)S(1)}, u32[]{:S(2)}, u32[]{:S(2)}) async-start(bf16[8,256,256]{1,2,0:T(8,128)(2,1)} %broadcast_in_dim.84), calls=%async_computation.3 | async-start | bytes 2097152 | tf_op jit(solution)/shard_map/group_feats/all_to_all | solution.py:18
  122.4 8.5 %collective-permute-start.8 = (bf16[8,128,128]{2,1,0:T(8,128)(2,1)S(1)}, bf16[8,128,128]{2,1,0:T(8,128)(2,1)S(1)}, u32[]{:S(2)}, u32[]{:S(2)}) collective-permute-start(bf16[8,128,128]{2,1,0:T(8,128)(2,1)S(1)} %bitcast.69), channel_id=1, source_target_pairs={{0,64},{8,456},{64,0},{72,136},{128,192},{136,72},{192,128},{200,2... | collective-permute-start | bytes 786440 | tf_op jit(solution)/shard_map/section_mid/ppermute | solution.py:48
  124.3 9.2 %collective-permute-start.9 = (bf16[8,128,128]{2,1,0:T(8,128)(2,1)S(1)}, bf16[8,128,128]{2,1,0:T(8,128)(2,1)S(1)}, u32[]{:S(2)}, u32[]{:S(2)}) collective-permute-start(bf16[8,128,128]{2,1,0:T(8,128)(2,1)S(1)} %bitcast.70), channel_id=1, source_target_pairs={{0,448},{8,72},{64,128},{72,8},{128,64},{136,200},{192,256},{200,1... | collective-permute-start | bytes 786440 | tf_op jit(solution)/shard_map/section_mid/ppermute | solution.py:48
  130.9 7.6 %collective-permute-start.10 = (bf16[8,128,128]{2,1,0:T(8,128)(2,1)S(1)}, bf16[8,128,128]{2,1,0:T(8,128)(2,1)S(1)}, u32[]{:S(2)}, u32[]{:S(2)}) collective-permute-start(bf16[8,128,128]{2,1,0:T(8,128)(2,1)S(1)} %collective-permute-done.8.refs_1_), channel_id=1, source_target_pairs={{0,448},{8,72},{64,128},{72,8},{128,64},{136,200},{192,256},{200,1... | collective-permute-start | bytes 786440 | tf_op jit(solution)/shard_map/section_mid/ppermute | solution.py:48
  133.5 10.7 %collective-permute-start.11 = (bf16[8,128,128]{2,1,0:T(8,128)(2,1)S(1)}, bf16[8,128,128]{2,1,0:T(8,128)(2,1)}, u32[]{:S(2)}, u32[]{:S(2)}) collective-permute-start(bf16[8,128,128]{2,1,0:T(8,128)(2,1)S(1)} %collective-permute-done.9.refs_2_), channel_id=1, source_target_pairs={{0,64},{8,456},{64,0},{72,136},{128,192},{136,72},{192,128},{200,2... | collective-permute-start | bytes 786440 | tf_op jit(solution)/shard_map/section_mid/ppermute | solution.py:48
  138.5 9.4 %collective-permute-start.12 = (bf16[8,128,128]{2,1,0:T(8,128)(2,1)S(1)}, bf16[8,128,128]{2,1,0:T(8,128)(2,1)}, u32[]{:S(2)}, u32[]{:S(2)}) collective-permute-start(bf16[8,128,128]{2,1,0:T(8,128)(2,1)S(1)} %collective-permute-done.10.refs_3_), channel_id=1, source_target_pairs={{0,64},{8,456},{64,0},{72,136},{128,192},{136,72},{192,128},{200,2... | collective-permute-start | bytes 786440 | tf_op jit(solution)/shard_map/section_mid/ppermute | solution.py:48
  144.3 7.9 %collective-permute-start.13 = (bf16[8,128,128]{2,1,0:T(8,128)(2,1)}, bf16[8,128,128]{2,1,0:T(8,128)(2,1)}, u32[]{:S(2)}, u32[]{:S(2)}) collective-permute-start(bf16[8,128,128]{2,1,0:T(8,128)(2,1)} %collective-permute-done.11.refs_4_), channel_id=1, source_target_pairs={{0,448},{8,72},{64,128},{72,8},{128,64},{136,200},{192,256},{200,1... | collective-permute-start | bytes 786440 | tf_op jit(solution)/shard_map/section_mid/ppermute | solution.py:48
  147.9 9.7 %collective-permute-start.14 = (bf16[8,128,128]{2,1,0:T(8,128)(2,1)}, bf16[8,128,128]{2,1,0:T(8,128)(2,1)}, u32[]{:S(2)}, u32[]{:S(2)}) collective-permute-start(bf16[8,128,128]{2,1,0:T(8,128)(2,1)} %collective-permute-done.12.refs_5_), channel_id=1, source_target_pairs={{0,448},{8,72},{64,128},{72,8},{128,64},{136,200},{192,256},{200,1... | collective-permute-start | bytes 786440 | tf_op jit(solution)/shard_map/section_mid/ppermute | solution.py:48
  187.4 34.9 %copy-start.8 = (bf16[256,256]{1,0:T(8,128)(2,1)S(1)}, bf16[256,256]{1,0:T(8,128)(2,1)}, u32[]{:S(2)}) copy-start(bf16[256,256]{1,0:T(8,128)(2,1)} %param.16) | copy-start | bytes 393220
  204.5 18.7 %all-to-all-start.6 = ((bf16[32,64,128]{2,1,0:T(8,128)(2,1)}), bf16[32,64,128]{2,1,0:T(8,128)(2,1)S(1)}, u32[]{:S(2)}, u32[]{:S(2)}) async-start(bf16[32,64,128]{2,1,0:T(8,128)(2,1)} %broadcast_in_dim.86), calls=%async_computation.6 | async-start | bytes 1048576 | tf_op jit(solution)/shard_map/weight_sums/all_to_all | solution.py:18
  (6 other events, 62.7 us)

commit v4 on v3

--- a/solution.py
+++ b/solution.py
@@ -43,24 +43,28 @@
     return table
 
 
-def gather_y(mine):
+def gather_y(mine, beside=None):
     def swap(value, which):
         return lax.ppermute(value, ("y", "core"), y_pairs(which))
 
     first, second = swap(mine, 0), swap(mine, 1)
     third, fourth = swap(first, 1), swap(second, 0)
     fifth, sixth = swap(third, 0), swap(fourth, 1)
+    if beside is not None:
+        fifth, beside = lax.optimization_barrier((fifth, beside))
     last = swap(fifth, 1)
-    return mine, first, second, third, fourth, fifth, sixth, last
-
-
-def spmm_kernel(meta_ref, core_ref, *refs):
+    return (mine, first, second, third, fourth, fifth, sixth, last), beside
+
+
+def spmm_kernel(meta_ref, table_ref, place_ref, *refs):
     pieces, (own_ref, other_ref, out_ref, x_ref, adj_ref, x_sem, adj_sem) = refs[:Y], refs[Y:]
-    core = core_ref[0]
+    core = place_ref[1]
+    at = (place_ref[0] * CORE + core) * Y
     per_side, slots = own_ref.shape[0], own_ref.shape[1]
     per_piece = pieces[0].shape[0]
     together = 4
     groups = per_side // together
+    empty = x_ref.shape[0] - 1
     x_copies = [
         pltpu.make_async_copy(ref, x_ref.at[pl.ds(p * per_piece, per_piece)], x_sem.at[p])
         for p, ref in enumerate(pieces)
@@ -78,6 +82,7 @@
     for side, ref in enumerate((own_ref, other_ref)):
         for m in range(groups):
             adj_copy(ref, side, m).start()
+    x_ref[empty] = jnp.zeros(x_ref.shape[1:], x_ref.dtype)
     for copy in x_copies:
         copy.wait()
 
@@ -92,8 +97,9 @@
                 count = meta_ref[base + slots]
                 blocks = []
                 for k in range(slots):
-                    block = x_ref[meta_ref[base + k]]
-                    blocks.append(jnp.where(k < count, block, jnp.zeros_like(block)))
+                    block = meta_ref[base + k]
+                    found = table_ref[at + block // per_piece] * per_piece + block % per_piece
+                    blocks.append(x_ref[jnp.where(k < count, found, empty)])
                 adj = [adj_ref[side * per_side + i, k] for k in range(slots)]
                 out_ref[i, j] = jnp.dot(
                     jnp.concatenate(adj, axis=1),
@@ -105,7 +111,7 @@
         lax.fori_loop(0, groups, some_rows, 0)
 
 
-def spmm(meta, core, pieces, own, other):
+def spmm(meta, place, pieces, own, other):
     smem = pl.BlockSpec(memory_space=pltpu.SMEM)
     anywhere = pl.BlockSpec(memory_space=pl.ANY)
     blocks, bs, half = pieces[0].shape
@@ -113,16 +119,16 @@
     return pl.pallas_call(
         spmm_kernel,
         out_shape=jax.ShapeDtypeStruct((NCOL, CORE, bs, half), BF16),
-        in_specs=[smem, smem] + [anywhere] * (Y + 2),
+        in_specs=[smem, smem, smem] + [anywhere] * (Y + 2),
         out_specs=pl.BlockSpec(memory_space=pltpu.VMEM),
         scratch_shapes=[
-            pltpu.VMEM((blocks * Y, bs, half), BF16),
+            pltpu.VMEM((blocks * Y + 1, bs, half), BF16),
             pltpu.VMEM((rows,) + own.shape[1:], BF16),
             pltpu.SemaphoreType.DMA((Y,)),
             pltpu.SemaphoreType.DMA((rows // 4,)),
         ],
         compiler_params=pltpu.CompilerParams(vmem_limit_bytes=60 * 1024 * 1024),
-    )(meta, core, *pieces, own, other)
+    )(meta, jnp.asarray(piece_table().reshape(-1)), place, *pieces, own, other)
 
 
 def contract_rows(a, b):
@@ -151,19 +157,11 @@
         [block_cols[:, 0], block_counts, jnp.zeros((NCOL, 16 - 13), jnp.int32)], axis=1
     )
     meta = lax.all_gather(meta, "core", axis=0, tiled=True).reshape(-1)
-    row = lax.dynamic_slice_in_dim(
-        jnp.asarray(piece_table()), lax.axis_index("y") * CORE + core, 1, axis=0
-    )[0]
-    per_piece = ZL * CORE
-    place = sum(
-        jnp.where(meta // per_piece == y, row[y] * per_piece, 0) for y in range(Y)
-    ) + meta % per_piece
-    is_count = jnp.arange(meta.shape[0]) % 16 == 12
-    meta = jnp.where(is_count, meta, place)
-    core_id = core.astype(jnp.int32).reshape(1)
+    place = jnp.stack([lax.axis_index("y"), core]).astype(jnp.int32)
 
     with jax.named_scope("pair_inputs"):
         grad_top = jnp.where(mask_top > 0, grad_out, jnp.zeros_like(grad_out))
+        grad_top, meta = lax.optimization_barrier((grad_top, meta))
         unit_top = my_half(lax.all_gather(grad_top, "core", axis=0, tiled=True))
         pair = lax.all_gather(
             jnp.stack([mask_mid.astype(BF16), feats_mid, feats_in]), "core", axis=1, tiled=True
@@ -180,7 +178,8 @@
         units = gather_z(unit_top)
         adj, units = lax.optimization_barrier((adj, units))
         other_adj = lax.ppermute(adj, "core", [(0, 1), (1, 0)])
-        partial_top = spmm(meta, core_id, gather_y(units), adj, other_adj)
+        pieces, other_adj = gather_y(units, other_adj)
+        partial_top = spmm(meta, place, pieces, adj, other_adj)
         parts = lax.all_to_all(
             partial_top.reshape(NCOL, CORE * bs, half), COLS, 0, 0, tiled=True
         )
@@ -191,7 +190,7 @@
         hidden = times_transpose(agg_top_both, weight_half)
         grad_mid = jnp.where(mask_pair > 0, hidden, jnp.zeros_like(hidden)).astype(BF16)
     with jax.named_scope("section_mid"):
-        partial_mid = spmm(meta, core_id, gather_y(gather_z(grad_mid)), adj, other_adj)
+        partial_mid = spmm(meta, place, gather_y(gather_z(grad_mid))[0], adj, other_adj)
         term_first = contract_rows(feats_in_group, partial_mid.reshape(-1, half))
         terms = jnp.stack([term_first, term_second]).astype(BF16)
         terms = terms.reshape(2, NCOL, feats // NCOL, half).transpose(1, 0, 2, 3)

time: 237 us -> 233 us (0.983)
  waiting for transfers between devices: 40 us -> 34.5 us
  blocking collectives: 97.8 us -> 103 us
  between operations: 6.01 us -> 1.03 us
  starting transfers between devices: 63.9 us -> 66.5 us
    all_to_all x1, waiting for transfers between devices: 11.7 us -> 0.06 us  [local(): lax.all_to_all(partial_top.reshape(NCOL, CORE * bs, half), COLS, 0, 0, ti...]
    all_gather x1, blocking collectives: 3.19 us -> 10.7 us  [local(): agg_top_both = lax.all_gather(agg_top, 'core', axis=1, tiled=True)]
    all_gather x1, blocking collectives: 2.3 us -> 9.68 us  [local(): lax.all_gather(jnp.stack([mask_mid.astype(BF16), feats_mid, feats_in]), '...]
    all_gather x1, blocking collectives: 8.43 us -> 1.9 us  [local(): unit_top = my_half(lax.all_gather(grad_top, 'core', axis=0, tiled=True))]
    ppermute x14, waiting for transfers between devices: 21 us -> 27.1 us  [swap(): return lax.ppermute(value, ('y', 'core'), y_pairs(which))]
    all_to_all x2, blocking collectives: 26.7 us -> 24.2 us  [everyone(): lax.all_to_all(jnp.broadcast_to(value[None], (count,) + value.shape), axe...]
  transfers between devices with their start and end apart: 19 -> 19, of which waited for: 11 -> 16; matrix products, arithmetic and copies ran while one was open for 3% -> 2% of each run, Pallas kernels for 0% -> 0%
where the time goes in v4:
time: 233 us; the launch traced here: 232 us
  blocking collectives  103 us (44%)
  starting transfers between devices  66.5 us (29%)
  waiting for transfers between devices  34.5 us (15%)
  Pallas kernels  13.2 us (6%)
  local copies, waits for them, and re-layouts  6.54 us (3%)
  other arithmetic  4.43 us (2%)
  matrix products  2.72 us (1%)
    ppermute x14, starting transfers between devices, swap(): return lax.ppermute(value, ('y', 'core'), y_pairs(which))  40.1 us
    ppermute x14, waiting for transfers between devices, swap(): return lax.ppermute(value, ('y', 'core'), y_pairs(which))  27.1 us
    all_to_all x2, blocking collectives, everyone(): lax.all_to_all(jnp.broadcast_to(value[None], (count,) + value.shape), axe...  24.2 us
    all_to_all x1, blocking collectives, local(): parts = lax.all_to_all(sent, COLS, 0, 0, tiled=True)  22.4 us
    all_gather x1, blocking collectives, local(): own_nodes = lax.all_gather(agg_mid, 'core', axis=1, tiled=True)  14.1 us
    all_to_all x3, starting transfers between devices, everyone(): lax.all_to_all(jnp.broadcast_to(value[None], (count,) + value.shape), axe...  13.3 us
    pallas_call x2, Pallas kernels, spmm(): pl.pallas_call(spmm_kernel, out_shape=jax.ShapeDtypeStruct((NCOL, CORE, b...  13.2 us
    all_gather x1, blocking collectives, local(): whole = lax.all_gather(over_x * norm_scale, 'core', axis=3, tiled=True)  11.9 us
  transfers between devices with their start and end apart: 19, of which 16 were waited for; matrix products, arithmetic and copies ran while one was open for 2% of the time, Pallas kernels for 0%

profile of v4, /device:TPU:1, one launch (start us, length us, event | category | flops | bytes accessed | tf_op | source)
XLA Modules:
  0.0 232.2 jit_solution(9558112413696959186)
XLA Ops:
  2.3 8.4 %all_gather.18 = s32[16,16]{1,0:T(8,128)S(1)} all-gather(s32[8,16]{1,0:T(8,128)S(1)} %add_add_fusion), channel_id=1, replica_groups=mesh['y'=8,'zl'=4,'core'=2,'x'=4,'zh'=2] {'core'}, dimensions={0}, use_global_device_ids=true | all-gather | bytes 1536 | tf_op jit(solution)/shard_map/all_gather | solution.py:159
  14.2 10.7 %all_to_all.35 = bf16[4,256,128]{2,1,0:T(8,128)(2,1)S(1)} all-to-all(bf16[4,256,128]{2,1,0:T(8,128)(2,1)S(1)} %broadcast_in_dim.17), channel_id=1, replica_groups=mesh['y'=8,'zl'=4,'core'=2,'x'=4,'zh'=2] {'zl'}, dimensions={0} | all-to-all | bytes 524288 | tf_op jit(solution)/shard_map/section_top/all_to_all | solution.py:18
  24.9 3.4 %collective-permute-start.5 = (bf16[8,12,128,128]{3,2,1,0:T(8,128)(2,1)}, bf16[8,12,128,128]{3,2,1,0:T(8,128)(2,1)S(1)}, u32[]{:S(2)}, u32[]{:S(2)}) collective-permute-start(bf16[8,12,128,128]{3,2,1,0:T(8,128)(2,1)} %bitcast.50), channel_id=1, source_target_pairs={{0,8},{8,0},{1,9},{9,1},{2,10},{10,2},{3,11},{11,3},{4,12},{12,4},... | collective-permute-start | bytes 9437192 | tf_op jit(solution)/shard_map/section_top/ppermute | solution.py:180
  28.3 4.1 %collective-permute-start = (bf16[8,128,128]{2,1,0:T(8,128)(2,1)S(1)}, bf16[8,128,128]{2,1,0:T(8,128)(2,1)S(1)}, u32[]{:S(2)}, u32[]{:S(2)}) collective-permute-start(bf16[8,128,128]{2,1,0:T(8,128)(2,1)S(1)} %bitcast.62), channel_id=1, source_target_pairs={{0,64},{8,456},{64,0},{72,136},{128,192},{136,72},{192,128},{200,2... | collective-permute-start | bytes 786440 | tf_op jit(solution)/shard_map/section_top/ppermute | solution.py:48
  39.8 3.3 %collective-permute-start.3 = (bf16[8,128,128]{2,1,0:T(8,128)(2,1)S(1)}, bf16[8,128,128]{2,1,0:T(8,128)(2,1)}, u32[]{:S(2)}, u32[]{:S(2)}) collective-permute-start(bf16[8,128,128]{2,1,0:T(8,128)(2,1)S(1)} %collective-permute-done.1.refs_2_), channel_id=1, source_target_pairs={{0,64},{8,456},{64,0},{72,136},{128,192},{136,72},{192,128},{200,2... | collective-permute-start | bytes 786440 | tf_op jit(solution)/shard_map/section_top/ppermute | solution.py:48
  44.0 4.1 %collective-permute-start.4 = (bf16[8,128,128]{2,1,0:T(8,128)(2,1)S(1)}, bf16[8,128,128]{2,1,0:T(8,128)(2,1)}, u32[]{:S(2)}, u32[]{:S(2)}) collective-permute-start(bf16[8,128,128]{2,1,0:T(8,128)(2,1)S(1)} %collective-permute-done.2.refs_3_), channel_id=1, source_target_pairs={{0,64},{8,456},{64,0},{72,136},{128,192},{136,72},{192,128},{200,2... | collective-permute-start | bytes 786440 | tf_op jit(solution)/shard_map/section_top/ppermute | solution.py:48
  60.2 6.6 %section_top.1 = bf16[8,2,128,128]{3,2,1,0:T(8,128)(2,1)} custom-call(s32[256]{0:T(256)} %reshape.67.meta_ref, s32[128]{0:T(128)} %constant.32.clone.table_ref, s32[2]{0:T(128)} %pad_add_fusion.place_ref, bf16[8,128,128]{2,1,0:T(8,128)(2,1)} %bitcast.64, bf16[8,128,128]{2,1,0:T(8,128)(2,1)} %copy-done.7, bf16[8,128,128]{2,1,0:T(8,128)(2,1)} %copy-done.8, ...), custom_call_target="tpu_custom_call" | custom-call | tf_op jit(solution)/shard_map/section_top/pallas_call | solution.py:119
  66.8 9.8 %all-to-all-start.1 = ((bf16[8,256,128]{2,1,0:T(8,128)(2,1)}), bf16[8,256,128]{2,1,0:T(8,128)(2,1)S(1)}, u32[]{:S(2)}, u32[]{:S(2)}) async-start(bf16[8,256,128]{2,1,0:T(8,128)(2,1)} %bitcast.57), calls=%async_computation.1 | async-start | bytes 1048576 | tf_op jit(solution)/shard_map/section_top/all_to_all | solution.py:183
  78.4 9.7 %all_gather.19 = bf16[3,256,256]{2,1,0:T(8,128)(2,1)S(1)} all-gather(bf16[3,128,256]{2,1,0:T(8,128)(2,1)S(1)} %pad_maximum_fusion.1), channel_id=1, replica_groups=mesh['y'=8,'zl'=4,'core'=2,'x'=4,'zh'=2] {'core'}, dimensions={1}, use_global_device_ids=true | all-gather | bytes 589824 | tf_op jit(solution)/shard_map/pair_inputs/all_gather | solution.py:166
  88.2 10.7 %all_gather.21 = bf16[256,256]{1,0:T(8,128)(2,1)S(1)} all-gather(bf16[256,128]{1,0:T(8,128)(2,1)S(1)} %reduce_sum.42), channel_id=1, replica_groups=mesh['y'=8,'zl'=4,'core'=2,'x'=4,'zh'=2] {'core'}, dimensions={1}, use_global_device_ids=true | all-gather | bytes 196608 | tf_op jit(solution)/shard_map/section_top/all_gather | solution.py:187
  99.8 3.9 %all-to-all-start.2 = ((bf16[4,256,128]{2,1,0:T(8,128)(2,1)}), bf16[4,256,128]{2,1,0:T(8,128)(2,1)S(1)}, u32[]{:S(2)}, u32[]{:S(2)}) async-start(bf16[4,256,128]{2,1,0:T(8,128)(2,1)} %broadcast_in_dim.19), calls=%async_computation.2 | async-start | bytes 524288 | tf_op jit(solution)/shard_map/section_mid/all_to_all | solution.py:18
  103.8 7.3 %all-to-all-done.2 = bf16[4,256,128]{2,1,0:T(8,128)(2,1)S(1)} async-done(((bf16[4,256,128]{2,1,0:T(8,128)(2,1)}), bf16[4,256,128]{2,1,0:T(8,128)(2,1)S(1)}, u32[]{:S(2)}, u32[]{:S(2)}) %all-to-all-start.2) | async-done | bytes 262176 | tf_op jit(solution)/shard_map/section_mid/all_to_all | solution.py:18
  112.2 3.6 %all-to-all-start.3 = ((bf16[8,256,256]{1,2,0:T(8,128)(2,1)}), bf16[8,256,256]{1,2,0:T(8,128)(2,1)S(1)}, u32[]{:S(2)}, u32[]{:S(2)}) async-start(bf16[8,256,256]{1,2,0:T(8,128)(2,1)} %broadcast_in_dim.42), calls=%async_computation.3 | async-start | bytes 2097152 | tf_op jit(solution)/shard_map/group_feats/all_to_all | solution.py:18
  115.8 5.4 %collective-permute-start.8 = (bf16[8,128,128]{2,1,0:T(8,128)(2,1)S(1)}, bf16[8,128,128]{2,1,0:T(8,128)(2,1)S(1)}, u32[]{:S(2)}, u32[]{:S(2)}) collective-permute-start(bf16[8,128,128]{2,1,0:T(8,128)(2,1)S(1)} %bitcast.59), channel_id=1, source_target_pairs={{0,64},{8,456},{64,0},{72,136},{128,192},{136,72},{192,128},{200,2... | collective-permute-start | bytes 786440 | tf_op jit(solution)/shard_map/section_mid/ppermute | solution.py:48
  129.1 3.1 %collective-permute-start.11 = (bf16[8,128,128]{2,1,0:T(8,128)(2,1)S(1)}, bf16[8,128,128]{2,1,0:T(8,128)(2,1)}, u32[]{:S(2)}, u32[]{:S(2)}) collective-permute-start(bf16[8,128,128]{2,1,0:T(8,128)(2,1)S(1)} %collective-permute-done.9.refs_2_), channel_id=1, source_target_pairs={{0,64},{8,456},{64,0},{72,136},{128,192},{136,72},{192,128},{200,2... | collective-permute-start | bytes 786440 | tf_op jit(solution)/shard_map/section_mid/ppermute | solution.py:48
  132.7 4.3 %collective-permute-start.12 = (bf16[8,128,128]{2,1,0:T(8,128)(2,1)S(1)}, bf16[8,128,128]{2,1,0:T(8,128)(2,1)}, u32[]{:S(2)}, u32[]{:S(2)}) collective-permute-start(bf16[8,128,128]{2,1,0:T(8,128)(2,1)S(1)} %collective-permute-done.10.refs_3_), channel_id=1, source_target_pairs={{0,64},{8,456},{64,0},{72,136},{128,192},{136,72},{192,128},{200,2... | collective-permute-start | bytes 786440 | tf_op jit(solution)/shard_map/section_mid/ppermute | solution.py:48
  136.9 3.3 %collective-permute-done.11.refs_4_ = bf16[8,128,128]{2,1,0:T(8,128)(2,1)} collective-permute-done((bf16[8,128,128]{2,1,0:T(8,128)(2,1)S(1)}, bf16[8,128,128]{2,1,0:T(8,128)(2,1)}, u32[]{:S(2)}, u32[]{:S(2)}) %collective-permute-start.11) | collective-permute-done | bytes 262176 | tf_op jit(solution)/shard_map/section_mid/ppermute | solution.py:48
  149.6 3.7 %collective-permute-done.14.refs_7_ = bf16[8,128,128]{2,1,0:T(8,128)(2,1)} collective-permute-done((bf16[8,128,128]{2,1,0:T(8,128)(2,1)}, bf16[8,128,128]{2,1,0:T(8,128)(2,1)}, u32[]{:S(2)}, u32[]{:S(2)}) %collective-permute-start.14) | collective-permute-done | bytes 262176 | tf_op jit(solution)/shard_map/section_mid/ppermute | solution.py:48
  153.3 6.6 %section_mid.1 = bf16[8,2,128,128]{3,2,1,0:T(8,128)(2,1)} custom-call(s32[256]{0:T(256)} %reshape.67.meta_ref, s32[128]{0:T(128)} %constant.32.clone.table_ref, s32[2]{0:T(128)} %pad_add_fusion.place_ref, bf16[8,128,128]{2,1,0:T(8,128)(2,1)} %bitcast.61, bf16[8,128,128]{2,1,0:T(8,128)(2,1)} %copy-done.5, bf16[8,128,128]{2,1,0:T(8,128)(2,1)} %copy-done.6, ...), custom_call_target="tpu_custom_call" | custom-call | tf_op jit(solution)/shard_map/section_mid/pallas_call | solution.py:119
  161.6 22.4 %all_to_all.36 = bf16[8,320,128]{2,1,0:T(8,128)(2,1)S(1)} all-to-all(bf16[8,320,128]{2,1,0:T(8,128)(2,1)S(1)} %pad_maximum_fusion), channel_id=1, replica_groups=mesh['y'=8,'zl'=4,'core'=2,'x'=4,'zh'=2] {'x','zh'}, dimensions={0} | all-to-all | bytes 1310720 | tf_op jit(solution)/shard_map/section_mid/all_to_all | solution.py:200
  184.1 13.5 %all_to_all.37 = bf16[8,64,128]{2,1,0:T(8,128)(2,1)S(1)} all-to-all(bf16[8,64,128]{2,1,0:T(8,128)(2,1)S(1)} %broadcast_in_dim.43), channel_id=1, replica_groups=mesh['y'=8,'zl'=4,'core'=2,'x'=4,'zh'=2] {'y'}, dimensions={0} | all-to-all | bytes 262144 | tf_op jit(solution)/shard_map/weight_sums/all_to_all | solution.py:18
  198.5 5.8 %all-to-all-start.6 = ((bf16[32,64,128]{2,1,0:T(8,128)(2,1)}), bf16[32,64,128]{2,1,0:T(8,128)(2,1)S(1)}, u32[]{:S(2)}, u32[]{:S(2)}) async-start(bf16[32,64,128]{2,1,0:T(8,128)(2,1)} %broadcast_in_dim.44), calls=%async_computation.6 | async-start | bytes 1048576 | tf_op jit(solution)/shard_map/weight_sums/all_to_all | solution.py:18
  204.4 14.1 %all_gather.22 = bf16[256,256]{1,0:T(8,128)(2,1)S(1)} all-gather(bf16[256,128]{1,0:T(8,128)(2,1)S(1)} %slice.35), channel_id=1, replica_groups=mesh['y'=8,'zl'=4,'core'=2,'x'=4,'zh'=2] {'core'}, dimensions={1}, use_global_device_ids=true | all-gather | bytes 196608 | tf_op jit(solution)/shard_map/section_mid/all_gather | solution.py:203
  219.4 11.9 %all_gather.23 = f32[8,2,32,256]{3,2,1,0:T(8,128)S(1)} all-gather(f32[8,2,32,128]{3,2,1,0:T(8,128)S(1)} %bitcast.65), channel_id=1, replica_groups=mesh['y'=8,'zl'=4,'core'=2,'x'=4,'zh'=2] {'core'}, dimensions={3}, use_global_device_ids=true | all-gather | bytes 786432 | tf_op jit(solution)/shard_map/weight_sums/all_gather | solution.py:213
  (84 shorter events, 51.5 us)
Async XLA Ops:
  0.6 98.3 %copy-start = (bf16[256,256]{1,0:T(8,128)(2,1)S(1)}, bf16[256,256]{1,0:T(8,128)(2,1)}, u32[]{:S(2)}) copy-start(bf16[256,256]{1,0:T(8,128)(2,1)} %param.18) | copy-start | bytes 393220
  24.9 35.3 %copy-start.4 = (bf16[4,256,128]{2,1,0:T(8,128)(2,1)}, bf16[4,256,128]{2,1,0:T(8,128)(2,1)S(1)}, u32[]{:S(2)}) copy-start(bf16[4,256,128]{2,1,0:T(8,128)(2,1)S(1)} %all_to_all.35) | copy-start | bytes 786436
  24.9 27.5 %collective-permute-start.5 = (bf16[8,12,128,128]{3,2,1,0:T(8,128)(2,1)}, bf16[8,12,128,128]{3,2,1,0:T(8,128)(2,1)S(1)}, u32[]{:S(2)}, u32[]{:S(2)}) collective-permute-start(bf16[8,12,128,128]{3,2,1,0:T(8,128)(2,1)} %bitcast.50), channel_id=1, source_target_pairs={{0,8},{8,0},{1,9},{9,1},{2,10},{10,2},{3,11},{11,3},{4,12},{12,4},... | collective-permute-start | bytes 9437192 | tf_op jit(solution)/shard_map/section_top/ppermute | solution.py:180
  28.3 8.3 %collective-permute-start = (bf16[8,128,128]{2,1,0:T(8,128)(2,1)S(1)}, bf16[8,128,128]{2,1,0:T(8,128)(2,1)S(1)}, u32[]{:S(2)}, u32[]{:S(2)}) collective-permute-start(bf16[8,128,128]{2,1,0:T(8,128)(2,1)S(1)} %bitcast.62), channel_id=1, source_target_pairs={{0,64},{8,456},{64,0},{72,136},{128,192},{136,72},{192,128},{200,2... | collective-permute-start | bytes 786440 | tf_op jit(solution)/shard_map/section_top/ppermute | solution.py:48
  32.4 7.4 %collective-permute-start.1 = (bf16[8,128,128]{2,1,0:T(8,128)(2,1)S(1)}, bf16[8,128,128]{2,1,0:T(8,128)(2,1)S(1)}, u32[]{:S(2)}, u32[]{:S(2)}) collective-permute-start(bf16[8,128,128]{2,1,0:T(8,128)(2,1)S(1)} %bitcast.63), channel_id=1, source_target_pairs={{0,448},{8,72},{64,128},{72,8},{128,64},{136,200},{192,256},{200,1... | collective-permute-start | bytes 786440 | tf_op jit(solution)/shard_map/section_top/ppermute | solution.py:48
  36.6 7.4 %collective-permute-start.2 = (bf16[8,128,128]{2,1,0:T(8,128)(2,1)S(1)}, bf16[8,128,128]{2,1,0:T(8,128)(2,1)S(1)}, u32[]{:S(2)}, u32[]{:S(2)}) collective-permute-start(bf16[8,128,128]{2,1,0:T(8,128)(2,1)S(1)} %collective-permute-done.refs_1_), channel_id=1, source_target_pairs={{0,448},{8,72},{64,128},{72,8},{128,64},{136,200},{192,256},{200,1... | collective-permute-start | bytes 786440 | tf_op jit(solution)/shard_map/section_top/ppermute | solution.py:48
  39.8 8.4 %collective-permute-start.3 = (bf16[8,128,128]{2,1,0:T(8,128)(2,1)S(1)}, bf16[8,128,128]{2,1,0:T(8,128)(2,1)}, u32[]{:S(2)}, u32[]{:S(2)}) collective-permute-start(bf16[8,128,128]{2,1,0:T(8,128)(2,1)S(1)} %collective-permute-done.1.refs_2_), channel_id=1, source_target_pairs={{0,64},{8,456},{64,0},{72,136},{128,192},{136,72},{192,128},{200,2... | collective-permute-start | bytes 786440 | tf_op jit(solution)/shard_map/section_top/ppermute | solution.py:48
  44.0 8.4 %collective-permute-start.4 = (bf16[8,128,128]{2,1,0:T(8,128)(2,1)S(1)}, bf16[8,128,128]{2,1,0:T(8,128)(2,1)}, u32[]{:S(2)}, u32[]{:S(2)}) collective-permute-start(bf16[8,128,128]{2,1,0:T(8,128)(2,1)S(1)} %collective-permute-done.2.refs_3_), channel_id=1, source_target_pairs={{0,64},{8,456},{64,0},{72,136},{128,192},{136,72},{192,128},{200,2... | collective-permute-start | bytes 786440 | tf_op jit(solution)/shard_map/section_top/ppermute | solution.py:48
  48.3 9.4 %collective-permute-start.6 = (bf16[8,128,128]{2,1,0:T(8,128)(2,1)}, bf16[8,128,128]{2,1,0:T(8,128)(2,1)}, u32[]{:S(2)}, u32[]{:S(2)}) collective-permute-start(bf16[8,128,128]{2,1,0:T(8,128)(2,1)} %collective-permute-done.3.refs_4_), channel_id=1, source_target_pairs={{0,448},{8,72},{64,128},{72,8},{128,64},{136,200},{192,256},{200,1... | collective-permute-start | bytes 786440 | tf_op jit(solution)/shard_map/section_top/ppermute | solution.py:48
  52.5 7.7 %collective-permute-start.7 = (bf16[8,128,128]{2,1,0:T(8,128)(2,1)}, bf16[8,128,128]{2,1,0:T(8,128)(2,1)}, u32[]{:S(2)}, u32[]{:S(2)}) collective-permute-start(bf16[8,128,128]{2,1,0:T(8,128)(2,1)} %collective-permute-done.4.refs_5_), channel_id=1, source_target_pairs={{0,448},{8,72},{64,128},{72,8},{128,64},{136,200},{192,256},{200,1... | collective-permute-start | bytes 786440 | tf_op jit(solution)/shard_map/section_top/ppermute | solution.py:48
  66.8 21.4 %all-to-all-start.1 = ((bf16[8,256,128]{2,1,0:T(8,128)(2,1)}), bf16[8,256,128]{2,1,0:T(8,128)(2,1)S(1)}, u32[]{:S(2)}, u32[]{:S(2)}) async-start(bf16[8,256,128]{2,1,0:T(8,128)(2,1)} %bitcast.57), calls=%async_computation.1 | async-start | bytes 1048576 | tf_op jit(solution)/shard_map/section_top/all_to_all | solution.py:183
  99.8 11.3 %all-to-all-start.2 = ((bf16[4,256,128]{2,1,0:T(8,128)(2,1)}), bf16[4,256,128]{2,1,0:T(8,128)(2,1)S(1)}, u32[]{:S(2)}, u32[]{:S(2)}) async-start(bf16[4,256,128]{2,1,0:T(8,128)(2,1)} %broadcast_in_dim.19), calls=%async_computation.2 | async-start | bytes 524288 | tf_op jit(solution)/shard_map/section_mid/all_to_all | solution.py:18
  112.2 33.5 %all-to-all-start.3 = ((bf16[8,256,256]{1,2,0:T(8,128)(2,1)}), bf16[8,256,256]{1,2,0:T(8,128)(2,1)S(1)}, u32[]{:S(2)}, u32[]{:S(2)}) async-start(bf16[8,256,256]{1,2,0:T(8,128)(2,1)} %broadcast_in_dim.42), calls=%async_computation.3 | async-start | bytes 2097152 | tf_op jit(solution)/shard_map/group_feats/all_to_all | solution.py:18
  115.8 9.5 %collective-permute-start.8 = (bf16[8,128,128]{2,1,0:T(8,128)(2,1)S(1)}, bf16[8,128,128]{2,1,0:T(8,128)(2,1)S(1)}, u32[]{:S(2)}, u32[]{:S(2)}) collective-permute-start(bf16[8,128,128]{2,1,0:T(8,128)(2,1)S(1)} %bitcast.59), channel_id=1, source_target_pairs={{0,64},{8,456},{64,0},{72,136},{128,192},{136,72},{192,128},{200,2... | collective-permute-start | bytes 786440 | tf_op jit(solution)/shard_map/section_mid/ppermute | solution.py:48
  121.2 7.9 %collective-permute-start.9 = (bf16[8,128,128]{2,1,0:T(8,128)(2,1)S(1)}, bf16[8,128,128]{2,1,0:T(8,128)(2,1)S(1)}, u32[]{:S(2)}, u32[]{:S(2)}) collective-permute-start(bf16[8,128,128]{2,1,0:T(8,128)(2,1)S(1)} %bitcast.60), channel_id=1, source_target_pairs={{0,448},{8,72},{64,128},{72,8},{128,64},{136,200},{192,256},{200,1... | collective-permute-start | bytes 786440 | tf_op jit(solution)/shard_map/section_mid/ppermute | solution.py:48
  125.2 21.6 %copy-start.5 = (bf16[8,128,128]{2,1,0:T(8,128)(2,1)}, bf16[8,128,128]{2,1,0:T(8,128)(2,1)S(1)}, u32[]{:S(2)}) copy-start(bf16[8,128,128]{2,1,0:T(8,128)(2,1)S(1)} %collective-permute-done.8.refs_1_) | copy-start | bytes 786436
  125.2 7.4 %collective-permute-start.10 = (bf16[8,128,128]{2,1,0:T(8,128)(2,1)S(1)}, bf16[8,128,128]{2,1,0:T(8,128)(2,1)S(1)}, u32[]{:S(2)}, u32[]{:S(2)}) collective-permute-start(bf16[8,128,128]{2,1,0:T(8,128)(2,1)S(1)} %collective-permute-done.8.refs_1_), channel_id=1, source_target_pairs={{0,448},{8,72},{64,128},{72,8},{128,64},{136,200},{192,256},{200,1... | collective-permute-start | bytes 786440 | tf_op jit(solution)/shard_map/section_mid/ppermute | solution.py:48
  129.1 17.8 %copy-start.6 = (bf16[8,128,128]{2,1,0:T(8,128)(2,1)}, bf16[8,128,128]{2,1,0:T(8,128)(2,1)S(1)}, u32[]{:S(2)}) copy-start(bf16[8,128,128]{2,1,0:T(8,128)(2,1)S(1)} %collective-permute-done.9.refs_2_) | copy-start | bytes 786436
  129.1 11.2 %collective-permute-start.11 = (bf16[8,128,128]{2,1,0:T(8,128)(2,1)S(1)}, bf16[8,128,128]{2,1,0:T(8,128)(2,1)}, u32[]{:S(2)}, u32[]{:S(2)}) collective-permute-start(bf16[8,128,128]{2,1,0:T(8,128)(2,1)S(1)} %collective-permute-done.9.refs_2_), channel_id=1, source_target_pairs={{0,64},{8,456},{64,0},{72,136},{128,192},{136,72},{192,128},{200,2... | collective-permute-start | bytes 786440 | tf_op jit(solution)/shard_map/section_mid/ppermute | solution.py:48
  132.7 10.5 %collective-permute-start.12 = (bf16[8,128,128]{2,1,0:T(8,128)(2,1)S(1)}, bf16[8,128,128]{2,1,0:T(8,128)(2,1)}, u32[]{:S(2)}, u32[]{:S(2)}) collective-permute-start(bf16[8,128,128]{2,1,0:T(8,128)(2,1)S(1)} %collective-permute-done.10.refs_3_), channel_id=1, source_target_pairs={{0,64},{8,456},{64,0},{72,136},{128,192},{136,72},{192,128},{200,2... | collective-permute-start | bytes 786440 | tf_op jit(solution)/shard_map/section_mid/ppermute | solution.py:48
  140.3 9.3 %collective-permute-start.13 = (bf16[8,128,128]{2,1,0:T(8,128)(2,1)}, bf16[8,128,128]{2,1,0:T(8,128)(2,1)}, u32[]{:S(2)}, u32[]{:S(2)}) collective-permute-start(bf16[8,128,128]{2,1,0:T(8,128)(2,1)} %collective-permute-done.11.refs_4_), channel_id=1, source_target_pairs={{0,448},{8,72},{64,128},{72,8},{128,64},{136,200},{192,256},{200,1... | collective-permute-start | bytes 786440 | tf_op jit(solution)/shard_map/section_mid/ppermute | solution.py:48
  143.1 10.2 %collective-permute-start.14 = (bf16[8,128,128]{2,1,0:T(8,128)(2,1)}, bf16[8,128,128]{2,1,0:T(8,128)(2,1)}, u32[]{:S(2)}, u32[]{:S(2)}) collective-permute-start(bf16[8,128,128]{2,1,0:T(8,128)(2,1)} %collective-permute-done.12.refs_5_), channel_id=1, source_target_pairs={{0,448},{8,72},{64,128},{72,8},{128,64},{136,200},{192,256},{200,1... | collective-permute-start | bytes 786440 | tf_op jit(solution)/shard_map/section_mid/ppermute | solution.py:48
  184.0 34.4 %copy-start.11 = (bf16[256,256]{1,0:T(8,128)(2,1)S(1)}, bf16[256,256]{1,0:T(8,128)(2,1)}, u32[]{:S(2)}) copy-start(bf16[256,256]{1,0:T(8,128)(2,1)} %param.17) | copy-start | bytes 393220
  198.5 20.8 %all-to-all-start.6 = ((bf16[32,64,128]{2,1,0:T(8,128)(2,1)}), bf16[32,64,128]{2,1,0:T(8,128)(2,1)S(1)}, u32[]{:S(2)}, u32[]{:S(2)}) async-start(bf16[32,64,128]{2,1,0:T(8,128)(2,1)} %broadcast_in_dim.44), calls=%async_computation.6 | async-start | bytes 1048576 | tf_op jit(solution)/shard_map/weight_sums/all_to_all | solution.py:18
  (7 other events, 70.5 us)

commit v5 on v4

--- a/solution.py
+++ b/solution.py
@@ -12,6 +12,7 @@
 COLS = ("x", "zh")
 NCOL = X * ZH
 BF16, F32 = jnp.bfloat16, jnp.float32
+CHUNK, TOGETHER = 4, 8
 
 
 def everyone(value, axes, count):
@@ -57,65 +58,89 @@
 
 
 def spmm_kernel(meta_ref, table_ref, place_ref, *refs):
-    pieces, (own_ref, other_ref, out_ref, x_ref, adj_ref, x_sem, adj_sem) = refs[:Y], refs[Y:]
+    pieces, refs = refs[:Y], refs[Y:]
+    own_ref, other_ref, out_ref, x_ref, adj_ref, acc_ref, list_ref, x_sem, adj_sem = refs
     core = place_ref[1]
     at = (place_ref[0] * CORE + core) * Y
     per_side, slots = own_ref.shape[0], own_ref.shape[1]
+    chunks = slots // CHUNK
     per_piece = pieces[0].shape[0]
-    together = 4
-    groups = per_side // together
     empty = x_ref.shape[0] - 1
     x_copies = [
         pltpu.make_async_copy(ref, x_ref.at[pl.ds(p * per_piece, per_piece)], x_sem.at[p])
         for p, ref in enumerate(pieces)
     ]
-
-    def adj_copy(ref, side, m):
-        return pltpu.make_async_copy(
-            ref.at[pl.ds(m * together, together)],
-            adj_ref.at[pl.ds(side * per_side + m * together, together)],
-            adj_sem.at[side * groups + m],
-        )
-
     for copy in x_copies:
         copy.start()
+
+    def adj_copy(ref, i, c, item):
+        return pltpu.make_async_copy(
+            ref.at[i, pl.ds(c * CHUNK, CHUNK)], adj_ref.at[item], adj_sem.at[item]
+        )
+
+    total = jnp.int32(0)
     for side, ref in enumerate((own_ref, other_ref)):
-        for m in range(groups):
-            adj_copy(ref, side, m).start()
+        j = jnp.bitwise_xor(core, side)
+        for i in range(per_side):
+            count = meta_ref[(j * per_side + i) * 16 + slots]
+            for c in range(chunks):
+                live = count > c * CHUNK
+
+                @pl.when(live)
+                def _(ref=ref, i=i, c=c, side=side, total=total):
+                    list_ref[total] = (side * per_side + i) * chunks + c
+                    adj_copy(ref, i, c, total).start()
+
+                total = total + live.astype(jnp.int32)
+
+    acc_ref[...] = jnp.zeros(acc_ref.shape, acc_ref.dtype)
     x_ref[empty] = jnp.zeros(x_ref.shape[1:], x_ref.dtype)
     for copy in x_copies:
         copy.wait()
 
-    for side, ref in enumerate((own_ref, other_ref)):
+    def some_items(s, carry):
+        for t in range(TOGETHER):
+            item = s * TOGETHER + t
+
+            @pl.when(item < total)
+            def _(item=item):
+                adj_copy(own_ref, 0, 0, item).wait()
+
+        for t in range(TOGETHER):
+            item = s * TOGETHER + t
+            real = item < total
+            item = jnp.where(real, item, 0)
+            what = list_ref[item]
+            row, c = what // chunks, what % chunks
+            j = jnp.bitwise_xor(core, row // per_side)
+            base = (j * per_side + row % per_side) * 16
+            count = jnp.where(real, meta_ref[base + slots], 0)
+            blocks = []
+            for k in range(CHUNK):
+                slot = c * CHUNK + k
+                block = meta_ref[base + slot]
+                found = table_ref[at + block // per_piece] * per_piece + block % per_piece
+                blocks.append(x_ref[jnp.where(slot < count, found, empty)])
+            acc_ref[row] += jnp.dot(
+                jnp.concatenate([adj_ref[item, k] for k in range(CHUNK)], axis=1),
+                jnp.concatenate(blocks, axis=0),
+                preferred_element_type=F32,
+            )
+        return carry
+
+    lax.fori_loop(0, (total + TOGETHER - 1) // TOGETHER, some_items, 0)
+    for side in range(CORE):
         j = jnp.bitwise_xor(core, side)
-
-        def some_rows(m, carry, side=side, ref=ref, j=j):
-            adj_copy(ref, side, m).wait()
-            for t in range(together):
-                i = m * together + t
-                base = (j * per_side + i) * 16
-                count = meta_ref[base + slots]
-                blocks = []
-                for k in range(slots):
-                    block = meta_ref[base + k]
-                    found = table_ref[at + block // per_piece] * per_piece + block % per_piece
-                    blocks.append(x_ref[jnp.where(k < count, found, empty)])
-                adj = [adj_ref[side * per_side + i, k] for k in range(slots)]
-                out_ref[i, j] = jnp.dot(
-                    jnp.concatenate(adj, axis=1),
-                    jnp.concatenate(blocks, axis=0),
-                    preferred_element_type=F32,
-                ).astype(out_ref.dtype)
-            return carry
-
-        lax.fori_loop(0, groups, some_rows, 0)
+        for i in range(per_side):
+            out_ref[i, j] = acc_ref[side * per_side + i].astype(out_ref.dtype)
 
 
 def spmm(meta, place, pieces, own, other):
     smem = pl.BlockSpec(memory_space=pltpu.SMEM)
     anywhere = pl.BlockSpec(memory_space=pl.ANY)
     blocks, bs, half = pieces[0].shape
-    rows = own.shape[0] * CORE
+    rows, slots = own.shape[0] * CORE, own.shape[1]
+    items = rows * (slots // CHUNK)
     return pl.pallas_call(
         spmm_kernel,
         out_shape=jax.ShapeDtypeStruct((NCOL, CORE, bs, half), BF16),
@@ -123,9 +148,11 @@
         out_specs=pl.BlockSpec(memory_space=pltpu.VMEM),
         scratch_shapes=[
             pltpu.VMEM((blocks * Y + 1, bs, half), BF16),
-            pltpu.VMEM((rows,) + own.shape[1:], BF16),
+            pltpu.VMEM((items, CHUNK, bs, bs), BF16),
+            pltpu.VMEM((rows, bs, half), F32),
+            pltpu.SMEM((items,), jnp.int32),
             pltpu.SemaphoreType.DMA((Y,)),
-            pltpu.SemaphoreType.DMA((rows // 4,)),
+            pltpu.SemaphoreType.DMA((items,)),
         ],
         compiler_params=pltpu.CompilerParams(vmem_limit_bytes=60 * 1024 * 1024),
     )(meta, jnp.asarray(piece_table().reshape(-1)), place, *pieces, own, other)
@@ -153,16 +180,17 @@
         return lax.dynamic_slice_in_dim(v, core * half, half, axis=v.ndim - 1)
 
     adj = adj_blocks[:, 0]
-    meta = jnp.concatenate(
-        [block_cols[:, 0], block_counts, jnp.zeros((NCOL, 16 - 13), jnp.int32)], axis=1
-    )
-    meta = lax.all_gather(meta, "core", axis=0, tiled=True).reshape(-1)
     place = jnp.stack([lax.axis_index("y"), core]).astype(jnp.int32)
 
     with jax.named_scope("pair_inputs"):
         grad_top = jnp.where(mask_top > 0, grad_out, jnp.zeros_like(grad_out))
-        grad_top, meta = lax.optimization_barrier((grad_top, meta))
-        unit_top = my_half(lax.all_gather(grad_top, "core", axis=0, tiled=True))
+        meta = jnp.concatenate([block_cols[:, 0], block_counts], axis=1).astype(BF16)
+        meta = jnp.pad(meta, ((0, 16 - meta.shape[0]), (0, feats - meta.shape[1])))
+        joined = lax.all_gather(jnp.concatenate([grad_top, meta], axis=0), "core", axis=0)
+        unit_top = my_half(joined[:, :bs]).reshape(CORE * bs, half)
+        meta = joined[:, bs : bs + NCOL, :16].astype(jnp.int32).reshape(-1)
+        unit_top, adj = lax.optimization_barrier((unit_top, adj))
+        other_adj = lax.ppermute(adj, "core", [(0, 1), (1, 0)])
         pair = lax.all_gather(
             jnp.stack([mask_mid.astype(BF16), feats_mid, feats_in]), "core", axis=1, tiled=True
         )
@@ -175,10 +203,7 @@
         return everyone(unit, "zl", ZL).reshape(-1, bs, half)
 
     with jax.named_scope("section_top"):
-        units = gather_z(unit_top)
-        adj, units = lax.optimization_barrier((adj, units))
-        other_adj = lax.ppermute(adj, "core", [(0, 1), (1, 0)])
-        pieces, other_adj = gather_y(units, other_adj)
+        pieces, other_adj = gather_y(gather_z(unit_top), other_adj)
         partial_top = spmm(meta, place, pieces, adj, other_adj)
         parts = lax.all_to_all(
             partial_top.reshape(NCOL, CORE * bs, half), COLS, 0, 0, tiled=True

time: 233 us -> 236 us (1.013)
  waiting for transfers between devices: 34.5 us -> 39.1 us
    ppermute x14, waiting for transfers between devices: 27.1 us -> 31.8 us  [swap(): return lax.ppermute(value, ('y', 'core'), y_pairs(which))]
    all_to_all x3, starting transfers between devices: 13.3 us -> 15.9 us  [everyone(): lax.all_to_all(jnp.broadcast_to(value[None], (count,) + value.shape), axe...]
    all_gather x2 -> x1, blocking collectives: 10.3 us -> 8.42 us  [local(): lax.all_gather(jnp.concatenate([grad_top, meta], axis=0), 'core', axis=0)]
  transfers between devices with their start and end apart: 19 -> 19, of which waited for: 16 -> 14; matrix products, arithmetic and copies ran while one was open for 2% -> 3% of each run, Pallas kernels for 0% -> 0%
where the time goes in v5:
time: 236 us; the launch traced here: 234 us
  blocking collectives  101 us (43%)
  starting transfers between devices  65.7 us (28%)
  waiting for transfers between devices  39.1 us (17%)
  Pallas kernels  12.8 us (5%)
  local copies, waits for them, and re-layouts  6.47 us (3%)
  other arithmetic  5.82 us (2%)
  matrix products  2.73 us (1%)
    ppermute x14, starting transfers between devices, swap(): return lax.ppermute(value, ('y', 'core'), y_pairs(which))  38.1 us
    ppermute x14, waiting for transfers between devices, swap(): return lax.ppermute(value, ('y', 'core'), y_pairs(which))  31.8 us
    all_to_all x2, blocking collectives, everyone(): lax.all_to_all(jnp.broadcast_to(value[None], (count,) + value.shape), axe...  22.9 us
    all_to_all x1, blocking collectives, local(): parts = lax.all_to_all(sent, COLS, 0, 0, tiled=True)  21.9 us
    all_to_all x3, starting transfers between devices, everyone(): lax.all_to_all(jnp.broadcast_to(value[None], (count,) + value.shape), axe...  15.9 us
    all_gather x1, blocking collectives, local(): own_nodes = lax.all_gather(agg_mid, 'core', axis=1, tiled=True)  13.9 us
    pallas_call x2, Pallas kernels, spmm(): pl.pallas_call(spmm_kernel, out_shape=jax.ShapeDtypeStruct((NCOL, CORE, b...  12.8 us
    all_gather x1, blocking collectives, local(): whole = lax.all_gather(over_x * norm_scale, 'core', axis=3, tiled=True)  11.9 us
  transfers between devices with their start and end apart: 19, of which 14 were waited for; matrix products, arithmetic and copies ran while one was open for 3% of the time, Pallas kernels for 0%

profile of v5, /device:TPU:1, one launch (start us, length us, event | category | flops | bytes accessed | tf_op | source)
XLA Modules:
  0.0 234.3 jit_solution(2960944718013440924)
XLA Ops:
  3.2 8.4 %all-gather = bf16[288,256]{1,0:T(8,128)(2,1)S(1)} all-gather(bf16[144,256]{1,0:T(8,128)(2,1)S(1)} %pad_maximum_fusion.2), channel_id=2, replica_groups=mesh['y'=8,'zl'=4,'core'=2,'x'=4,'zh'=2] {'core'}, dimensions={0}, use_global_device_ids=true | all-gather | bytes 221184 | tf_op jit(solution)/shard_map/pair_inputs/all_gather | solution.py:189
  14.6 10.6 %all_to_all.35 = bf16[4,256,128]{2,1,0:T(8,128)(2,1)S(1)} all-to-all(bf16[4,256,128]{2,1,0:T(8,128)(2,1)S(1)} %broadcast_in_dim.17), channel_id=1, replica_groups=mesh['y'=8,'zl'=4,'core'=2,'x'=4,'zh'=2] {'zl'}, dimensions={0} | all-to-all | bytes 524288 | tf_op jit(solution)/shard_map/section_top/all_to_all | solution.py:19
  25.2 3.2 %collective-permute-start = (bf16[8,128,128]{2,1,0:T(8,128)(2,1)S(1)}, bf16[8,128,128]{2,1,0:T(8,128)(2,1)S(1)}, u32[]{:S(2)}, u32[]{:S(2)}) collective-permute-start(bf16[8,128,128]{2,1,0:T(8,128)(2,1)S(1)} %bitcast.66), channel_id=1, source_target_pairs={{0,64},{8,456},{64,0},{72,136},{128,192},{136,72},{192,128},{200,2... | collective-permute-start | bytes 786440 | tf_op jit(solution)/shard_map/section_top/ppermute | solution.py:49
  30.3 3.2 %collective-permute-done.refs_1_ = bf16[8,128,128]{2,1,0:T(8,128)(2,1)S(1)} collective-permute-done((bf16[8,128,128]{2,1,0:T(8,128)(2,1)S(1)}, bf16[8,128,128]{2,1,0:T(8,128)(2,1)S(1)}, u32[]{:S(2)}, u32[]{:S(2)}) %collective-permute-start) | collective-permute-done | bytes 262176 | tf_op jit(solution)/shard_map/section_top/ppermute | solution.py:49
  37.6 4.1 %collective-permute-start.3 = (bf16[8,128,128]{2,1,0:T(8,128)(2,1)}, bf16[8,128,128]{2,1,0:T(8,128)(2,1)}, u32[]{:S(2)}, u32[]{:S(2)}) collective-permute-start(bf16[8,128,128]{2,1,0:T(8,128)(2,1)} %collective-permute-done.1.refs_2_), channel_id=1, source_target_pairs={{0,64},{8,456},{64,0},{72,136},{128,192},{136,72},{192,128},{200,2... | collective-permute-start | bytes 786440 | tf_op jit(solution)/shard_map/section_top/ppermute | solution.py:49
  44.2 4.3 %collective-permute-done.3.refs_4_ = bf16[8,128,128]{2,1,0:T(8,128)(2,1)} collective-permute-done((bf16[8,128,128]{2,1,0:T(8,128)(2,1)}, bf16[8,128,128]{2,1,0:T(8,128)(2,1)}, u32[]{:S(2)}, u32[]{:S(2)}) %collective-permute-start.3) | collective-permute-done | bytes 262176 | tf_op jit(solution)/shard_map/section_top/ppermute | solution.py:49
  58.4 3.2 %collective-permute-done.7.refs_7_ = bf16[8,128,128]{2,1,0:T(8,128)(2,1)} collective-permute-done((bf16[8,128,128]{2,1,0:T(8,128)(2,1)}, bf16[8,128,128]{2,1,0:T(8,128)(2,1)}, u32[]{:S(2)}, u32[]{:S(2)}) %collective-permute-start.7) | collective-permute-done | bytes 262176 | tf_op jit(solution)/shard_map/section_top/ppermute | solution.py:49
  61.6 6.4 %section_top.1 = bf16[8,2,128,128]{3,2,1,0:T(8,128)(2,1)} custom-call(s32[256]{0:T(256)} %reshape.85.meta_ref, s32[128]{0:T(128)} %constant.32.clone.table_ref, s32[2]{0:T(128)} %pad_add_fusion.place_ref, bf16[8,128,128]{2,1,0:T(8,128)(2,1)} %bitcast.68, bf16[8,128,128]{2,1,0:T(8,128)(2,1)} %copy-done.7, ...), custom_call_target="tpu_custom_call" | custom-call | tf_op jit(solution)/shard_map/section_top/pallas_call | solution.py:144
  68.0 9.4 %all-to-all-start.1 = ((bf16[8,256,128]{2,1,0:T(8,128)(2,1)}), bf16[8,256,128]{2,1,0:T(8,128)(2,1)S(1)}, u32[]{:S(2)}, u32[]{:S(2)}) async-start(bf16[8,256,128]{2,1,0:T(8,128)(2,1)} %bitcast.61), calls=%async_computation.1 | async-start | bytes 1048576 | tf_op jit(solution)/shard_map/section_top/all_to_all | solution.py:208
  79.2 11.1 %all_gather.20 = bf16[3,256,256]{2,1,0:T(8,128)(2,1)S(1)} all-gather(bf16[3,128,256]{2,1,0:T(8,128)(2,1)S(1)} %pad_maximum_fusion.1), channel_id=1, replica_groups=mesh['y'=8,'zl'=4,'core'=2,'x'=4,'zh'=2] {'core'}, dimensions={1}, use_global_device_ids=true | all-gather | bytes 589824 | tf_op jit(solution)/shard_map/pair_inputs/all_gather | solution.py:194
  90.4 10.6 %all_gather.21 = bf16[256,256]{1,0:T(8,128)(2,1)S(1)} all-gather(bf16[256,128]{1,0:T(8,128)(2,1)S(1)} %reduce_sum.42), channel_id=1, replica_groups=mesh['y'=8,'zl'=4,'core'=2,'x'=4,'zh'=2] {'core'}, dimensions={1}, use_global_device_ids=true | all-gather | bytes 196608 | tf_op jit(solution)/shard_map/section_top/all_gather | solution.py:212
  101.9 4.2 %all-to-all-start.2 = ((bf16[4,256,128]{2,1,0:T(8,128)(2,1)}), bf16[4,256,128]{2,1,0:T(8,128)(2,1)S(1)}, u32[]{:S(2)}, u32[]{:S(2)}) async-start(bf16[4,256,128]{2,1,0:T(8,128)(2,1)} %broadcast_in_dim.19), calls=%async_computation.2 | async-start | bytes 524288 | tf_op jit(solution)/shard_map/section_mid/all_to_all | solution.py:19
  106.2 7.3 %all-to-all-done.2 = bf16[4,256,128]{2,1,0:T(8,128)(2,1)S(1)} async-done(((bf16[4,256,128]{2,1,0:T(8,128)(2,1)}), bf16[4,256,128]{2,1,0:T(8,128)(2,1)S(1)}, u32[]{:S(2)}, u32[]{:S(2)}) %all-to-all-start.2) | async-done | bytes 262176 | tf_op jit(solution)/shard_map/section_mid/all_to_all | solution.py:19
  114.5 3.9 %all-to-all-start.3 = ((bf16[8,256,256]{1,2,0:T(8,128)(2,1)}), bf16[8,256,256]{1,2,0:T(8,128)(2,1)S(1)}, u32[]{:S(2)}, u32[]{:S(2)}) async-start(bf16[8,256,256]{1,2,0:T(8,128)(2,1)} %broadcast_in_dim.42), calls=%async_computation.3 | async-start | bytes 2097152 | tf_op jit(solution)/shard_map/group_feats/all_to_all | solution.py:19
  118.4 4.7 %collective-permute-start.8 = (bf16[8,128,128]{2,1,0:T(8,128)(2,1)S(1)}, bf16[8,128,128]{2,1,0:T(8,128)(2,1)S(1)}, u32[]{:S(2)}, u32[]{:S(2)}) collective-permute-start(bf16[8,128,128]{2,1,0:T(8,128)(2,1)S(1)} %bitcast.63), channel_id=1, source_target_pairs={{0,64},{8,456},{64,0},{72,136},{128,192},{136,72},{192,128},{200,2... | collective-permute-start | bytes 786440 | tf_op jit(solution)/shard_map/section_mid/ppermute | solution.py:49
  134.3 4.6 %collective-permute-start.12 = (bf16[8,128,128]{2,1,0:T(8,128)(2,1)S(1)}, bf16[8,128,128]{2,1,0:T(8,128)(2,1)}, u32[]{:S(2)}, u32[]{:S(2)}) collective-permute-start(bf16[8,128,128]{2,1,0:T(8,128)(2,1)S(1)} %collective-permute-done.10.refs_3_), channel_id=1, source_target_pairs={{0,64},{8,456},{64,0},{72,136},{128,192},{136,72},{192,128},{200,2... | collective-permute-start | bytes 786440 | tf_op jit(solution)/shard_map/section_mid/ppermute | solution.py:49
  138.9 3.9 %collective-permute-done.11.refs_4_ = bf16[8,128,128]{2,1,0:T(8,128)(2,1)S(1)} collective-permute-done((bf16[8,128,128]{2,1,0:T(8,128)(2,1)S(1)}, bf16[8,128,128]{2,1,0:T(8,128)(2,1)S(1)}, u32[]{:S(2)}, u32[]{:S(2)}) %collective-permute-start.11) | collective-permute-done | bytes 262176 | tf_op jit(solution)/shard_map/section_mid/ppermute | solution.py:49
  149.6 3.1 %collective-permute-done.13.refs_6_ = bf16[8,128,128]{2,1,0:T(8,128)(2,1)} collective-permute-done((bf16[8,128,128]{2,1,0:T(8,128)(2,1)S(1)}, bf16[8,128,128]{2,1,0:T(8,128)(2,1)}, u32[]{:S(2)}, u32[]{:S(2)}) %collective-permute-start.13) | collective-permute-done | bytes 262176 | tf_op jit(solution)/shard_map/section_mid/ppermute | solution.py:49
  155.6 6.4 %section_mid.1 = bf16[8,2,128,128]{3,2,1,0:T(8,128)(2,1)} custom-call(s32[256]{0:T(256)} %reshape.85.meta_ref, s32[128]{0:T(128)} %constant.32.clone.table_ref, s32[2]{0:T(128)} %pad_add_fusion.place_ref, bf16[8,128,128]{2,1,0:T(8,128)(2,1)} %bitcast.65, bf16[8,128,128]{2,1,0:T(8,128)(2,1)} %copy-done.6, bf16[8,128,128]{2,1,0:T(8,128)(2,1)} %copy-done.8, ...), custom_call_target="tpu_custom_call" | custom-call | tf_op jit(solution)/shard_map/section_mid/pallas_call | solution.py:144
  163.6 21.9 %all_to_all.36 = bf16[8,320,128]{2,1,0:T(8,128)(2,1)S(1)} all-to-all(bf16[8,320,128]{2,1,0:T(8,128)(2,1)S(1)} %pad_maximum_fusion), channel_id=1, replica_groups=mesh['y'=8,'zl'=4,'core'=2,'x'=4,'zh'=2] {'x','zh'}, dimensions={0} | all-to-all | bytes 1310720 | tf_op jit(solution)/shard_map/section_mid/all_to_all | solution.py:225
  185.6 12.3 %all_to_all.37 = bf16[8,64,128]{2,1,0:T(8,128)(2,1)S(1)} all-to-all(bf16[8,64,128]{2,1,0:T(8,128)(2,1)S(1)} %broadcast_in_dim.43), channel_id=1, replica_groups=mesh['y'=8,'zl'=4,'core'=2,'x'=4,'zh'=2] {'y'}, dimensions={0} | all-to-all | bytes 262144 | tf_op jit(solution)/shard_map/weight_sums/all_to_all | solution.py:19
  198.9 7.9 %all-to-all-start.6 = ((bf16[32,64,128]{2,1,0:T(8,128)(2,1)}), bf16[32,64,128]{2,1,0:T(8,128)(2,1)S(1)}, u32[]{:S(2)}, u32[]{:S(2)}) async-start(bf16[32,64,128]{2,1,0:T(8,128)(2,1)} %broadcast_in_dim.44), calls=%async_computation.6 | async-start | bytes 1048576 | tf_op jit(solution)/shard_map/weight_sums/all_to_all | solution.py:19
  206.8 13.9 %all_gather.22 = bf16[256,256]{1,0:T(8,128)(2,1)S(1)} all-gather(bf16[256,128]{1,0:T(8,128)(2,1)S(1)} %slice.45), channel_id=1, replica_groups=mesh['y'=8,'zl'=4,'core'=2,'x'=4,'zh'=2] {'core'}, dimensions={1}, use_global_device_ids=true | all-gather | bytes 196608 | tf_op jit(solution)/shard_map/section_mid/all_gather | solution.py:228
  221.6 11.9 %all_gather.23 = f32[8,2,32,256]{3,2,1,0:T(8,128)S(1)} all-gather(f32[8,2,32,128]{3,2,1,0:T(8,128)S(1)} %bitcast.69), channel_id=1, replica_groups=mesh['y'=8,'zl'=4,'core'=2,'x'=4,'zh'=2] {'core'}, dimensions={3}, use_global_device_ids=true | all-gather | bytes 786432 | tf_op jit(solution)/shard_map/weight_sums/all_gather | solution.py:238
  (86 shorter events, 53.0 us)
Async XLA Ops:
  0.6 100.3 %copy-start = (bf16[256,256]{1,0:T(8,128)(2,1)S(1)}, bf16[256,256]{1,0:T(8,128)(2,1)}, u32[]{:S(2)}) copy-start(bf16[256,256]{1,0:T(8,128)(2,1)} %param.18) | copy-start | bytes 393220
  12.3 39.0 %collective-permute-start.5 = (bf16[8,12,128,128]{3,2,1,0:T(8,128)(2,1)}, bf16[8,12,128,128]{3,2,1,0:T(8,128)(2,1)S(1)}, u32[]{:S(2)}, u32[]{:S(2)}) collective-permute-start(bf16[8,12,128,128]{3,2,1,0:T(8,128)(2,1)} %bitcast.54), channel_id=1, source_target_pairs={{0,8},{8,0},{1,9},{9,1},{2,10},{10,2},{3,11},{11,3},{4,12},{12,4},... | collective-permute-start | bytes 9437192 | tf_op jit(solution)/shard_map/pair_inputs/ppermute | solution.py:193
  25.2 36.3 %copy-start.4 = (bf16[4,256,128]{2,1,0:T(8,128)(2,1)}, bf16[4,256,128]{2,1,0:T(8,128)(2,1)S(1)}, u32[]{:S(2)}) copy-start(bf16[4,256,128]{2,1,0:T(8,128)(2,1)S(1)} %all_to_all.35) | copy-start | bytes 786436
  25.2 8.3 %collective-permute-start = (bf16[8,128,128]{2,1,0:T(8,128)(2,1)S(1)}, bf16[8,128,128]{2,1,0:T(8,128)(2,1)S(1)}, u32[]{:S(2)}, u32[]{:S(2)}) collective-permute-start(bf16[8,128,128]{2,1,0:T(8,128)(2,1)S(1)} %bitcast.66), channel_id=1, source_target_pairs={{0,64},{8,456},{64,0},{72,136},{128,192},{136,72},{192,128},{200,2... | collective-permute-start | bytes 786440 | tf_op jit(solution)/shard_map/section_top/ppermute | solution.py:49
  28.4 9.2 %collective-permute-start.1 = (bf16[8,128,128]{2,1,0:T(8,128)(2,1)S(1)}, bf16[8,128,128]{2,1,0:T(8,128)(2,1)}, u32[]{:S(2)}, u32[]{:S(2)}) collective-permute-start(bf16[8,128,128]{2,1,0:T(8,128)(2,1)S(1)} %bitcast.67), channel_id=1, source_target_pairs={{0,448},{8,72},{64,128},{72,8},{128,64},{136,200},{192,256},{200,1... | collective-permute-start | bytes 786440 | tf_op jit(solution)/shard_map/section_top/ppermute | solution.py:49
  33.5 8.2 %collective-permute-start.2 = (bf16[8,128,128]{2,1,0:T(8,128)(2,1)S(1)}, bf16[8,128,128]{2,1,0:T(8,128)(2,1)}, u32[]{:S(2)}, u32[]{:S(2)}) collective-permute-start(bf16[8,128,128]{2,1,0:T(8,128)(2,1)S(1)} %collective-permute-done.refs_1_), channel_id=1, source_target_pairs={{0,448},{8,72},{64,128},{72,8},{128,64},{136,200},{192,256},{200,1... | collective-permute-start | bytes 786440 | tf_op jit(solution)/shard_map/section_top/ppermute | solution.py:49
  37.6 10.9 %collective-permute-start.3 = (bf16[8,128,128]{2,1,0:T(8,128)(2,1)}, bf16[8,128,128]{2,1,0:T(8,128)(2,1)}, u32[]{:S(2)}, u32[]{:S(2)}) collective-permute-start(bf16[8,128,128]{2,1,0:T(8,128)(2,1)} %collective-permute-done.1.refs_2_), channel_id=1, source_target_pairs={{0,64},{8,456},{64,0},{72,136},{128,192},{136,72},{192,128},{200,2... | collective-permute-start | bytes 786440 | tf_op jit(solution)/shard_map/section_top/ppermute | solution.py:49
  41.7 9.6 %collective-permute-start.4 = (bf16[8,128,128]{2,1,0:T(8,128)(2,1)}, bf16[8,128,128]{2,1,0:T(8,128)(2,1)}, u32[]{:S(2)}, u32[]{:S(2)}) collective-permute-start(bf16[8,128,128]{2,1,0:T(8,128)(2,1)} %collective-permute-done.2.refs_3_), channel_id=1, source_target_pairs={{0,64},{8,456},{64,0},{72,136},{128,192},{136,72},{192,128},{200,2... | collective-permute-start | bytes 786440 | tf_op jit(solution)/shard_map/section_top/ppermute | solution.py:49
  48.5 9.9 %collective-permute-start.6 = (bf16[8,128,128]{2,1,0:T(8,128)(2,1)}, bf16[8,128,128]{2,1,0:T(8,128)(2,1)}, u32[]{:S(2)}, u32[]{:S(2)}) collective-permute-start(bf16[8,128,128]{2,1,0:T(8,128)(2,1)} %collective-permute-done.3.refs_4_), channel_id=1, source_target_pairs={{0,448},{8,72},{64,128},{72,8},{128,64},{136,200},{192,256},{200,1... | collective-permute-start | bytes 786440 | tf_op jit(solution)/shard_map/section_top/ppermute | solution.py:49
  51.3 10.2 %collective-permute-start.7 = (bf16[8,128,128]{2,1,0:T(8,128)(2,1)}, bf16[8,128,128]{2,1,0:T(8,128)(2,1)}, u32[]{:S(2)}, u32[]{:S(2)}) collective-permute-start(bf16[8,128,128]{2,1,0:T(8,128)(2,1)} %collective-permute-done.4.refs_5_), channel_id=1, source_target_pairs={{0,448},{8,72},{64,128},{72,8},{128,64},{136,200},{192,256},{200,1... | collective-permute-start | bytes 786440 | tf_op jit(solution)/shard_map/section_top/ppermute | solution.py:49
  68.0 22.3 %all-to-all-start.1 = ((bf16[8,256,128]{2,1,0:T(8,128)(2,1)}), bf16[8,256,128]{2,1,0:T(8,128)(2,1)S(1)}, u32[]{:S(2)}, u32[]{:S(2)}) async-start(bf16[8,256,128]{2,1,0:T(8,128)(2,1)} %bitcast.61), calls=%async_computation.1 | async-start | bytes 1048576 | tf_op jit(solution)/shard_map/section_top/all_to_all | solution.py:208
  101.9 11.6 %all-to-all-start.2 = ((bf16[4,256,128]{2,1,0:T(8,128)(2,1)}), bf16[4,256,128]{2,1,0:T(8,128)(2,1)S(1)}, u32[]{:S(2)}, u32[]{:S(2)}) async-start(bf16[4,256,128]{2,1,0:T(8,128)(2,1)} %broadcast_in_dim.19), calls=%async_computation.2 | async-start | bytes 524288 | tf_op jit(solution)/shard_map/section_mid/all_to_all | solution.py:19
  114.5 33.6 %all-to-all-start.3 = ((bf16[8,256,256]{1,2,0:T(8,128)(2,1)}), bf16[8,256,256]{1,2,0:T(8,128)(2,1)S(1)}, u32[]{:S(2)}, u32[]{:S(2)}) async-start(bf16[8,256,256]{1,2,0:T(8,128)(2,1)} %broadcast_in_dim.42), calls=%async_computation.3 | async-start | bytes 2097152 | tf_op jit(solution)/shard_map/group_feats/all_to_all | solution.py:19
  118.4 8.7 %collective-permute-start.8 = (bf16[8,128,128]{2,1,0:T(8,128)(2,1)S(1)}, bf16[8,128,128]{2,1,0:T(8,128)(2,1)S(1)}, u32[]{:S(2)}, u32[]{:S(2)}) collective-permute-start(bf16[8,128,128]{2,1,0:T(8,128)(2,1)S(1)} %bitcast.63), channel_id=1, source_target_pairs={{0,64},{8,456},{64,0},{72,136},{128,192},{136,72},{192,128},{200,2... | collective-permute-start | bytes 786440 | tf_op jit(solution)/shard_map/section_mid/ppermute | solution.py:49
  123.2 8.6 %collective-permute-start.9 = (bf16[8,128,128]{2,1,0:T(8,128)(2,1)S(1)}, bf16[8,128,128]{2,1,0:T(8,128)(2,1)S(1)}, u32[]{:S(2)}, u32[]{:S(2)}) collective-permute-start(bf16[8,128,128]{2,1,0:T(8,128)(2,1)S(1)} %bitcast.64), channel_id=1, source_target_pairs={{0,448},{8,72},{64,128},{72,8},{128,64},{136,200},{192,256},{200,1... | collective-permute-start | bytes 786440 | tf_op jit(solution)/shard_map/section_mid/ppermute | solution.py:49
  127.1 22.3 %copy-start.6 = (bf16[8,128,128]{2,1,0:T(8,128)(2,1)}, bf16[8,128,128]{2,1,0:T(8,128)(2,1)S(1)}, u32[]{:S(2)}) copy-start(bf16[8,128,128]{2,1,0:T(8,128)(2,1)S(1)} %collective-permute-done.8.refs_1_) | copy-start | bytes 786436
  127.1 7.2 %collective-permute-start.10 = (bf16[8,128,128]{2,1,0:T(8,128)(2,1)S(1)}, bf16[8,128,128]{2,1,0:T(8,128)(2,1)S(1)}, u32[]{:S(2)}, u32[]{:S(2)}) collective-permute-start(bf16[8,128,128]{2,1,0:T(8,128)(2,1)S(1)} %collective-permute-done.8.refs_1_), channel_id=1, source_target_pairs={{0,448},{8,72},{64,128},{72,8},{128,64},{136,200},{192,256},{200,1... | collective-permute-start | bytes 786440 | tf_op jit(solution)/shard_map/section_mid/ppermute | solution.py:49
  131.8 17.6 %copy-start.8 = (bf16[8,128,128]{2,1,0:T(8,128)(2,1)}, bf16[8,128,128]{2,1,0:T(8,128)(2,1)S(1)}, u32[]{:S(2)}) copy-start(bf16[8,128,128]{2,1,0:T(8,128)(2,1)S(1)} %collective-permute-done.9.refs_2_) | copy-start | bytes 786436
  131.8 11.0 %collective-permute-start.11 = (bf16[8,128,128]{2,1,0:T(8,128)(2,1)S(1)}, bf16[8,128,128]{2,1,0:T(8,128)(2,1)S(1)}, u32[]{:S(2)}, u32[]{:S(2)}) collective-permute-start(bf16[8,128,128]{2,1,0:T(8,128)(2,1)S(1)} %collective-permute-done.9.refs_2_), channel_id=1, source_target_pairs={{0,64},{8,456},{64,0},{72,136},{128,192},{136,72},{192,128},{200,2... | collective-permute-start | bytes 786440 | tf_op jit(solution)/shard_map/section_mid/ppermute | solution.py:49
  134.3 11.1 %collective-permute-start.12 = (bf16[8,128,128]{2,1,0:T(8,128)(2,1)S(1)}, bf16[8,128,128]{2,1,0:T(8,128)(2,1)}, u32[]{:S(2)}, u32[]{:S(2)}) collective-permute-start(bf16[8,128,128]{2,1,0:T(8,128)(2,1)S(1)} %collective-permute-done.10.refs_3_), channel_id=1, source_target_pairs={{0,64},{8,456},{64,0},{72,136},{128,192},{136,72},{192,128},{200,2... | collective-permute-start | bytes 786440 | tf_op jit(solution)/shard_map/section_mid/ppermute | solution.py:49
  142.8 9.9 %collective-permute-start.13 = (bf16[8,128,128]{2,1,0:T(8,128)(2,1)S(1)}, bf16[8,128,128]{2,1,0:T(8,128)(2,1)}, u32[]{:S(2)}, u32[]{:S(2)}) collective-permute-start(bf16[8,128,128]{2,1,0:T(8,128)(2,1)S(1)} %collective-permute-done.11.refs_4_), channel_id=1, source_target_pairs={{0,448},{8,72},{64,128},{72,8},{128,64},{136,200},{192,256},{200,1... | collective-permute-start | bytes 786440 | tf_op jit(solution)/shard_map/section_mid/ppermute | solution.py:49
  145.4 10.2 %collective-permute-start.14 = (bf16[8,128,128]{2,1,0:T(8,128)(2,1)}, bf16[8,128,128]{2,1,0:T(8,128)(2,1)}, u32[]{:S(2)}, u32[]{:S(2)}) collective-permute-start(bf16[8,128,128]{2,1,0:T(8,128)(2,1)} %collective-permute-done.12.refs_5_), channel_id=1, source_target_pairs={{0,448},{8,72},{64,128},{72,8},{128,64},{136,200},{192,256},{200,1... | collective-permute-start | bytes 786440 | tf_op jit(solution)/shard_map/section_mid/ppermute | solution.py:49
  185.6 35.0 %copy-start.11 = (bf16[256,256]{1,0:T(8,128)(2,1)S(1)}, bf16[256,256]{1,0:T(8,128)(2,1)}, u32[]{:S(2)}) copy-start(bf16[256,256]{1,0:T(8,128)(2,1)} %param.17) | copy-start | bytes 393220
  198.9 22.6 %all-to-all-start.6 = ((bf16[32,64,128]{2,1,0:T(8,128)(2,1)}), bf16[32,64,128]{2,1,0:T(8,128)(2,1)S(1)}, u32[]{:S(2)}, u32[]{:S(2)}) async-start(bf16[32,64,128]{2,1,0:T(8,128)(2,1)} %broadcast_in_dim.44), calls=%async_computation.6 | async-start | bytes 1048576 | tf_op jit(solution)/shard_map/weight_sums/all_to_all | solution.py:19
  (7 other events, 48.0 us)

commit v6 on v4

--- a/solution.py
+++ b/solution.py
@@ -43,17 +43,20 @@
     return table
 
 
-def gather_y(mine, beside=None):
+def gather_y(mine, beside=None, run=None):
     def swap(value, which):
         return lax.ppermute(value, ("y", "core"), y_pairs(which))
 
     first, second = swap(mine, 0), swap(mine, 1)
+    if run is not None:
+        first, second, beside = lax.optimization_barrier((first, second, beside))
+        beside = run(beside)
     third, fourth = swap(first, 1), swap(second, 0)
+    if run is not None:
+        third, fourth, beside = lax.optimization_barrier((third, fourth, beside))
     fifth, sixth = swap(third, 0), swap(fourth, 1)
-    if beside is not None:
-        fifth, beside = lax.optimization_barrier((fifth, beside))
-    last = swap(fifth, 1)
-    return (mine, first, second, third, fourth, fifth, sixth, last), beside
+    opposite = lax.ppermute(mine, "y", [(y, (y + Y // 2) % Y) for y in range(Y)])
+    return (mine, first, second, third, fourth, fifth, sixth, opposite), beside
 
 
 def spmm_kernel(meta_ref, table_ref, place_ref, *refs):
@@ -156,18 +159,22 @@
     meta = jnp.concatenate(
         [block_cols[:, 0], block_counts, jnp.zeros((NCOL, 16 - 13), jnp.int32)], axis=1
     )
-    meta = lax.all_gather(meta, "core", axis=0, tiled=True).reshape(-1)
     place = jnp.stack([lax.axis_index("y"), core]).astype(jnp.int32)
 
     with jax.named_scope("pair_inputs"):
         grad_top = jnp.where(mask_top > 0, grad_out, jnp.zeros_like(grad_out))
-        grad_top, meta = lax.optimization_barrier((grad_top, meta))
         unit_top = my_half(lax.all_gather(grad_top, "core", axis=0, tiled=True))
         pair = lax.all_gather(
             jnp.stack([mask_mid.astype(BF16), feats_mid, feats_in]), "core", axis=1, tiled=True
         )
         mask_pair = my_half(pair[0])
         feats_mid_pair = pair[1]
+
+    def pair_blocks(blocks):
+        adj, meta = blocks
+        meta = lax.all_gather(meta, "core", axis=0, tiled=True).reshape(-1)
+        return lax.ppermute(adj, "core", [(0, 1), (1, 0)]), meta
+
     with jax.named_scope("group_feats"):
         feats_in_group = everyone(pair[2], COLS, NCOL).reshape(-1, feats)
 
@@ -175,10 +182,7 @@
         return everyone(unit, "zl", ZL).reshape(-1, bs, half)
 
     with jax.named_scope("section_top"):
-        units = gather_z(unit_top)
-        adj, units = lax.optimization_barrier((adj, units))
-        other_adj = lax.ppermute(adj, "core", [(0, 1), (1, 0)])
-        pieces, other_adj = gather_y(units, other_adj)
+        pieces, (other_adj, meta) = gather_y(gather_z(unit_top), (adj, meta), pair_blocks)
         partial_top = spmm(meta, place, pieces, adj, other_adj)
         parts = lax.all_to_all(
             partial_top.reshape(NCOL, CORE * bs, half), COLS, 0, 0, tiled=True
@@ -190,7 +194,8 @@
         hidden = times_transpose(agg_top_both, weight_half)
         grad_mid = jnp.where(mask_pair > 0, hidden, jnp.zeros_like(hidden)).astype(BF16)
     with jax.named_scope("section_mid"):
-        partial_mid = spmm(meta, place, gather_y(gather_z(grad_mid))[0], adj, other_adj)
+        pieces, _ = gather_y(gather_z(grad_mid))
+        partial_mid = spmm(meta, place, pieces, adj, other_adj)
         term_first = contract_rows(feats_in_group, partial_mid.reshape(-1, half))
         terms = jnp.stack([term_first, term_second]).astype(BF16)
         terms = terms.reshape(2, NCOL, feats // NCOL, half).transpose(1, 0, 2, 3)

time: 233 us -> 236 us (1.013)
  blocking collectives: 103 us -> 76.7 us
  waiting for transfers between devices: 34.5 us -> 59.7 us
  starting transfers between devices: 66.5 us -> 71.3 us
    all_to_all x1, waiting for transfers between devices: 0.06 us -> 10.9 us  [local(): lax.all_to_all(partial_top.reshape(NCOL, CORE * bs, half), COLS, 0, 0, ti...]
    all_gather x1, blocking collectives: 14.1 us -> 4.26 us  [local(): own_nodes = lax.all_gather(agg_mid, 'core', axis=1, tiled=True)]
    ppermute x1 -> x3, starting transfers between devices: 3.38 us -> 12.3 us  [the longest x2 9.03 us: gather_y(): lax.ppermute(mine, 'y', [(y, (y + Y // 2) % Y) for y in range(Y)])]
    all_to_all x3, waiting for transfers between devices: 7.31 us -> 14.6 us  [everyone(): lax.all_to_all(jnp.broadcast_to(value[None], (count,) + value.shape), axe...]
    all_gather x1, blocking collectives: 10.7 us -> 3.53 us  [local(): agg_top_both = lax.all_gather(agg_top, 'core', axis=1, tiled=True)]
    all_gather x1, blocking collectives: 9.68 us -> 2.74 us  [local(): lax.all_gather(jnp.stack([mask_mid.astype(BF16), feats_mid, feats_in]), '...]
    ppermute x1 -> x3, waiting for transfers between devices: 0.01 us -> 6.92 us  [the longest x2 6.91 us: gather_y(): lax.ppermute(mine, 'y', [(y, (y + Y // 2) % Y) for y in range(Y)])]
    ppermute x14 -> x12, starting transfers between devices: 40.1 us -> 33.4 us  [swap(): return lax.ppermute(value, ('y', 'core'), y_pairs(which))]
  transfers between devices with their start and end apart: 19 -> 19, of which waited for: 16 -> 13; matrix products, arithmetic and copies ran while one was open for 2% -> 2% of each run, Pallas kernels for 0% -> 0%
where the time goes in v6:
time: 236 us; the launch traced here: 235 us
  blocking collectives  76.7 us (32%)
  starting transfers between devices  71.3 us (30%)
  waiting for transfers between devices  59.7 us (25%)
  Pallas kernels  13.2 us (6%)
  local copies, waits for them, and re-layouts  6.55 us (3%)
  other arithmetic  3.77 us (2%)
  matrix products  2.72 us (1%)
    ppermute x12, starting transfers between devices, swap(): return lax.ppermute(value, ('y', 'core'), y_pairs(which))  33.4 us
    ppermute x12, waiting for transfers between devices, swap(): return lax.ppermute(value, ('y', 'core'), y_pairs(which))  27.2 us
    all_to_all x1, blocking collectives, local(): parts = lax.all_to_all(sent, COLS, 0, 0, tiled=True)  24.8 us
    all_to_all x2, blocking collectives, everyone(): lax.all_to_all(jnp.broadcast_to(value[None], (count,) + value.shape), axe...  23.4 us
    all_to_all x3, starting transfers between devices, everyone(): lax.all_to_all(jnp.broadcast_to(value[None], (count,) + value.shape), axe...  16 us
    all_to_all x3, waiting for transfers between devices, everyone(): lax.all_to_all(jnp.broadcast_to(value[None], (count,) + value.shape), axe...  14.6 us
    pallas_call x2, Pallas kernels, spmm(): pl.pallas_call(spmm_kernel, out_shape=jax.ShapeDtypeStruct((NCOL, CORE, b...  13.2 us
    all_to_all x1, waiting for transfers between devices, local(): lax.all_to_all(partial_top.reshape(NCOL, CORE * bs, half), COLS, 0, 0, ti...  10.9 us
  transfers between devices with their start and end apart: 19, of which 13 were waited for; matrix products, arithmetic and copies ran while one was open for 2% of the time, Pallas kernels for 0%

profile of v6, /device:TPU:1, one launch (start us, length us, event | category | flops | bytes accessed | tf_op | source)
XLA Modules:
  0.0 235.1 jit_solution(15046224500878263447)
XLA Ops:
  1.7 8.4 %all_gather.18 = bf16[256,256]{1,0:T(8,128)(2,1)S(1)} all-gather(bf16[128,256]{1,0:T(8,128)(2,1)S(1)} %compare_select_fusion), channel_id=1, replica_groups=mesh['y'=8,'zl'=4,'core'=2,'x'=4,'zh'=2] {'core'}, dimensions={0}, use_global_device_ids=true | all-gather | bytes 196608 | tf_op jit(solution)/shard_map/pair_inputs/all_gather | solution.py:166
  10.1 10.7 %all_to_all.35 = bf16[4,256,128]{2,1,0:T(8,128)(2,1)S(1)} all-to-all(bf16[4,256,128]{2,1,0:T(8,128)(2,1)S(1)} %broadcast_in_dim.17), channel_id=1, replica_groups=mesh['y'=8,'zl'=4,'core'=2,'x'=4,'zh'=2] {'zl'}, dimensions={0} | all-to-all | bytes 524288 | tf_op jit(solution)/shard_map/section_top/all_to_all | solution.py:18
  29.1 3.9 %collective-permute-done.1.refs_2_ = bf16[8,128,128]{2,1,0:T(8,128)(2,1)S(1)} collective-permute-done((bf16[8,128,128]{2,1,0:T(8,128)(2,1)S(1)}, bf16[8,128,128]{2,1,0:T(8,128)(2,1)S(1)}, u32[]{:S(2)}, u32[]{:S(2)}) %collective-permute-start.1) | collective-permute-done | bytes 262176 | tf_op jit(solution)/shard_map/section_top/ppermute | solution.py:48
  38.9 4.9 %collective-permute-start.3 = (bf16[8,128,128]{2,1,0:T(8,128)(2,1)}, bf16[8,128,128]{2,1,0:T(8,128)(2,1)}, u32[]{:S(2)}, u32[]{:S(2)}) collective-permute-start(bf16[8,128,128]{2,1,0:T(8,128)(2,1)} %copy-done.6), channel_id=1, source_target_pairs={{0,64},{8,456},{64,0},{72,136},{128,192},{136,72},{192,128},{200,2... | collective-permute-start | bytes 786440 | tf_op jit(solution)/shard_map/section_top/ppermute | solution.py:48
  43.7 3.6 %collective-permute-start.7 = (bf16[8,128,128]{2,1,0:T(8,128)(2,1)S(1)}, bf16[8,128,128]{2,1,0:T(8,128)(2,1)}, u32[]{:S(2)}, u32[]{:S(2)}) collective-permute-start(bf16[8,128,128]{2,1,0:T(8,128)(2,1)S(1)} %bitcast.65), channel_id=1, source_target_pairs={{0,256},{64,320},{128,384},{192,448},{256,0},{320,64},{384,128},{4... | collective-permute-start | bytes 786440 | tf_op jit(solution)/shard_map/section_top/ppermute | solution.py:58
  50.5 4.1 %collective-permute-start.5 = (bf16[8,128,128]{2,1,0:T(8,128)(2,1)}, bf16[8,128,128]{2,1,0:T(8,128)(2,1)}, u32[]{:S(2)}, u32[]{:S(2)}) collective-permute-start(bf16[8,128,128]{2,1,0:T(8,128)(2,1)} %collective-permute-done.2.refs_3_), channel_id=1, source_target_pairs={{0,64},{8,456},{64,0},{72,136},{128,192},{136,72},{192,128},{200,2... | collective-permute-start | bytes 786440 | tf_op jit(solution)/shard_map/section_top/ppermute | solution.py:48
  59.4 7.4 %collective-permute-done.5.refs_5_ = bf16[8,128,128]{2,1,0:T(8,128)(2,1)} collective-permute-done((bf16[8,128,128]{2,1,0:T(8,128)(2,1)}, bf16[8,128,128]{2,1,0:T(8,128)(2,1)}, u32[]{:S(2)}, u32[]{:S(2)}) %collective-permute-start.5) | collective-permute-done | bytes 262176 | tf_op jit(solution)/shard_map/section_top/ppermute | solution.py:48
  66.9 6.6 %section_top.1 = bf16[8,2,128,128]{3,2,1,0:T(8,128)(2,1)} custom-call(s32[256]{0:T(256)} %reshape.68.meta_ref, s32[128]{0:T(128)} %constant.32.clone.table_ref, s32[2]{0:T(128)} %pad_add_fusion.place_ref, bf16[8,128,128]{2,1,0:T(8,128)(2,1)} %bitcast.66, bf16[8,128,128]{2,1,0:T(8,128)(2,1)} %copy-done.5, bf16[8,128,128]{2,1,0:T(8,128)(2,1)} %copy-done.6, ...), custom_call_target="tpu_custom_call" | custom-call | tf_op jit(solution)/shard_map/section_top/pallas_call | solution.py:122
  73.5 9.8 %all-to-all-start.1 = ((bf16[8,256,128]{2,1,0:T(8,128)(2,1)}), bf16[8,256,128]{2,1,0:T(8,128)(2,1)S(1)}, u32[]{:S(2)}, u32[]{:S(2)}) async-start(bf16[8,256,128]{2,1,0:T(8,128)(2,1)} %bitcast.57), calls=%async_computation.1 | async-start | bytes 1048576 | tf_op jit(solution)/shard_map/section_top/all_to_all | solution.py:187
  87.9 10.9 %all-to-all-done.1 = bf16[8,256,128]{2,1,0:T(8,128)(2,1)S(1)} async-done(((bf16[8,256,128]{2,1,0:T(8,128)(2,1)}), bf16[8,256,128]{2,1,0:T(8,128)(2,1)S(1)}, u32[]{:S(2)}, u32[]{:S(2)}) %all-to-all-start.1) | async-done | bytes 524320 | tf_op jit(solution)/shard_map/section_top/all_to_all | solution.py:187
  103.3 4.3 %all-to-all-start.2 = ((bf16[4,256,128]{2,1,0:T(8,128)(2,1)}), bf16[4,256,128]{2,1,0:T(8,128)(2,1)S(1)}, u32[]{:S(2)}, u32[]{:S(2)}) async-start(bf16[4,256,128]{2,1,0:T(8,128)(2,1)} %broadcast_in_dim.19), calls=%async_computation.2 | async-start | bytes 524288 | tf_op jit(solution)/shard_map/section_mid/all_to_all | solution.py:18
  107.8 7.3 %all-to-all-done.2 = bf16[4,256,128]{2,1,0:T(8,128)(2,1)S(1)} async-done(((bf16[4,256,128]{2,1,0:T(8,128)(2,1)}), bf16[4,256,128]{2,1,0:T(8,128)(2,1)S(1)}, u32[]{:S(2)}, u32[]{:S(2)}) %all-to-all-start.2) | async-done | bytes 262176 | tf_op jit(solution)/shard_map/section_mid/all_to_all | solution.py:18
  116.1 3.6 %all-to-all-start.3 = ((bf16[8,256,256]{1,2,0:T(8,128)(2,1)}), bf16[8,256,256]{1,2,0:T(8,128)(2,1)S(1)}, u32[]{:S(2)}, u32[]{:S(2)}) async-start(bf16[8,256,256]{1,2,0:T(8,128)(2,1)} %broadcast_in_dim.42), calls=%async_computation.3 | async-start | bytes 2097152 | tf_op jit(solution)/shard_map/group_feats/all_to_all | solution.py:18
  119.7 4.3 %collective-permute-start.8 = (bf16[8,128,128]{2,1,0:T(8,128)(2,1)S(1)}, bf16[8,128,128]{2,1,0:T(8,128)(2,1)S(1)}, u32[]{:S(2)}, u32[]{:S(2)}) collective-permute-start(bf16[8,128,128]{2,1,0:T(8,128)(2,1)S(1)} %bitcast.59), channel_id=1, source_target_pairs={{0,64},{8,456},{64,0},{72,136},{128,192},{136,72},{192,128},{200,2... | collective-permute-start | bytes 786440 | tf_op jit(solution)/shard_map/section_mid/ppermute | solution.py:48
  135.7 5.4 %collective-permute-start.14 = (bf16[8,128,128]{2,1,0:T(8,128)(2,1)S(1)}, bf16[8,128,128]{2,1,0:T(8,128)(2,1)}, u32[]{:S(2)}, u32[]{:S(2)}) collective-permute-start(bf16[8,128,128]{2,1,0:T(8,128)(2,1)S(1)} %bitcast.61), channel_id=1, source_target_pairs={{0,256},{64,320},{128,384},{192,448},{256,0},{320,64},{384,128},{4... | collective-permute-start | bytes 786440 | tf_op jit(solution)/shard_map/section_mid/ppermute | solution.py:58
  148.1 4.7 %collective-permute-done.14.refs_7_ = bf16[8,128,128]{2,1,0:T(8,128)(2,1)} collective-permute-done((bf16[8,128,128]{2,1,0:T(8,128)(2,1)S(1)}, bf16[8,128,128]{2,1,0:T(8,128)(2,1)}, u32[]{:S(2)}, u32[]{:S(2)}) %collective-permute-start.14) | collective-permute-done | bytes 262176 | tf_op jit(solution)/shard_map/section_mid/ppermute | solution.py:58
  152.8 6.9 %collective-permute-done.12.refs_5_ = bf16[8,128,128]{2,1,0:T(8,128)(2,1)} collective-permute-done((bf16[8,128,128]{2,1,0:T(8,128)(2,1)}, bf16[8,128,128]{2,1,0:T(8,128)(2,1)}, u32[]{:S(2)}, u32[]{:S(2)}) %collective-permute-start.12) | collective-permute-done | bytes 262176 | tf_op jit(solution)/shard_map/section_mid/ppermute | solution.py:48
  159.7 6.6 %section_mid.1 = bf16[8,2,128,128]{3,2,1,0:T(8,128)(2,1)} custom-call(s32[256]{0:T(256)} %reshape.68.meta_ref, s32[128]{0:T(128)} %constant.32.clone.table_ref, s32[2]{0:T(128)} %pad_add_fusion.place_ref, bf16[8,128,128]{2,1,0:T(8,128)(2,1)} %bitcast.62, bf16[8,128,128]{2,1,0:T(8,128)(2,1)} %copy-done.7, bf16[8,128,128]{2,1,0:T(8,128)(2,1)} %copy-done.8, ...), custom_call_target="tpu_custom_call" | custom-call | tf_op jit(solution)/shard_map/section_mid/pallas_call | solution.py:122
  168.0 24.8 %all_to_all.36 = bf16[8,320,128]{2,1,0:T(8,128)(2,1)S(1)} all-to-all(bf16[8,320,128]{2,1,0:T(8,128)(2,1)S(1)} %pad_maximum_fusion), channel_id=1, replica_groups=mesh['y'=8,'zl'=4,'core'=2,'x'=4,'zh'=2] {'x','zh'}, dimensions={0} | all-to-all | bytes 1310720 | tf_op jit(solution)/shard_map/section_mid/all_to_all | solution.py:205
  192.9 12.7 %all_to_all.37 = bf16[8,64,128]{2,1,0:T(8,128)(2,1)S(1)} all-to-all(bf16[8,64,128]{2,1,0:T(8,128)(2,1)S(1)} %broadcast_in_dim.43), channel_id=1, replica_groups=mesh['y'=8,'zl'=4,'core'=2,'x'=4,'zh'=2] {'y'}, dimensions={0} | all-to-all | bytes 262144 | tf_op jit(solution)/shard_map/weight_sums/all_to_all | solution.py:18
  206.6 8.1 %all-to-all-start.6 = ((bf16[32,64,128]{2,1,0:T(8,128)(2,1)}), bf16[32,64,128]{2,1,0:T(8,128)(2,1)S(1)}, u32[]{:S(2)}, u32[]{:S(2)}) async-start(bf16[32,64,128]{2,1,0:T(8,128)(2,1)} %broadcast_in_dim.44), calls=%async_computation.6 | async-start | bytes 1048576 | tf_op jit(solution)/shard_map/weight_sums/all_to_all | solution.py:18
  214.7 4.3 %all_gather.22 = bf16[256,256]{1,0:T(8,128)(2,1)S(1)} all-gather(bf16[256,128]{1,0:T(8,128)(2,1)S(1)} %slice.35), channel_id=1, replica_groups=mesh['y'=8,'zl'=4,'core'=2,'x'=4,'zh'=2] {'core'}, dimensions={1}, use_global_device_ids=true | all-gather | bytes 196608 | tf_op jit(solution)/shard_map/section_mid/all_gather | solution.py:208
  219.8 7.3 %all-to-all-done.6 = bf16[32,64,128]{2,1,0:T(8,128)(2,1)S(1)} async-done(((bf16[32,64,128]{2,1,0:T(8,128)(2,1)}), bf16[32,64,128]{2,1,0:T(8,128)(2,1)S(1)}, u32[]{:S(2)}, u32[]{:S(2)}) %all-to-all-start.6) | async-done | bytes 524320 | tf_op jit(solution)/shard_map/weight_sums/all_to_all | solution.py:18
  227.2 7.0 %all_gather.23 = f32[8,2,32,256]{3,2,1,0:T(8,128)S(1)} all-gather(f32[8,2,32,128]{3,2,1,0:T(8,128)S(1)} %bitcast.67), channel_id=1, replica_groups=mesh['y'=8,'zl'=4,'core'=2,'x'=4,'zh'=2] {'core'}, dimensions={3}, use_global_device_ids=true | all-gather | bytes 786432 | tf_op jit(solution)/shard_map/weight_sums/all_gather | solution.py:218
  (84 shorter events, 56.5 us)
Async XLA Ops:
  0.6 101.8 %copy-start = (bf16[256,256]{1,0:T(8,128)(2,1)S(1)}, bf16[256,256]{1,0:T(8,128)(2,1)}, u32[]{:S(2)}) copy-start(bf16[256,256]{1,0:T(8,128)(2,1)} %param.18) | copy-start | bytes 393220
  0.6 24.9 %copy-start.11 = (s32[8,1]{0,1:T(1,128)S(1)}, s32[8,1]{0,1:T(1,128)}, u32[]{:S(2)}) copy-start(s32[8,1]{0,1:T(1,128)} %param.21) | copy-start | bytes 100
  0.7 25.1 %copy-start.10 = (s32[8,1,12]{2,1,0:T(1,128)S(1)}, s32[8,1,12]{2,1,0:T(1,128)}, u32[]{:S(2)}) copy-start(s32[8,1,12]{2,1,0:T(1,128)} %param.20) | copy-start | bytes 1156
  20.8 46.1 %copy-start.4 = (bf16[4,256,128]{2,1,0:T(8,128)(2,1)}, bf16[4,256,128]{2,1,0:T(8,128)(2,1)S(1)}, u32[]{:S(2)}) copy-start(bf16[4,256,128]{2,1,0:T(8,128)(2,1)S(1)} %all_to_all.35) | copy-start | bytes 786436
  20.8 8.3 %collective-permute-start = (bf16[8,128,128]{2,1,0:T(8,128)(2,1)S(1)}, bf16[8,128,128]{2,1,0:T(8,128)(2,1)S(1)}, u32[]{:S(2)}, u32[]{:S(2)}) collective-permute-start(bf16[8,128,128]{2,1,0:T(8,128)(2,1)S(1)} %bitcast.63), channel_id=1, source_target_pairs={{0,64},{8,456},{64,0},{72,136},{128,192},{136,72},{192,128},{200,2... | collective-permute-start | bytes 786440 | tf_op jit(solution)/shard_map/section_top/ppermute | solution.py:48
  23.7 9.4 %collective-permute-start.1 = (bf16[8,128,128]{2,1,0:T(8,128)(2,1)S(1)}, bf16[8,128,128]{2,1,0:T(8,128)(2,1)S(1)}, u32[]{:S(2)}, u32[]{:S(2)}) collective-permute-start(bf16[8,128,128]{2,1,0:T(8,128)(2,1)S(1)} %bitcast.64), channel_id=1, source_target_pairs={{0,448},{8,72},{64,128},{72,8},{128,64},{136,200},{192,256},{200,1... | collective-permute-start | bytes 786440 | tf_op jit(solution)/shard_map/section_top/ppermute | solution.py:48
  33.7 16.8 %collective-permute-start.4 = (bf16[8,12,128,128]{3,2,1,0:T(8,128)(2,1)}, bf16[8,12,128,128]{3,2,1,0:T(8,128)(2,1)S(1)}, u32[]{:S(2)}, u32[]{:S(2)}) collective-permute-start(bf16[8,12,128,128]{3,2,1,0:T(8,128)(2,1)} %bitcast.50), channel_id=1, source_target_pairs={{0,8},{8,0},{1,9},{9,1},{2,10},{10,2},{3,11},{11,3},{4,12},{12,4},... | collective-permute-start | bytes 9437192 | tf_op jit(solution)/shard_map/section_top/ppermute | solution.py:176
  36.9 13.6 %collective-permute-start.2 = (bf16[8,128,128]{2,1,0:T(8,128)(2,1)}, bf16[8,128,128]{2,1,0:T(8,128)(2,1)}, u32[]{:S(2)}, u32[]{:S(2)}) collective-permute-start(bf16[8,128,128]{2,1,0:T(8,128)(2,1)} %copy-done.5), channel_id=1, source_target_pairs={{0,448},{8,72},{64,128},{72,8},{128,64},{136,200},{192,256},{200,1... | collective-permute-start | bytes 786440 | tf_op jit(solution)/shard_map/section_top/ppermute | solution.py:48
  38.9 11.7 %collective-permute-start.3 = (bf16[8,128,128]{2,1,0:T(8,128)(2,1)}, bf16[8,128,128]{2,1,0:T(8,128)(2,1)}, u32[]{:S(2)}, u32[]{:S(2)}) collective-permute-start(bf16[8,128,128]{2,1,0:T(8,128)(2,1)} %copy-done.6), channel_id=1, source_target_pairs={{0,64},{8,456},{64,0},{72,136},{128,192},{136,72},{192,128},{200,2... | collective-permute-start | bytes 786440 | tf_op jit(solution)/shard_map/section_top/ppermute | solution.py:48
  43.7 15.7 %collective-permute-start.7 = (bf16[8,128,128]{2,1,0:T(8,128)(2,1)S(1)}, bf16[8,128,128]{2,1,0:T(8,128)(2,1)}, u32[]{:S(2)}, u32[]{:S(2)}) collective-permute-start(bf16[8,128,128]{2,1,0:T(8,128)(2,1)S(1)} %bitcast.65), channel_id=1, source_target_pairs={{0,256},{64,320},{128,384},{192,448},{256,0},{320,64},{384,128},{4... | collective-permute-start | bytes 786440 | tf_op jit(solution)/shard_map/section_top/ppermute | solution.py:58
  50.5 16.2 %collective-permute-start.5 = (bf16[8,128,128]{2,1,0:T(8,128)(2,1)}, bf16[8,128,128]{2,1,0:T(8,128)(2,1)}, u32[]{:S(2)}, u32[]{:S(2)}) collective-permute-start(bf16[8,128,128]{2,1,0:T(8,128)(2,1)} %collective-permute-done.2.refs_3_), channel_id=1, source_target_pairs={{0,64},{8,456},{64,0},{72,136},{128,192},{136,72},{192,128},{200,2... | collective-permute-start | bytes 786440 | tf_op jit(solution)/shard_map/section_top/ppermute | solution.py:48
  54.7 12.2 %collective-permute-start.6 = (bf16[8,128,128]{2,1,0:T(8,128)(2,1)}, bf16[8,128,128]{2,1,0:T(8,128)(2,1)}, u32[]{:S(2)}, u32[]{:S(2)}) collective-permute-start(bf16[8,128,128]{2,1,0:T(8,128)(2,1)} %collective-permute-done.3.refs_4_), channel_id=1, source_target_pairs={{0,448},{8,72},{64,128},{72,8},{128,64},{136,200},{192,256},{200,1... | collective-permute-start | bytes 786440 | tf_op jit(solution)/shard_map/section_top/ppermute | solution.py:48
  73.5 25.3 %all-to-all-start.1 = ((bf16[8,256,128]{2,1,0:T(8,128)(2,1)}), bf16[8,256,128]{2,1,0:T(8,128)(2,1)S(1)}, u32[]{:S(2)}, u32[]{:S(2)}) async-start(bf16[8,256,128]{2,1,0:T(8,128)(2,1)} %bitcast.57), calls=%async_computation.1 | async-start | bytes 1048576 | tf_op jit(solution)/shard_map/section_top/all_to_all | solution.py:187
  103.3 11.7 %all-to-all-start.2 = ((bf16[4,256,128]{2,1,0:T(8,128)(2,1)}), bf16[4,256,128]{2,1,0:T(8,128)(2,1)S(1)}, u32[]{:S(2)}, u32[]{:S(2)}) async-start(bf16[4,256,128]{2,1,0:T(8,128)(2,1)} %broadcast_in_dim.19), calls=%async_computation.2 | async-start | bytes 524288 | tf_op jit(solution)/shard_map/section_mid/all_to_all | solution.py:18
  116.1 30.6 %all-to-all-start.3 = ((bf16[8,256,256]{1,2,0:T(8,128)(2,1)}), bf16[8,256,256]{1,2,0:T(8,128)(2,1)S(1)}, u32[]{:S(2)}, u32[]{:S(2)}) async-start(bf16[8,256,256]{1,2,0:T(8,128)(2,1)} %broadcast_in_dim.42), calls=%async_computation.3 | async-start | bytes 2097152 | tf_op jit(solution)/shard_map/group_feats/all_to_all | solution.py:18
  119.7 8.5 %collective-permute-start.8 = (bf16[8,128,128]{2,1,0:T(8,128)(2,1)S(1)}, bf16[8,128,128]{2,1,0:T(8,128)(2,1)S(1)}, u32[]{:S(2)}, u32[]{:S(2)}) collective-permute-start(bf16[8,128,128]{2,1,0:T(8,128)(2,1)S(1)} %bitcast.59), channel_id=1, source_target_pairs={{0,64},{8,456},{64,0},{72,136},{128,192},{136,72},{192,128},{200,2... | collective-permute-start | bytes 786440 | tf_op jit(solution)/shard_map/section_mid/ppermute | solution.py:48
  124.0 8.8 %collective-permute-start.9 = (bf16[8,128,128]{2,1,0:T(8,128)(2,1)S(1)}, bf16[8,128,128]{2,1,0:T(8,128)(2,1)S(1)}, u32[]{:S(2)}, u32[]{:S(2)}) collective-permute-start(bf16[8,128,128]{2,1,0:T(8,128)(2,1)S(1)} %bitcast.60), channel_id=1, source_target_pairs={{0,448},{8,72},{64,128},{72,8},{128,64},{136,200},{192,256},{200,1... | collective-permute-start | bytes 786440 | tf_op jit(solution)/shard_map/section_mid/ppermute | solution.py:48
  128.2 12.9 %collective-permute-start.10 = (bf16[8,128,128]{2,1,0:T(8,128)(2,1)S(1)}, bf16[8,128,128]{2,1,0:T(8,128)(2,1)}, u32[]{:S(2)}, u32[]{:S(2)}) collective-permute-start(bf16[8,128,128]{2,1,0:T(8,128)(2,1)S(1)} %collective-permute-done.8.refs_1_), channel_id=1, source_target_pairs={{0,448},{8,72},{64,128},{72,8},{128,64},{136,200},{192,256},{200,1... | collective-permute-start | bytes 786440 | tf_op jit(solution)/shard_map/section_mid/ppermute | solution.py:48
  132.8 11.9 %collective-permute-start.11 = (bf16[8,128,128]{2,1,0:T(8,128)(2,1)S(1)}, bf16[8,128,128]{2,1,0:T(8,128)(2,1)}, u32[]{:S(2)}, u32[]{:S(2)}) collective-permute-start(bf16[8,128,128]{2,1,0:T(8,128)(2,1)S(1)} %collective-permute-done.9.refs_2_), channel_id=1, source_target_pairs={{0,64},{8,456},{64,0},{72,136},{128,192},{136,72},{192,128},{200,2... | collective-permute-start | bytes 786440 | tf_op jit(solution)/shard_map/section_mid/ppermute | solution.py:48
  135.7 17.1 %collective-permute-start.14 = (bf16[8,128,128]{2,1,0:T(8,128)(2,1)S(1)}, bf16[8,128,128]{2,1,0:T(8,128)(2,1)}, u32[]{:S(2)}, u32[]{:S(2)}) collective-permute-start(bf16[8,128,128]{2,1,0:T(8,128)(2,1)S(1)} %bitcast.61), channel_id=1, source_target_pairs={{0,256},{64,320},{128,384},{192,448},{256,0},{320,64},{384,128},{4... | collective-permute-start | bytes 786440 | tf_op jit(solution)/shard_map/section_mid/ppermute | solution.py:58
  141.2 18.5 %collective-permute-start.12 = (bf16[8,128,128]{2,1,0:T(8,128)(2,1)}, bf16[8,128,128]{2,1,0:T(8,128)(2,1)}, u32[]{:S(2)}, u32[]{:S(2)}) collective-permute-start(bf16[8,128,128]{2,1,0:T(8,128)(2,1)} %collective-permute-done.10.refs_3_), channel_id=1, source_target_pairs={{0,64},{8,456},{64,0},{72,136},{128,192},{136,72},{192,128},{200,2... | collective-permute-start | bytes 786440 | tf_op jit(solution)/shard_map/section_mid/ppermute | solution.py:48
  144.7 15.0 %collective-permute-start.13 = (bf16[8,128,128]{2,1,0:T(8,128)(2,1)}, bf16[8,128,128]{2,1,0:T(8,128)(2,1)}, u32[]{:S(2)}, u32[]{:S(2)}) collective-permute-start(bf16[8,128,128]{2,1,0:T(8,128)(2,1)} %collective-permute-done.11.refs_4_), channel_id=1, source_target_pairs={{0,448},{8,72},{64,128},{72,8},{128,64},{136,200},{192,256},{200,1... | collective-permute-start | bytes 786440 | tf_op jit(solution)/shard_map/section_mid/ppermute | solution.py:48
  192.9 26.1 %copy-start.9 = (bf16[256,256]{1,0:T(8,128)(2,1)S(1)}, bf16[256,256]{1,0:T(8,128)(2,1)}, u32[]{:S(2)}) copy-start(bf16[256,256]{1,0:T(8,128)(2,1)} %param.17) | copy-start | bytes 393220
  206.6 20.5 %all-to-all-start.6 = ((bf16[32,64,128]{2,1,0:T(8,128)(2,1)}), bf16[32,64,128]{2,1,0:T(8,128)(2,1)S(1)}, u32[]{:S(2)}, u32[]{:S(2)}) async-start(bf16[32,64,128]{2,1,0:T(8,128)(2,1)} %broadcast_in_dim.44), calls=%async_computation.6 | async-start | bytes 1048576 | tf_op jit(solution)/shard_map/weight_sums/all_to_all | solution.py:18
  (7 other events, 78.1 us)

commit v7 on v4

--- a/solution.py
+++ b/solution.py
@@ -43,17 +43,19 @@
     return table
 
 
-def gather_y(mine, beside=None):
+def gather_y(mine, early=None, late=None):
     def swap(value, which):
         return lax.ppermute(value, ("y", "core"), y_pairs(which))
 
     first, second = swap(mine, 0), swap(mine, 1)
     third, fourth = swap(first, 1), swap(second, 0)
+    if early is not None:
+        third, early = lax.optimization_barrier((third, early))
     fifth, sixth = swap(third, 0), swap(fourth, 1)
-    if beside is not None:
-        fifth, beside = lax.optimization_barrier((fifth, beside))
+    if late is not None:
+        fifth, late = lax.optimization_barrier((fifth, late))
     last = swap(fifth, 1)
-    return (mine, first, second, third, fourth, fifth, sixth, last), beside
+    return (mine, first, second, third, fourth, fifth, sixth, last), early, late
 
 
 def spmm_kernel(meta_ref, table_ref, place_ref, *refs):
@@ -161,24 +163,24 @@
 
     with jax.named_scope("pair_inputs"):
         grad_top = jnp.where(mask_top > 0, grad_out, jnp.zeros_like(grad_out))
-        grad_top, meta = lax.optimization_barrier((grad_top, meta))
         unit_top = my_half(lax.all_gather(grad_top, "core", axis=0, tiled=True))
         pair = lax.all_gather(
-            jnp.stack([mask_mid.astype(BF16), feats_mid, feats_in]), "core", axis=1, tiled=True
+            jnp.stack([mask_mid.astype(BF16), feats_mid]), "core", axis=1, tiled=True
         )
         mask_pair = my_half(pair[0])
         feats_mid_pair = pair[1]
-    with jax.named_scope("group_feats"):
-        feats_in_group = everyone(pair[2], COLS, NCOL).reshape(-1, feats)
-
     def gather_z(unit):
         return everyone(unit, "zl", ZL).reshape(-1, bs, half)
 
     with jax.named_scope("section_top"):
         units = gather_z(unit_top)
-        adj, units = lax.optimization_barrier((adj, units))
+        feats_in_pair = lax.all_gather(feats_in, "core", axis=0, tiled=True)
+        adj, feats_in_pair, units = lax.optimization_barrier((adj, feats_in_pair, units))
         other_adj = lax.ppermute(adj, "core", [(0, 1), (1, 0)])
-        pieces, other_adj = gather_y(units, other_adj)
+        feats_in_group = everyone(feats_in_pair, COLS, NCOL).reshape(-1, feats)
+        pieces, meta, (other_adj, feats_in_group) = gather_y(
+            units, meta, (other_adj, feats_in_group)
+        )
         partial_top = spmm(meta, place, pieces, adj, other_adj)
         parts = lax.all_to_all(
             partial_top.reshape(NCOL, CORE * bs, half), COLS, 0, 0, tiled=True

time: 233 us -> 231 us (level)
  blocking collectives: 103 us -> 91.2 us
  starting transfers between devices: 66.5 us -> 72.2 us
  local copies, waits for them, and re-layouts: 6.54 us -> 10 us
    all_to_all x1, waiting for transfers between devices: 0.06 us -> 7.4 us  [local(): lax.all_to_all(partial_top.reshape(NCOL, CORE * bs, half), COLS, 0, 0, ti...]
    all_gather x1, blocking collectives: 1.9 us -> 8.43 us  [local(): unit_top = my_half(lax.all_gather(grad_top, 'core', axis=0, tiled=True))]
    all_to_all x1, blocking collectives: 22.4 us -> 16.4 us  [local(): parts = lax.all_to_all(sent, COLS, 0, 0, tiled=True)]
    all_gather x1, blocking collectives: 10.7 us -> 4.92 us  [local(): agg_top_both = lax.all_gather(agg_top, 'core', axis=1, tiled=True)]
    ppermute x14, waiting for transfers between devices: 27.1 us -> 22.3 us  [swap(): return lax.ppermute(value, ('y', 'core'), y_pairs(which))]
    all_gather x1, blocking collectives: 8.36 us -> 5.23 us  [local(): meta = lax.all_gather(meta, 'core', axis=0, tiled=True).reshape(-1)]
    all_to_all x3, starting transfers between devices: 13.3 us -> 16.4 us  [everyone(): lax.all_to_all(jnp.broadcast_to(value[None], (count,) + value.shape), axe...]
    ppermute x14, starting transfers between devices: 40.1 us -> 42.8 us  [swap(): return lax.ppermute(value, ('y', 'core'), y_pairs(which))]
  transfers between devices with their start and end apart: 19 -> 19, of which waited for: 16 -> 12; matrix products, arithmetic and copies ran while one was open for 2% -> 5% of each run, Pallas kernels for 0% -> 0%
where the time goes in v7:
time: 231 us; the launch traced here: 230 us
  blocking collectives  91.2 us (39%)
  starting transfers between devices  72.2 us (31%)
  waiting for transfers between devices  36 us (16%)
  Pallas kernels  13.2 us (6%)
  local copies, waits for them, and re-layouts  10 us (4%)
  other arithmetic  3.79 us (2%)
  matrix products  2.72 us (1%)
    ppermute x14, starting transfers between devices, swap(): return lax.ppermute(value, ('y', 'core'), y_pairs(which))  42.8 us
    all_to_all x2, blocking collectives, everyone(): lax.all_to_all(jnp.broadcast_to(value[None], (count,) + value.shape), axe...  23.2 us
    ppermute x14, waiting for transfers between devices, swap(): return lax.ppermute(value, ('y', 'core'), y_pairs(which))  22.3 us
    all_to_all x3, starting transfers between devices, everyone(): lax.all_to_all(jnp.broadcast_to(value[None], (count,) + value.shape), axe...  16.4 us
    all_to_all x1, blocking collectives, local(): parts = lax.all_to_all(sent, COLS, 0, 0, tiled=True)  16.4 us
    all_gather x1, blocking collectives, local(): own_nodes = lax.all_gather(agg_mid, 'core', axis=1, tiled=True)  13.6 us
    pallas_call x2, Pallas kernels, spmm(): pl.pallas_call(spmm_kernel, out_shape=jax.ShapeDtypeStruct((NCOL, CORE, b...  13.2 us
    all_gather x1, blocking collectives, local(): whole = lax.all_gather(over_x * norm_scale, 'core', axis=3, tiled=True)  11.9 us
  transfers between devices with their start and end apart: 19, of which 12 were waited for; matrix products, arithmetic and copies ran while one was open for 5% of the time, Pallas kernels for 0%

profile of v7, /device:TPU:1, one launch (start us, length us, event | category | flops | bytes accessed | tf_op | source)
XLA Modules:
  0.0 230.2 jit_solution(17344977410480414645)
XLA Ops:
  1.7 8.4 %all_gather.22 = bf16[256,256]{1,0:T(8,128)(2,1)S(1)} all-gather(bf16[128,256]{1,0:T(8,128)(2,1)S(1)} %compare_select_fusion), channel_id=1, replica_groups=mesh['y'=8,'zl'=4,'core'=2,'x'=4,'zh'=2] {'core'}, dimensions={0}, use_global_device_ids=true | all-gather | bytes 196608 | tf_op jit(solution)/shard_map/pair_inputs/all_gather | solution.py:166
  16.3 5.4 %all-to-all-done = bf16[4,256,128]{2,1,0:T(8,128)(2,1)S(1)} async-done(((bf16[4,256,128]{2,1,0:T(8,128)(2,1)}), bf16[4,256,128]{2,1,0:T(8,128)(2,1)S(1)}, u32[]{:S(2)}, u32[]{:S(2)}) %all-to-all-start) | async-done | bytes 262176 | tf_op jit(solution)/shard_map/section_top/all_to_all | solution.py:18
  21.7 4.3 %collective-permute-start.5 = (bf16[8,12,128,128]{3,2,1,0:T(8,128)(2,1)}, bf16[8,12,128,128]{3,2,1,0:T(8,128)(2,1)S(1)}, u32[]{:S(2)}, u32[]{:S(2)}) collective-permute-start(bf16[8,12,128,128]{3,2,1,0:T(8,128)(2,1)} %bitcast.46), channel_id=1, source_target_pairs={{0,8},{8,0},{1,9},{9,1},{2,10},{10,2},{3,11},{11,3},{4,12},{12,4},... | collective-permute-start | bytes 9437192 | tf_op jit(solution)/shard_map/section_top/ppermute | solution.py:179
  29.5 8.2 %all-to-all-start.1 = ((bf16[8,256,256]{1,2,0:T(8,128)(2,1)}), bf16[8,256,256]{1,2,0:T(8,128)(2,1)}, u32[]{:S(2)}, u32[]{:S(2)}) async-start(bf16[8,256,256]{1,2,0:T(8,128)(2,1)} %broadcast_in_dim.16), calls=%async_computation.1 | async-start | bytes 2097152 | tf_op jit(solution)/shard_map/section_top/all_to_all | solution.py:18
  37.7 5.1 %collective-permute-start = (bf16[8,128,128]{2,1,0:T(8,128)(2,1)S(1)}, bf16[8,128,128]{2,1,0:T(8,128)(2,1)}, u32[]{:S(2)}, u32[]{:S(2)}) collective-permute-start(bf16[8,128,128]{2,1,0:T(8,128)(2,1)S(1)} %bitcast.55), channel_id=1, source_target_pairs={{0,64},{8,456},{64,0},{72,136},{128,192},{136,72},{192,128},{200,2... | collective-permute-start | bytes 786440 | tf_op jit(solution)/shard_map/section_top/ppermute | solution.py:48
  49.1 5.2 %all_gather.23 = s32[16,16]{1,0:T(8,128)S(1)} all-gather(s32[8,16]{1,0:T(8,128)S(1)} %add_add_fusion), channel_id=1, replica_groups=mesh['y'=8,'zl'=4,'core'=2,'x'=4,'zh'=2] {'core'}, dimensions={0}, use_global_device_ids=true | all-gather | bytes 1536 | tf_op jit(solution)/shard_map/all_gather | solution.py:161
  56.9 4.6 %collective-permute-start.4 = (bf16[8,128,128]{2,1,0:T(8,128)(2,1)}, bf16[8,128,128]{2,1,0:T(8,128)(2,1)}, u32[]{:S(2)}, u32[]{:S(2)}) collective-permute-start(bf16[8,128,128]{2,1,0:T(8,128)(2,1)} %collective-permute-done.1.refs_3_), channel_id=1, source_target_pairs={{0,64},{8,456},{64,0},{72,136},{128,192},{136,72},{192,128},{200,2... | collective-permute-start | bytes 786440 | tf_op jit(solution)/shard_map/section_top/ppermute | solution.py:48
  72.5 3.6 %collective-permute-done.7.refs_7_ = bf16[8,128,128]{2,1,0:T(8,128)(2,1)} collective-permute-done((bf16[8,128,128]{2,1,0:T(8,128)(2,1)}, bf16[8,128,128]{2,1,0:T(8,128)(2,1)}, u32[]{:S(2)}, u32[]{:S(2)}) %collective-permute-start.7) | collective-permute-done | bytes 262176 | tf_op jit(solution)/shard_map/section_top/ppermute | solution.py:48
  76.2 6.6 %section_top.1 = bf16[8,2,128,128]{3,2,1,0:T(8,128)(2,1)} custom-call(s32[256]{0:T(256)} %reshape.69.meta_ref, s32[128]{0:T(128)} %constant.32.clone.table_ref, s32[2]{0:T(128)} %pad_add_fusion.place_ref, bf16[8,128,128]{2,1,0:T(8,128)(2,1)} %bitcast.57, bf16[8,128,128]{2,1,0:T(8,128)(2,1)} %collective-permute-done.refs_1_, ...), custom_call_target="tpu_custom_call" | custom-call | tf_op jit(solution)/shard_map/section_top/pallas_call | solution.py:121
  82.8 8.6 %all-to-all-start.2 = ((bf16[8,256,128]{2,1,0:T(8,128)(2,1)}), bf16[8,256,128]{2,1,0:T(8,128)(2,1)S(1)}, u32[]{:S(2)}, u32[]{:S(2)}) async-start(bf16[8,256,128]{2,1,0:T(8,128)(2,1)} %bitcast.53), calls=%async_computation.2 | async-start | bytes 1048576 | tf_op jit(solution)/shard_map/section_top/all_to_all | solution.py:185
  93.2 5.5 %all_gather.24 = bf16[2,256,256]{2,1,0:T(8,128)(2,1)S(1)} all-gather(bf16[2,128,256]{2,1,0:T(8,128)(2,1)S(1)} %pad_maximum_fusion.1), channel_id=1, replica_groups=mesh['y'=8,'zl'=4,'core'=2,'x'=4,'zh'=2] {'core'}, dimensions={1}, use_global_device_ids=true | all-gather | bytes 393216 | tf_op jit(solution)/shard_map/pair_inputs/all_gather | solution.py:167
  98.7 7.4 %all-to-all-done.2 = bf16[8,256,128]{2,1,0:T(8,128)(2,1)S(1)} async-done(((bf16[8,256,128]{2,1,0:T(8,128)(2,1)}), bf16[8,256,128]{2,1,0:T(8,128)(2,1)S(1)}, u32[]{:S(2)}, u32[]{:S(2)}) %all-to-all-start.2) | async-done | bytes 524320 | tf_op jit(solution)/shard_map/section_top/all_to_all | solution.py:185
  106.2 4.9 %all_gather.25 = bf16[256,256]{1,0:T(8,128)(2,1)S(1)} all-gather(bf16[256,128]{1,0:T(8,128)(2,1)S(1)} %reduce_sum.42), channel_id=1, replica_groups=mesh['y'=8,'zl'=4,'core'=2,'x'=4,'zh'=2] {'core'}, dimensions={1}, use_global_device_ids=true | all-gather | bytes 196608 | tf_op jit(solution)/shard_map/section_top/all_gather | solution.py:189
  111.4 10.3 %all_to_all.35 = bf16[4,256,128]{2,1,0:T(8,128)(2,1)S(1)} all-to-all(bf16[4,256,128]{2,1,0:T(8,128)(2,1)S(1)} %broadcast_in_dim.18), channel_id=1, replica_groups=mesh['y'=8,'zl'=4,'core'=2,'x'=4,'zh'=2] {'zl'}, dimensions={0} | all-to-all | bytes 524288 | tf_op jit(solution)/shard_map/section_mid/all_to_all | solution.py:18
  121.7 3.5 %collective-permute-start.8 = (bf16[8,128,128]{2,1,0:T(8,128)(2,1)S(1)}, bf16[8,128,128]{2,1,0:T(8,128)(2,1)S(1)}, u32[]{:S(2)}, u32[]{:S(2)}) collective-permute-start(bf16[8,128,128]{2,1,0:T(8,128)(2,1)S(1)} %bitcast.58), channel_id=1, source_target_pairs={{0,64},{8,456},{64,0},{72,136},{128,192},{136,72},{192,128},{200,2... | collective-permute-start | bytes 786440 | tf_op jit(solution)/shard_map/section_mid/ppermute | solution.py:48
  125.2 4.0 %collective-permute-start.9 = (bf16[8,128,128]{2,1,0:T(8,128)(2,1)S(1)}, bf16[8,128,128]{2,1,0:T(8,128)(2,1)S(1)}, u32[]{:S(2)}, u32[]{:S(2)}) collective-permute-start(bf16[8,128,128]{2,1,0:T(8,128)(2,1)S(1)} %bitcast.59), channel_id=1, source_target_pairs={{0,448},{8,72},{64,128},{72,8},{128,64},{136,200},{192,256},{200,1... | collective-permute-start | bytes 786440 | tf_op jit(solution)/shard_map/section_mid/ppermute | solution.py:48
  141.7 4.7 %collective-permute-done.11.refs_4_ = bf16[8,128,128]{2,1,0:T(8,128)(2,1)} collective-permute-done((bf16[8,128,128]{2,1,0:T(8,128)(2,1)S(1)}, bf16[8,128,128]{2,1,0:T(8,128)(2,1)}, u32[]{:S(2)}, u32[]{:S(2)}) %collective-permute-start.11) | collective-permute-done | bytes 262176 | tf_op jit(solution)/shard_map/section_mid/ppermute | solution.py:48
  152.7 3.6 %collective-permute-done.13.refs_6_ = bf16[8,128,128]{2,1,0:T(8,128)(2,1)} collective-permute-done((bf16[8,128,128]{2,1,0:T(8,128)(2,1)}, bf16[8,128,128]{2,1,0:T(8,128)(2,1)}, u32[]{:S(2)}, u32[]{:S(2)}) %collective-permute-start.13) | collective-permute-done | bytes 262176 | tf_op jit(solution)/shard_map/section_mid/ppermute | solution.py:48
  159.5 6.6 %section_mid.1 = bf16[8,2,128,128]{3,2,1,0:T(8,128)(2,1)} custom-call(s32[256]{0:T(256)} %reshape.69.meta_ref, s32[128]{0:T(128)} %constant.32.clone.table_ref, s32[2]{0:T(128)} %pad_add_fusion.place_ref, bf16[8,128,128]{2,1,0:T(8,128)(2,1)} %bitcast.60, bf16[8,128,128]{2,1,0:T(8,128)(2,1)} %copy-done.6, bf16[8,128,128]{2,1,0:T(8,128)(2,1)} %copy-done.7, ...), custom_call_target="tpu_custom_call" | custom-call | tf_op jit(solution)/shard_map/section_mid/pallas_call | solution.py:121
  167.8 16.4 %all_to_all.36 = bf16[8,320,128]{2,1,0:T(8,128)(2,1)S(1)} all-to-all(bf16[8,320,128]{2,1,0:T(8,128)(2,1)S(1)} %pad_maximum_fusion), channel_id=1, replica_groups=mesh['y'=8,'zl'=4,'core'=2,'x'=4,'zh'=2] {'x','zh'}, dimensions={0} | all-to-all | bytes 1310720 | tf_op jit(solution)/shard_map/section_mid/all_to_all | solution.py:202
  184.2 12.9 %all_to_all.37 = bf16[8,64,128]{2,1,0:T(8,128)(2,1)S(1)} all-to-all(bf16[8,64,128]{2,1,0:T(8,128)(2,1)S(1)} %broadcast_in_dim.19), channel_id=1, replica_groups=mesh['y'=8,'zl'=4,'core'=2,'x'=4,'zh'=2] {'y'}, dimensions={0} | all-to-all | bytes 262144 | tf_op jit(solution)/shard_map/weight_sums/all_to_all | solution.py:18
  198.1 4.8 %all-to-all-start.6 = ((bf16[32,64,128]{2,1,0:T(8,128)(2,1)}), bf16[32,64,128]{2,1,0:T(8,128)(2,1)S(1)}, u32[]{:S(2)}, u32[]{:S(2)}) async-start(bf16[32,64,128]{2,1,0:T(8,128)(2,1)} %broadcast_in_dim.20), calls=%async_computation.6 | async-start | bytes 1048576 | tf_op jit(solution)/shard_map/weight_sums/all_to_all | solution.py:18
  203.0 13.6 %all_gather.26 = bf16[256,256]{1,0:T(8,128)(2,1)S(1)} all-gather(bf16[256,128]{1,0:T(8,128)(2,1)S(1)} %slice.30), channel_id=1, replica_groups=mesh['y'=8,'zl'=4,'core'=2,'x'=4,'zh'=2] {'core'}, dimensions={1}, use_global_device_ids=true | all-gather | bytes 196608 | tf_op jit(solution)/shard_map/section_mid/all_gather | solution.py:205
  217.5 11.9 %all_gather.27 = f32[8,2,32,256]{3,2,1,0:T(8,128)S(1)} all-gather(f32[8,2,32,128]{3,2,1,0:T(8,128)S(1)} %bitcast.61), channel_id=1, replica_groups=mesh['y'=8,'zl'=4,'core'=2,'x'=4,'zh'=2] {'core'}, dimensions={3}, use_global_device_ids=true | all-gather | bytes 786432 | tf_op jit(solution)/shard_map/weight_sums/all_gather | solution.py:215
  (89 shorter events, 58.9 us)
Async XLA Ops:
  0.6 110.5 %copy-start = (bf16[256,256]{1,0:T(8,128)(2,1)S(1)}, bf16[256,256]{1,0:T(8,128)(2,1)}, u32[]{:S(2)}) copy-start(bf16[256,256]{1,0:T(8,128)(2,1)} %param.18) | copy-start | bytes 393220
  10.8 10.8 %all-to-all-start = ((bf16[4,256,128]{2,1,0:T(8,128)(2,1)}), bf16[4,256,128]{2,1,0:T(8,128)(2,1)S(1)}, u32[]{:S(2)}, u32[]{:S(2)}) async-start(bf16[4,256,128]{2,1,0:T(8,128)(2,1)} %broadcast_in_dim.15), calls=%async_computation | async-start | bytes 524288 | tf_op jit(solution)/shard_map/section_top/all_to_all | solution.py:18
  21.7 47.1 %collective-permute-start.5 = (bf16[8,12,128,128]{3,2,1,0:T(8,128)(2,1)}, bf16[8,12,128,128]{3,2,1,0:T(8,128)(2,1)S(1)}, u32[]{:S(2)}, u32[]{:S(2)}) collective-permute-start(bf16[8,12,128,128]{3,2,1,0:T(8,128)(2,1)} %bitcast.46), channel_id=1, source_target_pairs={{0,8},{8,0},{1,9},{9,1},{2,10},{10,2},{3,11},{11,3},{4,12},{12,4},... | collective-permute-start | bytes 9437192 | tf_op jit(solution)/shard_map/section_top/ppermute | solution.py:179
  29.5 36.9 %all-to-all-start.1 = ((bf16[8,256,256]{1,2,0:T(8,128)(2,1)}), bf16[8,256,256]{1,2,0:T(8,128)(2,1)}, u32[]{:S(2)}, u32[]{:S(2)}) async-start(bf16[8,256,256]{1,2,0:T(8,128)(2,1)} %broadcast_in_dim.16), calls=%async_computation.1 | async-start | bytes 2097152 | tf_op jit(solution)/shard_map/section_top/all_to_all | solution.py:18
  37.7 9.2 %collective-permute-start = (bf16[8,128,128]{2,1,0:T(8,128)(2,1)S(1)}, bf16[8,128,128]{2,1,0:T(8,128)(2,1)}, u32[]{:S(2)}, u32[]{:S(2)}) collective-permute-start(bf16[8,128,128]{2,1,0:T(8,128)(2,1)S(1)} %bitcast.55), channel_id=1, source_target_pairs={{0,64},{8,456},{64,0},{72,136},{128,192},{136,72},{192,128},{200,2... | collective-permute-start | bytes 786440 | tf_op jit(solution)/shard_map/section_top/ppermute | solution.py:48
  42.8 12.2 %collective-permute-start.2 = (bf16[8,128,128]{2,1,0:T(8,128)(2,1)S(1)}, bf16[8,128,128]{2,1,0:T(8,128)(2,1)}, u32[]{:S(2)}, u32[]{:S(2)}) collective-permute-start(bf16[8,128,128]{2,1,0:T(8,128)(2,1)S(1)} %bitcast.56), channel_id=1, source_target_pairs={{0,448},{8,72},{64,128},{72,8},{128,64},{136,200},{192,256},{200,1... | collective-permute-start | bytes 786440 | tf_op jit(solution)/shard_map/section_top/ppermute | solution.py:48
  47.0 10.0 %collective-permute-start.1 = (bf16[8,128,128]{2,1,0:T(8,128)(2,1)}, bf16[8,128,128]{2,1,0:T(8,128)(2,1)}, u32[]{:S(2)}, u32[]{:S(2)}) collective-permute-start(bf16[8,128,128]{2,1,0:T(8,128)(2,1)} %collective-permute-done.refs_1_), channel_id=1, source_target_pairs={{0,448},{8,72},{64,128},{72,8},{128,64},{136,200},{192,256},{200,1... | collective-permute-start | bytes 786440 | tf_op jit(solution)/shard_map/section_top/ppermute | solution.py:48
  55.0 8.5 %collective-permute-start.3 = (bf16[8,128,128]{2,1,0:T(8,128)(2,1)}, bf16[8,128,128]{2,1,0:T(8,128)(2,1)S(1)}, u32[]{:S(2)}, u32[]{:S(2)}) collective-permute-start(bf16[8,128,128]{2,1,0:T(8,128)(2,1)} %collective-permute-done.2.refs_2_), channel_id=1, source_target_pairs={{0,64},{8,456},{64,0},{72,136},{128,192},{136,72},{192,128},{200,2... | collective-permute-start | bytes 786440 | tf_op jit(solution)/shard_map/section_top/ppermute | solution.py:48
  56.9 11.8 %collective-permute-start.4 = (bf16[8,128,128]{2,1,0:T(8,128)(2,1)}, bf16[8,128,128]{2,1,0:T(8,128)(2,1)}, u32[]{:S(2)}, u32[]{:S(2)}) collective-permute-start(bf16[8,128,128]{2,1,0:T(8,128)(2,1)} %collective-permute-done.1.refs_3_), channel_id=1, source_target_pairs={{0,64},{8,456},{64,0},{72,136},{128,192},{136,72},{192,128},{200,2... | collective-permute-start | bytes 786440 | tf_op jit(solution)/shard_map/section_top/ppermute | solution.py:48
  63.5 9.0 %collective-permute-start.6 = (bf16[8,128,128]{2,1,0:T(8,128)(2,1)S(1)}, bf16[8,128,128]{2,1,0:T(8,128)(2,1)}, u32[]{:S(2)}, u32[]{:S(2)}) collective-permute-start(bf16[8,128,128]{2,1,0:T(8,128)(2,1)S(1)} %collective-permute-done.3.refs_4_), channel_id=1, source_target_pairs={{0,448},{8,72},{64,128},{72,8},{128,64},{136,200},{192,256},{200,1... | collective-permute-start | bytes 786440 | tf_op jit(solution)/shard_map/section_top/ppermute | solution.py:48
  68.7 7.4 %collective-permute-start.7 = (bf16[8,128,128]{2,1,0:T(8,128)(2,1)}, bf16[8,128,128]{2,1,0:T(8,128)(2,1)}, u32[]{:S(2)}, u32[]{:S(2)}) collective-permute-start(bf16[8,128,128]{2,1,0:T(8,128)(2,1)} %collective-permute-done.4.refs_5_), channel_id=1, source_target_pairs={{0,448},{8,72},{64,128},{72,8},{128,64},{136,200},{192,256},{200,1... | collective-permute-start | bytes 786440 | tf_op jit(solution)/shard_map/section_top/ppermute | solution.py:48
  82.8 23.3 %all-to-all-start.2 = ((bf16[8,256,128]{2,1,0:T(8,128)(2,1)}), bf16[8,256,128]{2,1,0:T(8,128)(2,1)S(1)}, u32[]{:S(2)}, u32[]{:S(2)}) async-start(bf16[8,256,128]{2,1,0:T(8,128)(2,1)} %bitcast.53), calls=%async_computation.2 | async-start | bytes 1048576 | tf_op jit(solution)/shard_map/section_top/all_to_all | solution.py:185
  98.7 53.2 %copy-start.3 = (bf16[8,256,256]{2,1,0:T(8,128)(2,1)S(1)}, bf16[8,256,256]{2,1,0:T(8,128)(2,1)}, u32[]{:S(2)}) copy-start(bf16[8,256,256]{2,1,0:T(8,128)(2,1)} %copy.40) | copy-start | bytes 3145732
  121.7 31.0 %copy-start.5 = (bf16[4,256,128]{2,1,0:T(8,128)(2,1)}, bf16[4,256,128]{2,1,0:T(8,128)(2,1)S(1)}, u32[]{:S(2)}) copy-start(bf16[4,256,128]{2,1,0:T(8,128)(2,1)S(1)} %all_to_all.35) | copy-start | bytes 786436
  121.7 8.3 %collective-permute-start.8 = (bf16[8,128,128]{2,1,0:T(8,128)(2,1)S(1)}, bf16[8,128,128]{2,1,0:T(8,128)(2,1)S(1)}, u32[]{:S(2)}, u32[]{:S(2)}) collective-permute-start(bf16[8,128,128]{2,1,0:T(8,128)(2,1)S(1)} %bitcast.58), channel_id=1, source_target_pairs={{0,64},{8,456},{64,0},{72,136},{128,192},{136,72},{192,128},{200,2... | collective-permute-start | bytes 786440 | tf_op jit(solution)/shard_map/section_mid/ppermute | solution.py:48
  125.2 10.0 %collective-permute-start.9 = (bf16[8,128,128]{2,1,0:T(8,128)(2,1)S(1)}, bf16[8,128,128]{2,1,0:T(8,128)(2,1)S(1)}, u32[]{:S(2)}, u32[]{:S(2)}) collective-permute-start(bf16[8,128,128]{2,1,0:T(8,128)(2,1)S(1)} %bitcast.59), channel_id=1, source_target_pairs={{0,448},{8,72},{64,128},{72,8},{128,64},{136,200},{192,256},{200,1... | collective-permute-start | bytes 786440 | tf_op jit(solution)/shard_map/section_mid/ppermute | solution.py:48
  130.0 22.7 %copy-start.6 = (bf16[8,128,128]{2,1,0:T(8,128)(2,1)}, bf16[8,128,128]{2,1,0:T(8,128)(2,1)S(1)}, u32[]{:S(2)}) copy-start(bf16[8,128,128]{2,1,0:T(8,128)(2,1)S(1)} %collective-permute-done.8.refs_1_) | copy-start | bytes 786436
  130.0 8.7 %collective-permute-start.10 = (bf16[8,128,128]{2,1,0:T(8,128)(2,1)S(1)}, bf16[8,128,128]{2,1,0:T(8,128)(2,1)S(1)}, u32[]{:S(2)}, u32[]{:S(2)}) collective-permute-start(bf16[8,128,128]{2,1,0:T(8,128)(2,1)S(1)} %collective-permute-done.8.refs_1_), channel_id=1, source_target_pairs={{0,448},{8,72},{64,128},{72,8},{128,64},{136,200},{192,256},{200,1... | collective-permute-start | bytes 786440 | tf_op jit(solution)/shard_map/section_mid/ppermute | solution.py:48
  135.2 11.3 %collective-permute-start.11 = (bf16[8,128,128]{2,1,0:T(8,128)(2,1)S(1)}, bf16[8,128,128]{2,1,0:T(8,128)(2,1)}, u32[]{:S(2)}, u32[]{:S(2)}) collective-permute-start(bf16[8,128,128]{2,1,0:T(8,128)(2,1)S(1)} %collective-permute-done.9.refs_2_), channel_id=1, source_target_pairs={{0,64},{8,456},{64,0},{72,136},{128,192},{136,72},{192,128},{200,2... | collective-permute-start | bytes 786440 | tf_op jit(solution)/shard_map/section_mid/ppermute | solution.py:48
  138.7 10.4 %collective-permute-start.12 = (bf16[8,128,128]{2,1,0:T(8,128)(2,1)S(1)}, bf16[8,128,128]{2,1,0:T(8,128)(2,1)}, u32[]{:S(2)}, u32[]{:S(2)}) collective-permute-start(bf16[8,128,128]{2,1,0:T(8,128)(2,1)S(1)} %collective-permute-done.10.refs_3_), channel_id=1, source_target_pairs={{0,64},{8,456},{64,0},{72,136},{128,192},{136,72},{192,128},{200,2... | collective-permute-start | bytes 786440 | tf_op jit(solution)/shard_map/section_mid/ppermute | solution.py:48
  146.4 9.9 %collective-permute-start.13 = (bf16[8,128,128]{2,1,0:T(8,128)(2,1)}, bf16[8,128,128]{2,1,0:T(8,128)(2,1)}, u32[]{:S(2)}, u32[]{:S(2)}) collective-permute-start(bf16[8,128,128]{2,1,0:T(8,128)(2,1)} %collective-permute-done.11.refs_4_), channel_id=1, source_target_pairs={{0,448},{8,72},{64,128},{72,8},{128,64},{136,200},{192,256},{200,1... | collective-permute-start | bytes 786440 | tf_op jit(solution)/shard_map/section_mid/ppermute | solution.py:48
  149.1 10.3 %collective-permute-start.14 = (bf16[8,128,128]{2,1,0:T(8,128)(2,1)}, bf16[8,128,128]{2,1,0:T(8,128)(2,1)}, u32[]{:S(2)}, u32[]{:S(2)}) collective-permute-start(bf16[8,128,128]{2,1,0:T(8,128)(2,1)} %collective-permute-done.12.refs_5_), channel_id=1, source_target_pairs={{0,448},{8,72},{64,128},{72,8},{128,64},{136,200},{192,256},{200,1... | collective-permute-start | bytes 786440 | tf_op jit(solution)/shard_map/section_mid/ppermute | solution.py:48
  184.2 32.3 %copy-start.10 = (bf16[256,256]{1,0:T(8,128)(2,1)S(1)}, bf16[256,256]{1,0:T(8,128)(2,1)}, u32[]{:S(2)}) copy-start(bf16[256,256]{1,0:T(8,128)(2,1)} %param.17) | copy-start | bytes 393220
  198.1 19.3 %all-to-all-start.6 = ((bf16[32,64,128]{2,1,0:T(8,128)(2,1)}), bf16[32,64,128]{2,1,0:T(8,128)(2,1)S(1)}, u32[]{:S(2)}, u32[]{:S(2)}) async-start(bf16[32,64,128]{2,1,0:T(8,128)(2,1)} %broadcast_in_dim.20), calls=%async_computation.6 | async-start | bytes 1048576 | tf_op jit(solution)/shard_map/weight_sums/all_to_all | solution.py:18
  (9 other events, 126.8 us)

commit v8 on v7

--- a/solution.py
+++ b/solution.py
@@ -165,7 +165,7 @@
         grad_top = jnp.where(mask_top > 0, grad_out, jnp.zeros_like(grad_out))
         unit_top = my_half(lax.all_gather(grad_top, "core", axis=0, tiled=True))
         pair = lax.all_gather(
-            jnp.stack([mask_mid.astype(BF16), feats_mid]), "core", axis=1, tiled=True
+            jnp.stack([mask_mid.astype(BF16), feats_mid, feats_in]), "core", axis=1, tiled=True
         )
         mask_pair = my_half(pair[0])
         feats_mid_pair = pair[1]
@@ -174,13 +174,9 @@
 
     with jax.named_scope("section_top"):
         units = gather_z(unit_top)
-        feats_in_pair = lax.all_gather(feats_in, "core", axis=0, tiled=True)
-        adj, feats_in_pair, units = lax.optimization_barrier((adj, feats_in_pair, units))
+        adj, units = lax.optimization_barrier((adj, units))
         other_adj = lax.ppermute(adj, "core", [(0, 1), (1, 0)])
-        feats_in_group = everyone(feats_in_pair, COLS, NCOL).reshape(-1, feats)
-        pieces, meta, (other_adj, feats_in_group) = gather_y(
-            units, meta, (other_adj, feats_in_group)
-        )
+        pieces, meta, other_adj = gather_y(units, meta, other_adj)
         partial_top = spmm(meta, place, pieces, adj, other_adj)
         parts = lax.all_to_all(
             partial_top.reshape(NCOL, CORE * bs, half), COLS, 0, 0, tiled=True
@@ -192,7 +188,13 @@
         hidden = times_transpose(agg_top_both, weight_half)
         grad_mid = jnp.where(mask_pair > 0, hidden, jnp.zeros_like(hidden)).astype(BF16)
     with jax.named_scope("section_mid"):
-        partial_mid = spmm(meta, place, gather_y(gather_z(grad_mid))[0], adj, other_adj)
+        mine = pair[2]
+        other = lax.ppermute(mine, "zh", [(0, 1), (1, 0)])
+        units = gather_z(grad_mid)
+        first_zh = lax.axis_index("zh") == 0
+        both = jnp.stack([jnp.where(first_zh, mine, other), jnp.where(first_zh, other, mine)])
+        feats_in_group = everyone(both, "x", X).reshape(-1, feats)
+        partial_mid = spmm(meta, place, gather_y(units)[0], adj, other_adj)
         term_first = contract_rows(feats_in_group, partial_mid.reshape(-1, half))
         terms = jnp.stack([term_first, term_second]).astype(BF16)
         terms = terms.reshape(2, NCOL, feats // NCOL, half).transpose(1, 0, 2, 3)

time: 231 us -> 225 us (0.974)
  starting transfers between devices: 72.2 us -> 68.6 us
  local copies, waits for them, and re-layouts: 10 us -> 6.62 us
    ppermute x14, starting transfers between devices: 42.8 us -> 39.1 us  [swap(): return lax.ppermute(value, ('y', 'core'), y_pairs(which))]
    all_gather x2 -> x1, blocking collectives: 7.53 us -> 4.41 us  [local(): lax.all_gather(jnp.stack([mask_mid.astype(BF16), feats_mid, feats_in]), '...]
    ppermute x14, waiting for transfers between devices: 22.3 us -> 25.1 us  [swap(): return lax.ppermute(value, ('y', 'core'), y_pairs(which))]
    all_gather x1, blocking collectives: 4.92 us -> 7.43 us  [local(): agg_top_both = lax.all_gather(agg_top, 'core', axis=1, tiled=True)]
    all_to_all x2, blocking collectives: 23.2 us -> 25.6 us  [everyone(): lax.all_to_all(jnp.broadcast_to(value[None], (count,) + value.shape), axe...]
  transfers between devices with their start and end apart: 19 -> 20, of which waited for: 12 -> 13; matrix products, arithmetic and copies ran while one was open for 5% -> 3% of each run, Pallas kernels for 0% -> 0%
where the time goes in v8:
time: 225 us; the launch traced here: 224 us
  blocking collectives  91.3 us (41%)
  starting transfers between devices  68.6 us (30%)
  waiting for transfers between devices  36.6 us (16%)
  Pallas kernels  13.2 us (6%)
  local copies, waits for them, and re-layouts  6.62 us (3%)
  other arithmetic  3.92 us (2%)
  matrix products  2.72 us (1%)
    ppermute x14, starting transfers between devices, swap(): return lax.ppermute(value, ('y', 'core'), y_pairs(which))  39.1 us
    all_to_all x2, blocking collectives, everyone(): lax.all_to_all(jnp.broadcast_to(value[None], (count,) + value.shape), axe...  25.6 us
    ppermute x14, waiting for transfers between devices, swap(): return lax.ppermute(value, ('y', 'core'), y_pairs(which))  25.1 us
    all_to_all x1, blocking collectives, local(): parts = lax.all_to_all(sent, COLS, 0, 0, tiled=True)  16.7 us
    all_to_all x3, starting transfers between devices, everyone(): lax.all_to_all(jnp.broadcast_to(value[None], (count,) + value.shape), axe...  14.4 us
    pallas_call x2, Pallas kernels, spmm(): pl.pallas_call(spmm_kernel, out_shape=jax.ShapeDtypeStruct((NCOL, CORE, b...  13.2 us
    all_gather x1, blocking collectives, local(): own_nodes = lax.all_gather(agg_mid, 'core', axis=1, tiled=True)  12.4 us
    all_gather x1, blocking collectives, local(): whole = lax.all_gather(over_x * norm_scale, 'core', axis=3, tiled=True)  11.9 us
  transfers between devices with their start and end apart: 20, of which 13 were waited for; matrix products, arithmetic and copies ran while one was open for 3% of the time, Pallas kernels for 0%

profile of v8, /device:TPU:1, one launch (start us, length us, event | category | flops | bytes accessed | tf_op | source)
XLA Modules:
  0.0 224.2 jit_solution(6219368622530676791)
XLA Ops:
  1.7 8.4 %all_gather.18 = bf16[256,256]{1,0:T(8,128)(2,1)S(1)} all-gather(bf16[128,256]{1,0:T(8,128)(2,1)S(1)} %compare_select_fusion), channel_id=1, replica_groups=mesh['y'=8,'zl'=4,'core'=2,'x'=4,'zh'=2] {'core'}, dimensions={0}, use_global_device_ids=true | all-gather | bytes 196608 | tf_op jit(solution)/shard_map/pair_inputs/all_gather | solution.py:166
  10.1 10.7 %all_to_all.35 = bf16[4,256,128]{2,1,0:T(8,128)(2,1)S(1)} all-to-all(bf16[4,256,128]{2,1,0:T(8,128)(2,1)S(1)} %broadcast_in_dim.15), channel_id=1, replica_groups=mesh['y'=8,'zl'=4,'core'=2,'x'=4,'zh'=2] {'zl'}, dimensions={0} | all-to-all | bytes 524288 | tf_op jit(solution)/shard_map/section_top/all_to_all | solution.py:18
  20.8 3.4 %collective-permute-start.5 = (bf16[8,12,128,128]{3,2,1,0:T(8,128)(2,1)}, bf16[8,12,128,128]{3,2,1,0:T(8,128)(2,1)S(1)}, u32[]{:S(2)}, u32[]{:S(2)}) collective-permute-start(bf16[8,12,128,128]{3,2,1,0:T(8,128)(2,1)} %bitcast.58), channel_id=1, source_target_pairs={{0,8},{8,0},{1,9},{9,1},{2,10},{10,2},{3,11},{11,3},{4,12},{12,4},... | collective-permute-start | bytes 9437192 | tf_op jit(solution)/shard_map/section_top/ppermute | solution.py:178
  24.3 4.1 %collective-permute-start = (bf16[8,128,128]{2,1,0:T(8,128)(2,1)S(1)}, bf16[8,128,128]{2,1,0:T(8,128)(2,1)}, u32[]{:S(2)}, u32[]{:S(2)}) collective-permute-start(bf16[8,128,128]{2,1,0:T(8,128)(2,1)S(1)} %bitcast.70), channel_id=1, source_target_pairs={{0,64},{8,456},{64,0},{72,136},{128,192},{136,72},{192,128},{200,2... | collective-permute-start | bytes 786440 | tf_op jit(solution)/shard_map/section_top/ppermute | solution.py:48
  34.9 4.5 %all_gather.19 = s32[16,16]{1,0:T(8,128)S(1)} all-gather(s32[8,16]{1,0:T(8,128)S(1)} %add_add_fusion), channel_id=1, replica_groups=mesh['y'=8,'zl'=4,'core'=2,'x'=4,'zh'=2] {'core'}, dimensions={0}, use_global_device_ids=true | all-gather | bytes 1536 | tf_op jit(solution)/shard_map/all_gather | solution.py:161
  42.0 4.6 %collective-permute-start.4 = (bf16[8,128,128]{2,1,0:T(8,128)(2,1)}, bf16[8,128,128]{2,1,0:T(8,128)(2,1)}, u32[]{:S(2)}, u32[]{:S(2)}) collective-permute-start(bf16[8,128,128]{2,1,0:T(8,128)(2,1)} %collective-permute-done.1.refs_3_), channel_id=1, source_target_pairs={{0,64},{8,456},{64,0},{72,136},{128,192},{136,72},{192,128},{200,2... | collective-permute-start | bytes 786440 | tf_op jit(solution)/shard_map/section_top/ppermute | solution.py:48
  59.2 6.6 %section_top.1 = bf16[8,2,128,128]{3,2,1,0:T(8,128)(2,1)} custom-call(s32[256]{0:T(256)} %reshape.69.meta_ref, s32[128]{0:T(128)} %constant.34.clone.table_ref, s32[2]{0:T(128)} %pad_add_fusion.place_ref, bf16[8,128,128]{2,1,0:T(8,128)(2,1)} %bitcast.72, bf16[8,128,128]{2,1,0:T(8,128)(2,1)} %collective-permute-done.refs_1_, ...), custom_call_target="tpu_custom_call" | custom-call | tf_op jit(solution)/shard_map/section_top/pallas_call | solution.py:121
  65.8 9.8 %all-to-all-start.1 = ((bf16[8,256,128]{2,1,0:T(8,128)(2,1)}), bf16[8,256,128]{2,1,0:T(8,128)(2,1)S(1)}, u32[]{:S(2)}, u32[]{:S(2)}) async-start(bf16[8,256,128]{2,1,0:T(8,128)(2,1)} %bitcast.65), calls=%async_computation.1 | async-start | bytes 1048576 | tf_op jit(solution)/shard_map/section_top/all_to_all | solution.py:181
  77.4 4.4 %all_gather.20 = bf16[3,256,256]{2,1,0:T(8,128)(2,1)S(1)} all-gather(bf16[3,128,256]{2,1,0:T(8,128)(2,1)S(1)} %pad_maximum_fusion.2), channel_id=1, replica_groups=mesh['y'=8,'zl'=4,'core'=2,'x'=4,'zh'=2] {'core'}, dimensions={1}, use_global_device_ids=true | all-gather | bytes 589824 | tf_op jit(solution)/shard_map/pair_inputs/all_gather | solution.py:167
  81.9 5.3 %all-to-all-done.1 = bf16[8,256,128]{2,1,0:T(8,128)(2,1)S(1)} async-done(((bf16[8,256,128]{2,1,0:T(8,128)(2,1)}), bf16[8,256,128]{2,1,0:T(8,128)(2,1)S(1)}, u32[]{:S(2)}, u32[]{:S(2)}) %all-to-all-start.1) | async-done | bytes 524320 | tf_op jit(solution)/shard_map/section_top/all_to_all | solution.py:181
  87.3 7.4 %all_gather.21 = bf16[256,256]{1,0:T(8,128)(2,1)S(1)} all-gather(bf16[256,128]{1,0:T(8,128)(2,1)S(1)} %reduce_sum.42), channel_id=1, replica_groups=mesh['y'=8,'zl'=4,'core'=2,'x'=4,'zh'=2] {'core'}, dimensions={1}, use_global_device_ids=true | all-gather | bytes 196608 | tf_op jit(solution)/shard_map/section_top/all_gather | solution.py:185
  95.6 4.3 %all-to-all-start.2 = ((bf16[4,256,128]{2,1,0:T(8,128)(2,1)}), bf16[4,256,128]{2,1,0:T(8,128)(2,1)S(1)}, u32[]{:S(2)}, u32[]{:S(2)}) async-start(bf16[4,256,128]{2,1,0:T(8,128)(2,1)} %broadcast_in_dim.17), calls=%async_computation.2 | async-start | bytes 524288 | tf_op jit(solution)/shard_map/section_mid/all_to_all | solution.py:18
  101.9 5.5 %all-to-all-done.2 = bf16[4,256,128]{2,1,0:T(8,128)(2,1)S(1)} async-done(((bf16[4,256,128]{2,1,0:T(8,128)(2,1)}), bf16[4,256,128]{2,1,0:T(8,128)(2,1)S(1)}, u32[]{:S(2)}, u32[]{:S(2)}) %all-to-all-start.2) | async-done | bytes 262176 | tf_op jit(solution)/shard_map/section_mid/all_to_all | solution.py:18
  107.4 3.7 %collective-permute-start.8 = (bf16[8,128,128]{2,1,0:T(8,128)(2,1)S(1)}, bf16[8,128,128]{2,1,0:T(8,128)(2,1)S(1)}, u32[]{:S(2)}, u32[]{:S(2)}) collective-permute-start(bf16[8,128,128]{2,1,0:T(8,128)(2,1)S(1)} %bitcast.67), channel_id=1, source_target_pairs={{0,64},{8,456},{64,0},{72,136},{128,192},{136,72},{192,128},{200,2... | collective-permute-start | bytes 786440 | tf_op jit(solution)/shard_map/section_mid/ppermute | solution.py:48
  113.5 3.5 %all-to-all-start.3 = ((bf16[4,2,256,256]{2,1,3,0:T(2,128)(2,1)}), bf16[4,2,256,256]{2,1,3,0:T(2,128)(2,1)S(1)}, u32[]{:S(2)}, u32[]{:S(2)}) async-start(bf16[4,2,256,256]{2,1,3,0:T(2,128)(2,1)} %broadcast_in_dim.18), calls=%async_computation.3 | async-start | bytes 2097152 | tf_op jit(solution)/shard_map/section_mid/all_to_all | solution.py:18
  125.8 3.8 %collective-permute-start.11 = (bf16[8,128,128]{2,1,0:T(8,128)(2,1)S(1)}, bf16[8,128,128]{2,1,0:T(8,128)(2,1)}, u32[]{:S(2)}, u32[]{:S(2)}) collective-permute-start(bf16[8,128,128]{2,1,0:T(8,128)(2,1)S(1)} %collective-permute-done.9.refs_2_), channel_id=1, source_target_pairs={{0,64},{8,456},{64,0},{72,136},{128,192},{136,72},{192,128},{200,2... | collective-permute-start | bytes 786440 | tf_op jit(solution)/shard_map/section_mid/ppermute | solution.py:48
  132.7 4.6 %collective-permute-done.11.refs_4_ = bf16[8,128,128]{2,1,0:T(8,128)(2,1)} collective-permute-done((bf16[8,128,128]{2,1,0:T(8,128)(2,1)S(1)}, bf16[8,128,128]{2,1,0:T(8,128)(2,1)}, u32[]{:S(2)}, u32[]{:S(2)}) %collective-permute-start.11) | collective-permute-done | bytes 262176 | tf_op jit(solution)/shard_map/section_mid/ppermute | solution.py:48
  145.2 5.4 %collective-permute-done.14.refs_7_ = bf16[8,128,128]{2,1,0:T(8,128)(2,1)} collective-permute-done((bf16[8,128,128]{2,1,0:T(8,128)(2,1)}, bf16[8,128,128]{2,1,0:T(8,128)(2,1)}, u32[]{:S(2)}, u32[]{:S(2)}) %collective-permute-start.14) | collective-permute-done | bytes 262176 | tf_op jit(solution)/shard_map/section_mid/ppermute | solution.py:48
  150.6 6.6 %section_mid.1 = bf16[8,2,128,128]{3,2,1,0:T(8,128)(2,1)} custom-call(s32[256]{0:T(256)} %reshape.69.meta_ref, s32[128]{0:T(128)} %constant.34.clone.table_ref, s32[2]{0:T(128)} %pad_add_fusion.place_ref, bf16[8,128,128]{2,1,0:T(8,128)(2,1)} %bitcast.69, bf16[8,128,128]{2,1,0:T(8,128)(2,1)} %copy-done.5, bf16[8,128,128]{2,1,0:T(8,128)(2,1)} %copy-done.6, ...), custom_call_target="tpu_custom_call" | custom-call | tf_op jit(solution)/shard_map/section_mid/pallas_call | solution.py:121
  158.9 16.7 %all_to_all.36 = bf16[8,320,128]{2,1,0:T(8,128)(2,1)S(1)} all-to-all(bf16[8,320,128]{2,1,0:T(8,128)(2,1)S(1)} %pad_maximum_fusion), channel_id=1, replica_groups=mesh['y'=8,'zl'=4,'core'=2,'x'=4,'zh'=2] {'x','zh'}, dimensions={0} | all-to-all | bytes 1310720 | tf_op jit(solution)/shard_map/section_mid/all_to_all | solution.py:204
  175.7 14.9 %all_to_all.37 = bf16[8,64,128]{2,1,0:T(8,128)(2,1)S(1)} all-to-all(bf16[8,64,128]{2,1,0:T(8,128)(2,1)S(1)} %broadcast_in_dim.19), channel_id=1, replica_groups=mesh['y'=8,'zl'=4,'core'=2,'x'=4,'zh'=2] {'y'}, dimensions={0} | all-to-all | bytes 262144 | tf_op jit(solution)/shard_map/weight_sums/all_to_all | solution.py:18
  191.5 6.6 %all-to-all-start.6 = ((bf16[32,64,128]{2,1,0:T(8,128)(2,1)}), bf16[32,64,128]{2,1,0:T(8,128)(2,1)S(1)}, u32[]{:S(2)}, u32[]{:S(2)}) async-start(bf16[32,64,128]{2,1,0:T(8,128)(2,1)} %broadcast_in_dim.20), calls=%async_computation.6 | async-start | bytes 1048576 | tf_op jit(solution)/shard_map/weight_sums/all_to_all | solution.py:18
  198.1 12.4 %all_gather.22 = bf16[256,256]{1,0:T(8,128)(2,1)S(1)} all-gather(bf16[256,128]{1,0:T(8,128)(2,1)S(1)} %slice.35), channel_id=1, replica_groups=mesh['y'=8,'zl'=4,'core'=2,'x'=4,'zh'=2] {'core'}, dimensions={1}, use_global_device_ids=true | all-gather | bytes 196608 | tf_op jit(solution)/shard_map/section_mid/all_gather | solution.py:207
  211.4 11.9 %all_gather.23 = f32[8,2,32,256]{3,2,1,0:T(8,128)S(1)} all-gather(f32[8,2,32,128]{3,2,1,0:T(8,128)S(1)} %bitcast.73), channel_id=1, replica_groups=mesh['y'=8,'zl'=4,'core'=2,'x'=4,'zh'=2] {'core'}, dimensions={3}, use_global_device_ids=true | all-gather | bytes 786432 | tf_op jit(solution)/shard_map/weight_sums/all_gather | solution.py:217
  (86 shorter events, 53.9 us)
Async XLA Ops:
  0.6 94.1 %copy-start = (bf16[256,256]{1,0:T(8,128)(2,1)S(1)}, bf16[256,256]{1,0:T(8,128)(2,1)}, u32[]{:S(2)}) copy-start(bf16[256,256]{1,0:T(8,128)(2,1)} %param.18) | copy-start | bytes 393220
  0.7 34.1 %copy-start.9 = (s32[8,1,12]{2,1,0:T(1,128)S(1)}, s32[8,1,12]{2,1,0:T(1,128)}, u32[]{:S(2)}) copy-start(s32[8,1,12]{2,1,0:T(1,128)} %param.20) | copy-start | bytes 1156
  20.8 38.4 %copy-start.4 = (bf16[4,256,128]{2,1,0:T(8,128)(2,1)}, bf16[4,256,128]{2,1,0:T(8,128)(2,1)S(1)}, u32[]{:S(2)}) copy-start(bf16[4,256,128]{2,1,0:T(8,128)(2,1)S(1)} %all_to_all.35) | copy-start | bytes 786436
  20.8 30.7 %collective-permute-start.5 = (bf16[8,12,128,128]{3,2,1,0:T(8,128)(2,1)}, bf16[8,12,128,128]{3,2,1,0:T(8,128)(2,1)S(1)}, u32[]{:S(2)}, u32[]{:S(2)}) collective-permute-start(bf16[8,12,128,128]{3,2,1,0:T(8,128)(2,1)} %bitcast.58), channel_id=1, source_target_pairs={{0,8},{8,0},{1,9},{9,1},{2,10},{10,2},{3,11},{11,3},{4,12},{12,4},... | collective-permute-start | bytes 9437192 | tf_op jit(solution)/shard_map/section_top/ppermute | solution.py:178
  24.3 8.4 %collective-permute-start = (bf16[8,128,128]{2,1,0:T(8,128)(2,1)S(1)}, bf16[8,128,128]{2,1,0:T(8,128)(2,1)}, u32[]{:S(2)}, u32[]{:S(2)}) collective-permute-start(bf16[8,128,128]{2,1,0:T(8,128)(2,1)S(1)} %bitcast.70), channel_id=1, source_target_pairs={{0,64},{8,456},{64,0},{72,136},{128,192},{136,72},{192,128},{200,2... | collective-permute-start | bytes 786440 | tf_op jit(solution)/shard_map/section_top/ppermute | solution.py:48
  28.4 11.6 %collective-permute-start.2 = (bf16[8,128,128]{2,1,0:T(8,128)(2,1)S(1)}, bf16[8,128,128]{2,1,0:T(8,128)(2,1)}, u32[]{:S(2)}, u32[]{:S(2)}) collective-permute-start(bf16[8,128,128]{2,1,0:T(8,128)(2,1)S(1)} %bitcast.71), channel_id=1, source_target_pairs={{0,448},{8,72},{64,128},{72,8},{128,64},{136,200},{192,256},{200,1... | collective-permute-start | bytes 786440 | tf_op jit(solution)/shard_map/section_top/ppermute | solution.py:48
  32.7 9.3 %collective-permute-start.1 = (bf16[8,128,128]{2,1,0:T(8,128)(2,1)}, bf16[8,128,128]{2,1,0:T(8,128)(2,1)}, u32[]{:S(2)}, u32[]{:S(2)}) collective-permute-start(bf16[8,128,128]{2,1,0:T(8,128)(2,1)} %collective-permute-done.refs_1_), channel_id=1, source_target_pairs={{0,448},{8,72},{64,128},{72,8},{128,64},{136,200},{192,256},{200,1... | collective-permute-start | bytes 786440 | tf_op jit(solution)/shard_map/section_top/ppermute | solution.py:48
  40.0 8.6 %collective-permute-start.3 = (bf16[8,128,128]{2,1,0:T(8,128)(2,1)}, bf16[8,128,128]{2,1,0:T(8,128)(2,1)}, u32[]{:S(2)}, u32[]{:S(2)}) collective-permute-start(bf16[8,128,128]{2,1,0:T(8,128)(2,1)} %collective-permute-done.2.refs_2_), channel_id=1, source_target_pairs={{0,64},{8,456},{64,0},{72,136},{128,192},{136,72},{192,128},{200,2... | collective-permute-start | bytes 786440 | tf_op jit(solution)/shard_map/section_top/ppermute | solution.py:48
  42.0 9.5 %collective-permute-start.4 = (bf16[8,128,128]{2,1,0:T(8,128)(2,1)}, bf16[8,128,128]{2,1,0:T(8,128)(2,1)}, u32[]{:S(2)}, u32[]{:S(2)}) collective-permute-start(bf16[8,128,128]{2,1,0:T(8,128)(2,1)} %collective-permute-done.1.refs_3_), channel_id=1, source_target_pairs={{0,64},{8,456},{64,0},{72,136},{128,192},{136,72},{192,128},{200,2... | collective-permute-start | bytes 786440 | tf_op jit(solution)/shard_map/section_top/ppermute | solution.py:48
  48.7 7.7 %collective-permute-start.6 = (bf16[8,128,128]{2,1,0:T(8,128)(2,1)}, bf16[8,128,128]{2,1,0:T(8,128)(2,1)}, u32[]{:S(2)}, u32[]{:S(2)}) collective-permute-start(bf16[8,128,128]{2,1,0:T(8,128)(2,1)} %collective-permute-done.3.refs_4_), channel_id=1, source_target_pairs={{0,448},{8,72},{64,128},{72,8},{128,64},{136,200},{192,256},{200,1... | collective-permute-start | bytes 786440 | tf_op jit(solution)/shard_map/section_top/ppermute | solution.py:48
  51.5 7.7 %collective-permute-start.7 = (bf16[8,128,128]{2,1,0:T(8,128)(2,1)}, bf16[8,128,128]{2,1,0:T(8,128)(2,1)}, u32[]{:S(2)}, u32[]{:S(2)}) collective-permute-start(bf16[8,128,128]{2,1,0:T(8,128)(2,1)} %collective-permute-done.4.refs_5_), channel_id=1, source_target_pairs={{0,448},{8,72},{64,128},{72,8},{128,64},{136,200},{192,256},{200,1... | collective-permute-start | bytes 786440 | tf_op jit(solution)/shard_map/section_top/ppermute | solution.py:48
  65.8 21.4 %all-to-all-start.1 = ((bf16[8,256,128]{2,1,0:T(8,128)(2,1)}), bf16[8,256,128]{2,1,0:T(8,128)(2,1)S(1)}, u32[]{:S(2)}, u32[]{:S(2)}) async-start(bf16[8,256,128]{2,1,0:T(8,128)(2,1)} %bitcast.65), calls=%async_computation.1 | async-start | bytes 1048576 | tf_op jit(solution)/shard_map/section_top/all_to_all | solution.py:181
  95.6 11.7 %all-to-all-start.2 = ((bf16[4,256,128]{2,1,0:T(8,128)(2,1)}), bf16[4,256,128]{2,1,0:T(8,128)(2,1)S(1)}, u32[]{:S(2)}, u32[]{:S(2)}) async-start(bf16[4,256,128]{2,1,0:T(8,128)(2,1)} %broadcast_in_dim.17), calls=%async_computation.2 | async-start | bytes 524288 | tf_op jit(solution)/shard_map/section_mid/all_to_all | solution.py:18
  100.0 11.8 %collective-permute-start.15 = (bf16[256,256]{1,0:T(8,128)(2,1)S(1)}, bf16[256,256]{1,0:T(8,128)(2,1)S(1)}, u32[]{:S(2)}, u32[]{:S(2)}) collective-permute-start(bf16[256,256]{1,0:T(8,128)(2,1)S(1)} %get-tuple-element.21), channel_id=1, source_target_pairs={{0,1},{1,0},{2,3},{3,2},{4,5},{5,4},{6,7},{7,6},{8,9},{9,8},{10,11... | collective-permute-start | bytes 393224 | tf_op jit(solution)/shard_map/section_mid/ppermute | solution.py:192
  107.4 12.1 %collective-permute-start.8 = (bf16[8,128,128]{2,1,0:T(8,128)(2,1)S(1)}, bf16[8,128,128]{2,1,0:T(8,128)(2,1)S(1)}, u32[]{:S(2)}, u32[]{:S(2)}) collective-permute-start(bf16[8,128,128]{2,1,0:T(8,128)(2,1)S(1)} %bitcast.67), channel_id=1, source_target_pairs={{0,64},{8,456},{64,0},{72,136},{128,192},{136,72},{192,128},{200,2... | collective-permute-start | bytes 786440 | tf_op jit(solution)/shard_map/section_mid/ppermute | solution.py:48
  113.5 29.9 %all-to-all-start.3 = ((bf16[4,2,256,256]{2,1,3,0:T(2,128)(2,1)}), bf16[4,2,256,256]{2,1,3,0:T(2,128)(2,1)S(1)}, u32[]{:S(2)}, u32[]{:S(2)}) async-start(bf16[4,2,256,256]{2,1,3,0:T(2,128)(2,1)} %broadcast_in_dim.18), calls=%async_computation.3 | async-start | bytes 2097152 | tf_op jit(solution)/shard_map/section_mid/all_to_all | solution.py:18
  117.0 8.8 %collective-permute-start.9 = (bf16[8,128,128]{2,1,0:T(8,128)(2,1)S(1)}, bf16[8,128,128]{2,1,0:T(8,128)(2,1)S(1)}, u32[]{:S(2)}, u32[]{:S(2)}) collective-permute-start(bf16[8,128,128]{2,1,0:T(8,128)(2,1)S(1)} %bitcast.68), channel_id=1, source_target_pairs={{0,448},{8,72},{64,128},{72,8},{128,64},{136,200},{192,256},{200,1... | collective-permute-start | bytes 786440 | tf_op jit(solution)/shard_map/section_mid/ppermute | solution.py:48
  119.5 10.0 %collective-permute-start.10 = (bf16[8,128,128]{2,1,0:T(8,128)(2,1)S(1)}, bf16[8,128,128]{2,1,0:T(8,128)(2,1)S(1)}, u32[]{:S(2)}, u32[]{:S(2)}) collective-permute-start(bf16[8,128,128]{2,1,0:T(8,128)(2,1)S(1)} %collective-permute-done.8.refs_1_), channel_id=1, source_target_pairs={{0,448},{8,72},{64,128},{72,8},{128,64},{136,200},{192,256},{200,1... | collective-permute-start | bytes 786440 | tf_op jit(solution)/shard_map/section_mid/ppermute | solution.py:48
  125.8 11.5 %collective-permute-start.11 = (bf16[8,128,128]{2,1,0:T(8,128)(2,1)S(1)}, bf16[8,128,128]{2,1,0:T(8,128)(2,1)}, u32[]{:S(2)}, u32[]{:S(2)}) collective-permute-start(bf16[8,128,128]{2,1,0:T(8,128)(2,1)S(1)} %collective-permute-done.9.refs_2_), channel_id=1, source_target_pairs={{0,64},{8,456},{64,0},{72,136},{128,192},{136,72},{192,128},{200,2... | collective-permute-start | bytes 786440 | tf_op jit(solution)/shard_map/section_mid/ppermute | solution.py:48
  129.6 11.2 %collective-permute-start.12 = (bf16[8,128,128]{2,1,0:T(8,128)(2,1)S(1)}, bf16[8,128,128]{2,1,0:T(8,128)(2,1)}, u32[]{:S(2)}, u32[]{:S(2)}) collective-permute-start(bf16[8,128,128]{2,1,0:T(8,128)(2,1)S(1)} %collective-permute-done.10.refs_3_), channel_id=1, source_target_pairs={{0,64},{8,456},{64,0},{72,136},{128,192},{136,72},{192,128},{200,2... | collective-permute-start | bytes 786440 | tf_op jit(solution)/shard_map/section_mid/ppermute | solution.py:48
  137.2 8.0 %collective-permute-start.13 = (bf16[8,128,128]{2,1,0:T(8,128)(2,1)}, bf16[8,128,128]{2,1,0:T(8,128)(2,1)}, u32[]{:S(2)}, u32[]{:S(2)}) collective-permute-start(bf16[8,128,128]{2,1,0:T(8,128)(2,1)} %collective-permute-done.11.refs_4_), channel_id=1, source_target_pairs={{0,448},{8,72},{64,128},{72,8},{128,64},{136,200},{192,256},{200,1... | collective-permute-start | bytes 786440 | tf_op jit(solution)/shard_map/section_mid/ppermute | solution.py:48
  140.8 9.8 %collective-permute-start.14 = (bf16[8,128,128]{2,1,0:T(8,128)(2,1)}, bf16[8,128,128]{2,1,0:T(8,128)(2,1)}, u32[]{:S(2)}, u32[]{:S(2)}) collective-permute-start(bf16[8,128,128]{2,1,0:T(8,128)(2,1)} %collective-permute-done.12.refs_5_), channel_id=1, source_target_pairs={{0,448},{8,72},{64,128},{72,8},{128,64},{136,200},{192,256},{200,1... | collective-permute-start | bytes 786440 | tf_op jit(solution)/shard_map/section_mid/ppermute | solution.py:48
  175.6 34.9 %copy-start.8 = (bf16[256,256]{1,0:T(8,128)(2,1)S(1)}, bf16[256,256]{1,0:T(8,128)(2,1)}, u32[]{:S(2)}) copy-start(bf16[256,256]{1,0:T(8,128)(2,1)} %param.17) | copy-start | bytes 393220
  191.5 19.8 %all-to-all-start.6 = ((bf16[32,64,128]{2,1,0:T(8,128)(2,1)}), bf16[32,64,128]{2,1,0:T(8,128)(2,1)S(1)}, u32[]{:S(2)}, u32[]{:S(2)}) async-start(bf16[32,64,128]{2,1,0:T(8,128)(2,1)} %broadcast_in_dim.20), calls=%async_computation.6 | async-start | bytes 1048576 | tf_op jit(solution)/shard_map/weight_sums/all_to_all | solution.py:18
  (7 other events, 112.5 us)

commit v9 on v8

--- a/solution.py
+++ b/solution.py
@@ -165,7 +165,7 @@
         grad_top = jnp.where(mask_top > 0, grad_out, jnp.zeros_like(grad_out))
         unit_top = my_half(lax.all_gather(grad_top, "core", axis=0, tiled=True))
         pair = lax.all_gather(
-            jnp.stack([mask_mid.astype(BF16), feats_mid, feats_in]), "core", axis=1, tiled=True
+            jnp.stack([mask_mid.astype(BF16), feats_mid]), "core", axis=1, tiled=True
         )
         mask_pair = my_half(pair[0])
         feats_mid_pair = pair[1]
@@ -174,9 +174,11 @@
 
     with jax.named_scope("section_top"):
         units = gather_z(unit_top)
-        adj, units = lax.optimization_barrier((adj, units))
+        mine = lax.all_gather(feats_in, "core", axis=0, tiled=True)
+        adj, mine, units = lax.optimization_barrier((adj, mine, units))
         other_adj = lax.ppermute(adj, "core", [(0, 1), (1, 0)])
-        pieces, meta, other_adj = gather_y(units, meta, other_adj)
+        other = lax.ppermute(mine, "zh", [(0, 1), (1, 0)])
+        pieces, meta, (other_adj, other) = gather_y(units, meta, (other_adj, other))
         partial_top = spmm(meta, place, pieces, adj, other_adj)
         parts = lax.all_to_all(
             partial_top.reshape(NCOL, CORE * bs, half), COLS, 0, 0, tiled=True
@@ -188,12 +190,11 @@
         hidden = times_transpose(agg_top_both, weight_half)
         grad_mid = jnp.where(mask_pair > 0, hidden, jnp.zeros_like(hidden)).astype(BF16)
     with jax.named_scope("section_mid"):
-        mine = pair[2]
-        other = lax.ppermute(mine, "zh", [(0, 1), (1, 0)])
-        units = gather_z(grad_mid)
         first_zh = lax.axis_index("zh") == 0
         both = jnp.stack([jnp.where(first_zh, mine, other), jnp.where(first_zh, other, mine)])
-        feats_in_group = everyone(both, "x", X).reshape(-1, feats)
+        both = jnp.broadcast_to(both[None], (X,) + both.shape)
+        units, both = lax.optimization_barrier((gather_z(grad_mid), both))
+        feats_in_group = lax.all_to_all(both, "x", 0, 0, tiled=True).reshape(-1, feats)
         partial_mid = spmm(meta, place, gather_y(units)[0], adj, other_adj)
         term_first = contract_rows(feats_in_group, partial_mid.reshape(-1, half))
         terms = jnp.stack([term_first, term_second]).astype(BF16)

time: 225 us -> 226 us (level)
  blocking collectives: 91.3 us -> 75 us
  starting transfers between devices: 68.6 us -> 78.7 us
  waiting for transfers between devices: 36.6 us -> 42 us
    all_to_all x2 -> x1, blocking collectives: 25.6 us -> 14.6 us  [everyone(): lax.all_to_all(jnp.broadcast_to(value[None], (count,) + value.shape), axe...]
    all_to_all x3, waiting for transfers between devices: 5.5 us -> 13.7 us  [everyone(): lax.all_to_all(jnp.broadcast_to(value[None], (count,) + value.shape), axe...]
    ppermute x1, starting transfers between devices: 1.91 us -> 8.48 us  [local(): other = lax.ppermute(mine, 'zh', [(0, 1), (1, 0)])]
    ppermute x14, waiting for transfers between devices: 25.1 us -> 18.6 us  [swap(): return lax.ppermute(value, ('y', 'core'), y_pairs(which))]
    ppermute x1, waiting for transfers between devices: 0.66 us -> 4.55 us  [local(): other = lax.ppermute(mine, 'zh', [(0, 1), (1, 0)])]
    all_to_all x0 -> x1, starting transfers between devices: none -> 3.53 us  [local(): lax.all_to_all(both, 'x', 0, 0, tiled=True).reshape(-1, feats)]
    all_gather x1, blocking collectives: 12.4 us -> 9.37 us  [local(): own_nodes = lax.all_gather(agg_mid, 'core', axis=1, tiled=True)]
    all_to_all x1, starting transfers between devices: 9.77 us -> 7.21 us  [local(): lax.all_to_all(partial_top.reshape(NCOL, CORE * bs, half), COLS, 0, 0, ti...]
  transfers between devices with their start and end apart: 20 -> 21, of which waited for: 13 -> 11; matrix products, arithmetic and copies ran while one was open for 3% -> 3% of each run, Pallas kernels for 0% -> 0%
where the time goes in v9:
time: 226 us; the launch traced here: 225 us
  starting transfers between devices  78.7 us (35%)
  blocking collectives  75 us (33%)
  waiting for transfers between devices  42 us (19%)
  Pallas kernels  13.3 us (6%)
  local copies, waits for them, and re-layouts  8 us (4%)
  other arithmetic  3.87 us (2%)
  matrix products  2.72 us (1%)
    ppermute x14, starting transfers between devices, swap(): return lax.ppermute(value, ('y', 'core'), y_pairs(which))  38.7 us
    ppermute x14, waiting for transfers between devices, swap(): return lax.ppermute(value, ('y', 'core'), y_pairs(which))  18.6 us
    all_to_all x1, blocking collectives, local(): parts = lax.all_to_all(sent, COLS, 0, 0, tiled=True)  16.8 us
    all_to_all x3, starting transfers between devices, everyone(): lax.all_to_all(jnp.broadcast_to(value[None], (count,) + value.shape), axe...  16.4 us
    all_to_all x1, blocking collectives, everyone(): lax.all_to_all(jnp.broadcast_to(value[None], (count,) + value.shape), axe...  14.6 us
    all_to_all x3, waiting for transfers between devices, everyone(): lax.all_to_all(jnp.broadcast_to(value[None], (count,) + value.shape), axe...  13.7 us
    pallas_call x2, Pallas kernels, spmm(): pl.pallas_call(spmm_kernel, out_shape=jax.ShapeDtypeStruct((NCOL, CORE, b...  13.3 us
    all_gather x1, blocking collectives, local(): whole = lax.all_gather(over_x * norm_scale, 'core', axis=3, tiled=True)  10.8 us
  transfers between devices with their start and end apart: 21, of which 11 were waited for; matrix products, arithmetic and copies ran while one was open for 3% of the time, Pallas kernels for 0%

profile of v9, /device:TPU:1, one launch (start us, length us, event | category | flops | bytes accessed | tf_op | source)
XLA Modules:
  0.0 224.7 jit_solution(10636449031801384994)
XLA Ops:
  1.7 8.4 %all_gather.22 = bf16[256,256]{1,0:T(8,128)(2,1)S(1)} all-gather(bf16[128,256]{1,0:T(8,128)(2,1)S(1)} %compare_select_fusion), channel_id=1, replica_groups=mesh['y'=8,'zl'=4,'core'=2,'x'=4,'zh'=2] {'core'}, dimensions={0}, use_global_device_ids=true | all-gather | bytes 196608 | tf_op jit(solution)/shard_map/pair_inputs/all_gather | solution.py:166
  16.3 5.4 %all-to-all-done = bf16[4,256,128]{2,1,0:T(8,128)(2,1)S(1)} async-done(((bf16[4,256,128]{2,1,0:T(8,128)(2,1)}), bf16[4,256,128]{2,1,0:T(8,128)(2,1)S(1)}, u32[]{:S(2)}, u32[]{:S(2)}) %all-to-all-start) | async-done | bytes 262176 | tf_op jit(solution)/shard_map/section_top/all_to_all | solution.py:18
  21.7 4.3 %collective-permute-start.5 = (bf16[8,12,128,128]{3,2,1,0:T(8,128)(2,1)}, bf16[8,12,128,128]{3,2,1,0:T(8,128)(2,1)S(1)}, u32[]{:S(2)}, u32[]{:S(2)}) collective-permute-start(bf16[8,12,128,128]{3,2,1,0:T(8,128)(2,1)} %bitcast.51), channel_id=1, source_target_pairs={{0,8},{8,0},{1,9},{9,1},{2,10},{10,2},{3,11},{11,3},{4,12},{12,4},... | collective-permute-start | bytes 9437192 | tf_op jit(solution)/shard_map/section_top/ppermute | solution.py:179
  31.3 3.8 %collective-permute-done.refs_1_ = bf16[8,128,128]{2,1,0:T(8,128)(2,1)} collective-permute-done((bf16[8,128,128]{2,1,0:T(8,128)(2,1)S(1)}, bf16[8,128,128]{2,1,0:T(8,128)(2,1)}, u32[]{:S(2)}, u32[]{:S(2)}) %collective-permute-start) | collective-permute-done | bytes 262176 | tf_op jit(solution)/shard_map/section_top/ppermute | solution.py:48
  47.0 8.5 %collective-permute-start.6 = (bf16[256,256]{1,0:T(8,128)(2,1)}, bf16[256,256]{1,0:T(8,128)(2,1)S(1)}, u32[]{:S(2)}, u32[]{:S(2)}) collective-permute-start(bf16[256,256]{1,0:T(8,128)(2,1)} %all_gather.21), channel_id=1, source_target_pairs={{0,1},{1,0},{2,3},{3,2},{4,5},{5,4},{6,7},{7,6},{8,9},{9,8},{10,11... | collective-permute-start | bytes 393224 | tf_op jit(solution)/shard_map/section_top/ppermute | solution.py:180
  57.4 4.5 %collective-permute-done.6 = bf16[256,256]{1,0:T(8,128)(2,1)S(1)} collective-permute-done((bf16[256,256]{1,0:T(8,128)(2,1)}, bf16[256,256]{1,0:T(8,128)(2,1)S(1)}, u32[]{:S(2)}, u32[]{:S(2)}) %collective-permute-start.6) | collective-permute-done | bytes 131104 | tf_op jit(solution)/shard_map/section_top/ppermute | solution.py:180
  65.1 4.9 %collective-permute-done.8.refs_7_ = bf16[8,128,128]{2,1,0:T(8,128)(2,1)} collective-permute-done((bf16[8,128,128]{2,1,0:T(8,128)(2,1)}, bf16[8,128,128]{2,1,0:T(8,128)(2,1)}, u32[]{:S(2)}, u32[]{:S(2)}) %collective-permute-start.8) | collective-permute-done | bytes 262176 | tf_op jit(solution)/shard_map/section_top/ppermute | solution.py:48
  70.0 6.6 %section_top.1 = bf16[8,2,128,128]{3,2,1,0:T(8,128)(2,1)} custom-call(s32[256]{0:T(256)} %reshape.69.meta_ref, s32[128]{0:T(128)} %constant.34.clone.table_ref, s32[2]{0:T(128)} %pad_add_fusion.place_ref, bf16[8,128,128]{2,1,0:T(8,128)(2,1)} %bitcast.65, bf16[8,128,128]{2,1,0:T(8,128)(2,1)} %collective-permute-done.refs_1_, ...), custom_call_target="tpu_custom_call" | custom-call | tf_op jit(solution)/shard_map/section_top/pallas_call | solution.py:121
  76.7 7.2 %all-to-all-start.1 = ((bf16[8,256,128]{2,1,0:T(8,128)(2,1)}), bf16[8,256,128]{2,1,0:T(8,128)(2,1)S(1)}, u32[]{:S(2)}, u32[]{:S(2)}) async-start(bf16[8,256,128]{2,1,0:T(8,128)(2,1)} %bitcast.58), calls=%async_computation.1 | async-start | bytes 1048576 | tf_op jit(solution)/shard_map/section_top/all_to_all | solution.py:183
  85.7 4.6 %all_gather.24 = bf16[2,256,256]{2,1,0:T(8,128)(2,1)S(1)} all-gather(bf16[2,128,256]{2,1,0:T(8,128)(2,1)S(1)} %pad_maximum_fusion.2), channel_id=1, replica_groups=mesh['y'=8,'zl'=4,'core'=2,'x'=4,'zh'=2] {'core'}, dimensions={1}, use_global_device_ids=true | all-gather | bytes 393216 | tf_op jit(solution)/shard_map/pair_inputs/all_gather | solution.py:167
  90.3 5.2 %all-to-all-done.1 = bf16[8,256,128]{2,1,0:T(8,128)(2,1)S(1)} async-done(((bf16[8,256,128]{2,1,0:T(8,128)(2,1)}), bf16[8,256,128]{2,1,0:T(8,128)(2,1)S(1)}, u32[]{:S(2)}, u32[]{:S(2)}) %all-to-all-start.1) | async-done | bytes 524320 | tf_op jit(solution)/shard_map/section_top/all_to_all | solution.py:183
  95.5 5.8 %all_gather.25 = bf16[256,256]{1,0:T(8,128)(2,1)S(1)} all-gather(bf16[256,128]{1,0:T(8,128)(2,1)S(1)} %reduce_sum.42), channel_id=1, replica_groups=mesh['y'=8,'zl'=4,'core'=2,'x'=4,'zh'=2] {'core'}, dimensions={1}, use_global_device_ids=true | all-gather | bytes 196608 | tf_op jit(solution)/shard_map/section_top/all_gather | solution.py:187
  102.3 8.1 %all-to-all-start.2 = ((bf16[4,256,128]{2,1,0:T(8,128)(2,1)}), bf16[4,256,128]{2,1,0:T(8,128)(2,1)S(1)}, u32[]{:S(2)}, u32[]{:S(2)}) async-start(bf16[4,256,128]{2,1,0:T(8,128)(2,1)} %broadcast_in_dim.17), calls=%async_computation.2 | async-start | bytes 524288 | tf_op jit(solution)/shard_map/section_mid/all_to_all | solution.py:18
  110.7 7.2 %all-to-all-done.2 = bf16[4,256,128]{2,1,0:T(8,128)(2,1)S(1)} async-done(((bf16[4,256,128]{2,1,0:T(8,128)(2,1)}), bf16[4,256,128]{2,1,0:T(8,128)(2,1)S(1)}, u32[]{:S(2)}, u32[]{:S(2)}) %all-to-all-start.2) | async-done | bytes 262176 | tf_op jit(solution)/shard_map/section_mid/all_to_all | solution.py:18
  121.3 3.5 %all-to-all-start.3 = ((bf16[4,2,256,256]{2,1,3,0:T(2,128)(2,1)}), bf16[4,2,256,256]{2,1,3,0:T(2,128)(2,1)S(1)}, u32[]{:S(2)}, u32[]{:S(2)}) async-start(bf16[4,2,256,256]{2,1,3,0:T(2,128)(2,1)} %broadcast_in_dim.18), calls=%async_computation.3 | async-start | bytes 2097152 | tf_op jit(solution)/shard_map/section_mid/all_to_all | solution.py:197
  124.8 3.5 %collective-permute-start.10 = (bf16[8,128,128]{2,1,0:T(8,128)(2,1)S(1)}, bf16[8,128,128]{2,1,0:T(8,128)(2,1)S(1)}, u32[]{:S(2)}, u32[]{:S(2)}) collective-permute-start(bf16[8,128,128]{2,1,0:T(8,128)(2,1)S(1)} %bitcast.61), channel_id=1, source_target_pairs={{0,448},{8,72},{64,128},{72,8},{128,64},{136,200},{192,256},{200,1... | collective-permute-start | bytes 786440 | tf_op jit(solution)/shard_map/section_mid/ppermute | solution.py:48
  132.5 4.3 %collective-permute-start.12 = (bf16[8,128,128]{2,1,0:T(8,128)(2,1)S(1)}, bf16[8,128,128]{2,1,0:T(8,128)(2,1)}, u32[]{:S(2)}, u32[]{:S(2)}) collective-permute-start(bf16[8,128,128]{2,1,0:T(8,128)(2,1)S(1)} %collective-permute-done.10.refs_2_), channel_id=1, source_target_pairs={{0,64},{8,456},{64,0},{72,136},{128,192},{136,72},{192,128},{200,2... | collective-permute-start | bytes 786440 | tf_op jit(solution)/shard_map/section_mid/ppermute | solution.py:48
  141.8 4.2 %collective-permute-start.14 = (bf16[8,128,128]{2,1,0:T(8,128)(2,1)}, bf16[8,128,128]{2,1,0:T(8,128)(2,1)}, u32[]{:S(2)}, u32[]{:S(2)}) collective-permute-start(bf16[8,128,128]{2,1,0:T(8,128)(2,1)} %collective-permute-done.12.refs_4_), channel_id=1, source_target_pairs={{0,448},{8,72},{64,128},{72,8},{128,64},{136,200},{192,256},{200,1... | collective-permute-start | bytes 786440 | tf_op jit(solution)/shard_map/section_mid/ppermute | solution.py:48
  156.0 6.6 %section_mid.1 = bf16[8,2,128,128]{3,2,1,0:T(8,128)(2,1)} custom-call(s32[256]{0:T(256)} %reshape.69.meta_ref, s32[128]{0:T(128)} %constant.34.clone.table_ref, s32[2]{0:T(128)} %pad_add_fusion.place_ref, bf16[8,128,128]{2,1,0:T(8,128)(2,1)} %bitcast.62, bf16[8,128,128]{2,1,0:T(8,128)(2,1)} %copy-done.6, bf16[8,128,128]{2,1,0:T(8,128)(2,1)} %copy-done.7, ...), custom_call_target="tpu_custom_call" | custom-call | tf_op jit(solution)/shard_map/section_mid/pallas_call | solution.py:121
  164.2 16.8 %all_to_all.35 = bf16[8,320,128]{2,1,0:T(8,128)(2,1)S(1)} all-to-all(bf16[8,320,128]{2,1,0:T(8,128)(2,1)S(1)} %pad_maximum_fusion), channel_id=1, replica_groups=mesh['y'=8,'zl'=4,'core'=2,'x'=4,'zh'=2] {'x','zh'}, dimensions={0} | all-to-all | bytes 1310720 | tf_op jit(solution)/shard_map/section_mid/all_to_all | solution.py:205
  181.2 14.6 %all_to_all.36 = bf16[8,64,128]{2,1,0:T(8,128)(2,1)S(1)} all-to-all(bf16[8,64,128]{2,1,0:T(8,128)(2,1)S(1)} %broadcast_in_dim.19), channel_id=1, replica_groups=mesh['y'=8,'zl'=4,'core'=2,'x'=4,'zh'=2] {'y'}, dimensions={0} | all-to-all | bytes 262144 | tf_op jit(solution)/shard_map/weight_sums/all_to_all | solution.py:18
  196.7 4.9 %all-to-all-start.6 = ((bf16[32,64,128]{2,1,0:T(8,128)(2,1)}), bf16[32,64,128]{2,1,0:T(8,128)(2,1)S(1)}, u32[]{:S(2)}, u32[]{:S(2)}) async-start(bf16[32,64,128]{2,1,0:T(8,128)(2,1)} %broadcast_in_dim.20), calls=%async_computation.6 | async-start | bytes 1048576 | tf_op jit(solution)/shard_map/weight_sums/all_to_all | solution.py:18
  201.6 9.4 %all_gather.26 = bf16[256,256]{1,0:T(8,128)(2,1)S(1)} all-gather(bf16[256,128]{1,0:T(8,128)(2,1)S(1)} %slice.30), channel_id=1, replica_groups=mesh['y'=8,'zl'=4,'core'=2,'x'=4,'zh'=2] {'core'}, dimensions={1}, use_global_device_ids=true | all-gather | bytes 196608 | tf_op jit(solution)/shard_map/section_mid/all_gather | solution.py:208
  213.1 10.8 %all_gather.27 = f32[8,2,32,256]{3,2,1,0:T(8,128)S(1)} all-gather(f32[8,2,32,128]{3,2,1,0:T(8,128)S(1)} %bitcast.66), channel_id=1, replica_groups=mesh['y'=8,'zl'=4,'core'=2,'x'=4,'zh'=2] {'core'}, dimensions={3}, use_global_device_ids=true | all-gather | bytes 786432 | tf_op jit(solution)/shard_map/weight_sums/all_gather | solution.py:218
  (96 shorter events, 60.5 us)
Async XLA Ops:
  0.6 100.7 %copy-start = (bf16[256,256]{1,0:T(8,128)(2,1)S(1)}, bf16[256,256]{1,0:T(8,128)(2,1)}, u32[]{:S(2)}) copy-start(bf16[256,256]{1,0:T(8,128)(2,1)} %param.18) | copy-start | bytes 393220
  0.7 36.5 %copy-start.13 = (s32[8,1,12]{2,1,0:T(1,128)S(1)}, s32[8,1,12]{2,1,0:T(1,128)}, u32[]{:S(2)}) copy-start(s32[8,1,12]{2,1,0:T(1,128)} %param.20) | copy-start | bytes 1156
  10.9 10.8 %all-to-all-start = ((bf16[4,256,128]{2,1,0:T(8,128)(2,1)}), bf16[4,256,128]{2,1,0:T(8,128)(2,1)S(1)}, u32[]{:S(2)}, u32[]{:S(2)}) async-start(bf16[4,256,128]{2,1,0:T(8,128)(2,1)} %broadcast_in_dim.15), calls=%async_computation | async-start | bytes 524288 | tf_op jit(solution)/shard_map/section_top/all_to_all | solution.py:18
  21.7 48.3 %copy-start.4 = (bf16[4,256,128]{2,1,0:T(8,128)(2,1)}, bf16[4,256,128]{2,1,0:T(8,128)(2,1)S(1)}, u32[]{:S(2)}) copy-start(bf16[4,256,128]{2,1,0:T(8,128)(2,1)S(1)} %all-to-all-done) | copy-start | bytes 786436
  21.7 40.3 %collective-permute-start.5 = (bf16[8,12,128,128]{3,2,1,0:T(8,128)(2,1)}, bf16[8,12,128,128]{3,2,1,0:T(8,128)(2,1)S(1)}, u32[]{:S(2)}, u32[]{:S(2)}) collective-permute-start(bf16[8,12,128,128]{3,2,1,0:T(8,128)(2,1)} %bitcast.51), channel_id=1, source_target_pairs={{0,8},{8,0},{1,9},{9,1},{2,10},{10,2},{3,11},{11,3},{4,12},{12,4},... | collective-permute-start | bytes 9437192 | tf_op jit(solution)/shard_map/section_top/ppermute | solution.py:179
  26.0 9.1 %collective-permute-start = (bf16[8,128,128]{2,1,0:T(8,128)(2,1)S(1)}, bf16[8,128,128]{2,1,0:T(8,128)(2,1)}, u32[]{:S(2)}, u32[]{:S(2)}) collective-permute-start(bf16[8,128,128]{2,1,0:T(8,128)(2,1)S(1)} %bitcast.63), channel_id=1, source_target_pairs={{0,64},{8,456},{64,0},{72,136},{128,192},{136,72},{192,128},{200,2... | collective-permute-start | bytes 786440 | tf_op jit(solution)/shard_map/section_top/ppermute | solution.py:48
  29.4 11.1 %collective-permute-start.2 = (bf16[8,128,128]{2,1,0:T(8,128)(2,1)S(1)}, bf16[8,128,128]{2,1,0:T(8,128)(2,1)}, u32[]{:S(2)}, u32[]{:S(2)}) collective-permute-start(bf16[8,128,128]{2,1,0:T(8,128)(2,1)S(1)} %bitcast.64), channel_id=1, source_target_pairs={{0,448},{8,72},{64,128},{72,8},{128,64},{136,200},{192,256},{200,1... | collective-permute-start | bytes 786440 | tf_op jit(solution)/shard_map/section_top/ppermute | solution.py:48
  35.1 8.5 %collective-permute-start.1 = (bf16[8,128,128]{2,1,0:T(8,128)(2,1)}, bf16[8,128,128]{2,1,0:T(8,128)(2,1)}, u32[]{:S(2)}, u32[]{:S(2)}) collective-permute-start(bf16[8,128,128]{2,1,0:T(8,128)(2,1)} %collective-permute-done.refs_1_), channel_id=1, source_target_pairs={{0,448},{8,72},{64,128},{72,8},{128,64},{136,200},{192,256},{200,1... | collective-permute-start | bytes 786440 | tf_op jit(solution)/shard_map/section_top/ppermute | solution.py:48
  40.5 15.0 %collective-permute-start.3 = (bf16[8,128,128]{2,1,0:T(8,128)(2,1)}, bf16[8,128,128]{2,1,0:T(8,128)(2,1)}, u32[]{:S(2)}, u32[]{:S(2)}) collective-permute-start(bf16[8,128,128]{2,1,0:T(8,128)(2,1)} %collective-permute-done.2.refs_2_), channel_id=1, source_target_pairs={{0,64},{8,456},{64,0},{72,136},{128,192},{136,72},{192,128},{200,2... | collective-permute-start | bytes 786440 | tf_op jit(solution)/shard_map/section_top/ppermute | solution.py:48
  43.5 18.4 %collective-permute-start.4 = (bf16[8,128,128]{2,1,0:T(8,128)(2,1)}, bf16[8,128,128]{2,1,0:T(8,128)(2,1)}, u32[]{:S(2)}, u32[]{:S(2)}) collective-permute-start(bf16[8,128,128]{2,1,0:T(8,128)(2,1)} %collective-permute-done.1.refs_3_), channel_id=1, source_target_pairs={{0,64},{8,456},{64,0},{72,136},{128,192},{136,72},{192,128},{200,2... | collective-permute-start | bytes 786440 | tf_op jit(solution)/shard_map/section_top/ppermute | solution.py:48
  47.0 15.0 %collective-permute-start.6 = (bf16[256,256]{1,0:T(8,128)(2,1)}, bf16[256,256]{1,0:T(8,128)(2,1)S(1)}, u32[]{:S(2)}, u32[]{:S(2)}) collective-permute-start(bf16[256,256]{1,0:T(8,128)(2,1)} %all_gather.21), channel_id=1, source_target_pairs={{0,1},{1,0},{2,3},{3,2},{4,5},{5,4},{6,7},{7,6},{8,9},{9,8},{10,11... | collective-permute-start | bytes 393224 | tf_op jit(solution)/shard_map/section_top/ppermute | solution.py:180
  55.5 9.7 %collective-permute-start.7 = (bf16[8,128,128]{2,1,0:T(8,128)(2,1)}, bf16[8,128,128]{2,1,0:T(8,128)(2,1)}, u32[]{:S(2)}, u32[]{:S(2)}) collective-permute-start(bf16[8,128,128]{2,1,0:T(8,128)(2,1)} %collective-permute-done.3.refs_4_), channel_id=1, source_target_pairs={{0,448},{8,72},{64,128},{72,8},{128,64},{136,200},{192,256},{200,1... | collective-permute-start | bytes 786440 | tf_op jit(solution)/shard_map/section_top/ppermute | solution.py:48
  62.6 7.4 %collective-permute-start.8 = (bf16[8,128,128]{2,1,0:T(8,128)(2,1)}, bf16[8,128,128]{2,1,0:T(8,128)(2,1)}, u32[]{:S(2)}, u32[]{:S(2)}) collective-permute-start(bf16[8,128,128]{2,1,0:T(8,128)(2,1)} %collective-permute-done.4.refs_5_), channel_id=1, source_target_pairs={{0,448},{8,72},{64,128},{72,8},{128,64},{136,200},{192,256},{200,1... | collective-permute-start | bytes 786440 | tf_op jit(solution)/shard_map/section_top/ppermute | solution.py:48
  76.7 18.8 %all-to-all-start.1 = ((bf16[8,256,128]{2,1,0:T(8,128)(2,1)}), bf16[8,256,128]{2,1,0:T(8,128)(2,1)S(1)}, u32[]{:S(2)}, u32[]{:S(2)}) async-start(bf16[8,256,128]{2,1,0:T(8,128)(2,1)} %bitcast.58), calls=%async_computation.1 | async-start | bytes 1048576 | tf_op jit(solution)/shard_map/section_top/all_to_all | solution.py:183
  102.3 15.6 %all-to-all-start.2 = ((bf16[4,256,128]{2,1,0:T(8,128)(2,1)}), bf16[4,256,128]{2,1,0:T(8,128)(2,1)S(1)}, u32[]{:S(2)}, u32[]{:S(2)}) async-start(bf16[4,256,128]{2,1,0:T(8,128)(2,1)} %broadcast_in_dim.17), calls=%async_computation.2 | async-start | bytes 524288 | tf_op jit(solution)/shard_map/section_mid/all_to_all | solution.py:18
  119.4 9.0 %collective-permute-start.9 = (bf16[8,128,128]{2,1,0:T(8,128)(2,1)S(1)}, bf16[8,128,128]{2,1,0:T(8,128)(2,1)S(1)}, u32[]{:S(2)}, u32[]{:S(2)}) collective-permute-start(bf16[8,128,128]{2,1,0:T(8,128)(2,1)S(1)} %bitcast.60), channel_id=1, source_target_pairs={{0,64},{8,456},{64,0},{72,136},{128,192},{136,72},{192,128},{200,2... | collective-permute-start | bytes 786440 | tf_op jit(solution)/shard_map/section_mid/ppermute | solution.py:48
  121.3 27.6 %all-to-all-start.3 = ((bf16[4,2,256,256]{2,1,3,0:T(2,128)(2,1)}), bf16[4,2,256,256]{2,1,3,0:T(2,128)(2,1)S(1)}, u32[]{:S(2)}, u32[]{:S(2)}) async-start(bf16[4,2,256,256]{2,1,3,0:T(2,128)(2,1)} %broadcast_in_dim.18), calls=%async_computation.3 | async-start | bytes 2097152 | tf_op jit(solution)/shard_map/section_mid/all_to_all | solution.py:197
  124.8 7.7 %collective-permute-start.10 = (bf16[8,128,128]{2,1,0:T(8,128)(2,1)S(1)}, bf16[8,128,128]{2,1,0:T(8,128)(2,1)S(1)}, u32[]{:S(2)}, u32[]{:S(2)}) collective-permute-start(bf16[8,128,128]{2,1,0:T(8,128)(2,1)S(1)} %bitcast.61), channel_id=1, source_target_pairs={{0,448},{8,72},{64,128},{72,8},{128,64},{136,200},{192,256},{200,1... | collective-permute-start | bytes 786440 | tf_op jit(solution)/shard_map/section_mid/ppermute | solution.py:48
  128.4 8.4 %collective-permute-start.11 = (bf16[8,128,128]{2,1,0:T(8,128)(2,1)S(1)}, bf16[8,128,128]{2,1,0:T(8,128)(2,1)S(1)}, u32[]{:S(2)}, u32[]{:S(2)}) collective-permute-start(bf16[8,128,128]{2,1,0:T(8,128)(2,1)S(1)} %collective-permute-done.9.refs_1_), channel_id=1, source_target_pairs={{0,448},{8,72},{64,128},{72,8},{128,64},{136,200},{192,256},{200,1... | collective-permute-start | bytes 786440 | tf_op jit(solution)/shard_map/section_mid/ppermute | solution.py:48
  132.5 9.3 %collective-permute-start.12 = (bf16[8,128,128]{2,1,0:T(8,128)(2,1)S(1)}, bf16[8,128,128]{2,1,0:T(8,128)(2,1)}, u32[]{:S(2)}, u32[]{:S(2)}) collective-permute-start(bf16[8,128,128]{2,1,0:T(8,128)(2,1)S(1)} %collective-permute-done.10.refs_2_), channel_id=1, source_target_pairs={{0,64},{8,456},{64,0},{72,136},{128,192},{136,72},{192,128},{200,2... | collective-permute-start | bytes 786440 | tf_op jit(solution)/shard_map/section_mid/ppermute | solution.py:48
  136.8 9.2 %collective-permute-start.13 = (bf16[8,128,128]{2,1,0:T(8,128)(2,1)S(1)}, bf16[8,128,128]{2,1,0:T(8,128)(2,1)}, u32[]{:S(2)}, u32[]{:S(2)}) collective-permute-start(bf16[8,128,128]{2,1,0:T(8,128)(2,1)S(1)} %collective-permute-done.11.refs_3_), channel_id=1, source_target_pairs={{0,64},{8,456},{64,0},{72,136},{128,192},{136,72},{192,128},{200,2... | collective-permute-start | bytes 786440 | tf_op jit(solution)/shard_map/section_mid/ppermute | solution.py:48
  141.8 11.0 %collective-permute-start.14 = (bf16[8,128,128]{2,1,0:T(8,128)(2,1)}, bf16[8,128,128]{2,1,0:T(8,128)(2,1)}, u32[]{:S(2)}, u32[]{:S(2)}) collective-permute-start(bf16[8,128,128]{2,1,0:T(8,128)(2,1)} %collective-permute-done.12.refs_4_), channel_id=1, source_target_pairs={{0,448},{8,72},{64,128},{72,8},{128,64},{136,200},{192,256},{200,1... | collective-permute-start | bytes 786440 | tf_op jit(solution)/shard_map/section_mid/ppermute | solution.py:48
  146.0 10.0 %collective-permute-start.15 = (bf16[8,128,128]{2,1,0:T(8,128)(2,1)}, bf16[8,128,128]{2,1,0:T(8,128)(2,1)}, u32[]{:S(2)}, u32[]{:S(2)}) collective-permute-start(bf16[8,128,128]{2,1,0:T(8,128)(2,1)} %collective-permute-done.13.refs_5_), channel_id=1, source_target_pairs={{0,448},{8,72},{64,128},{72,8},{128,64},{136,200},{192,256},{200,1... | collective-permute-start | bytes 786440 | tf_op jit(solution)/shard_map/section_mid/ppermute | solution.py:48
  196.7 16.3 %all-to-all-start.6 = ((bf16[32,64,128]{2,1,0:T(8,128)(2,1)}), bf16[32,64,128]{2,1,0:T(8,128)(2,1)S(1)}, u32[]{:S(2)}, u32[]{:S(2)}) async-start(bf16[32,64,128]{2,1,0:T(8,128)(2,1)} %broadcast_in_dim.20), calls=%async_computation.6 | async-start | bytes 1048576 | tf_op jit(solution)/shard_map/weight_sums/all_to_all | solution.py:18
  (12 other events, 188.3 us)

commit v10 on v9

--- a/solution.py
+++ b/solution.py
@@ -165,17 +165,15 @@
         grad_top = jnp.where(mask_top > 0, grad_out, jnp.zeros_like(grad_out))
         unit_top = my_half(lax.all_gather(grad_top, "core", axis=0, tiled=True))
         pair = lax.all_gather(
-            jnp.stack([mask_mid.astype(BF16), feats_mid]), "core", axis=1, tiled=True
-        )
-        mask_pair = my_half(pair[0])
-        feats_mid_pair = pair[1]
+            jnp.stack([mask_mid.astype(BF16), feats_mid, feats_in]), "core", axis=1, tiled=True
+        )
     def gather_z(unit):
         return everyone(unit, "zl", ZL).reshape(-1, bs, half)
 
     with jax.named_scope("section_top"):
         units = gather_z(unit_top)
-        mine = lax.all_gather(feats_in, "core", axis=0, tiled=True)
-        adj, mine, units = lax.optimization_barrier((adj, mine, units))
+        adj, pair, units = lax.optimization_barrier((adj, pair, units))
+        mask_pair, feats_mid_pair, mine = my_half(pair[0]), pair[1], pair[2]
         other_adj = lax.ppermute(adj, "core", [(0, 1), (1, 0)])
         other = lax.ppermute(mine, "zh", [(0, 1), (1, 0)])
         pieces, meta, (other_adj, other) = gather_y(units, meta, (other_adj, other))
@@ -191,7 +189,7 @@
         grad_mid = jnp.where(mask_pair > 0, hidden, jnp.zeros_like(hidden)).astype(BF16)
     with jax.named_scope("section_mid"):
         first_zh = lax.axis_index("zh") == 0
-        both = jnp.stack([jnp.where(first_zh, mine, other), jnp.where(first_zh, other, mine)])
+        both = jnp.concatenate([jnp.where(first_zh, mine, other), jnp.where(first_zh, other, mine)])
         both = jnp.broadcast_to(both[None], (X,) + both.shape)
         units, both = lax.optimization_barrier((gather_z(grad_mid), both))
         feats_in_group = lax.all_to_all(both, "x", 0, 0, tiled=True).reshape(-1, feats)

time: 226 us -> 227 us (level)
  blocking collectives: 75 us -> 91.9 us
  waiting for transfers between devices: 42 us -> 33.8 us
  starting transfers between devices: 78.7 us -> 70.6 us
    all_to_all x0 -> x1, blocking collectives: none -> 18.9 us  [local(): lax.all_to_all(partial_top.reshape(NCOL, CORE * bs, half), COLS, 0, 0, ti...]
    all_to_all x1 -> x0, starting transfers between devices: 7.21 us -> none  [local(): lax.all_to_all(partial_top.reshape(NCOL, CORE * bs, half), COLS, 0, 0, ti...]
    all_to_all x1 -> x0, waiting for transfers between devices: 5.16 us -> none  [local(): lax.all_to_all(partial_top.reshape(NCOL, CORE * bs, half), COLS, 0, 0, ti...]
    all_gather x2 -> x1, blocking collectives: 6.62 us -> 2.22 us  [local(): lax.all_gather(jnp.stack([mask_mid.astype(BF16), feats_mid, feats_in]), '...]
  transfers between devices with their start and end apart: 21 -> 20, of which waited for: 11 -> 10; matrix products, arithmetic and copies ran while one was open for 3% -> 3% of each run, Pallas kernels for 0% -> 0%
where the time goes in v10:
time: 227 us; the launch traced here: 226 us
  blocking collectives  91.9 us (40%)
  starting transfers between devices  70.6 us (31%)
  waiting for transfers between devices  33.8 us (15%)
  Pallas kernels  13.2 us (6%)
  local copies, waits for them, and re-layouts  9.03 us (4%)
  matrix products  3.35 us (1%)
  other arithmetic  3.07 us (1%)
    ppermute x14, starting transfers between devices, swap(): return lax.ppermute(value, ('y', 'core'), y_pairs(which))  38.8 us
    all_to_all x1, blocking collectives, local(): lax.all_to_all(partial_top.reshape(NCOL, CORE * bs, half), COLS, 0, 0, ti...  18.9 us
    ppermute x14, waiting for transfers between devices, swap(): return lax.ppermute(value, ('y', 'core'), y_pairs(which))  17.9 us
    all_to_all x1, blocking collectives, local(): parts = lax.all_to_all(sent, COLS, 0, 0, tiled=True)  17.4 us
    all_to_all x3, starting transfers between devices, everyone(): lax.all_to_all(jnp.broadcast_to(value[None], (count,) + value.shape), axe...  15.4 us
    all_to_all x1, blocking collectives, everyone(): lax.all_to_all(jnp.broadcast_to(value[None], (count,) + value.shape), axe...  14.3 us
    pallas_call x2, Pallas kernels, spmm(): pl.pallas_call(spmm_kernel, out_shape=jax.ShapeDtypeStruct((NCOL, CORE, b...  13.2 us
    all_gather x1, blocking collectives, local(): whole = lax.all_gather(over_x * norm_scale, 'core', axis=3, tiled=True)  11.8 us
  transfers between devices with their start and end apart: 20, of which 10 were waited for; matrix products, arithmetic and copies ran while one was open for 3% of the time, Pallas kernels for 0%

profile of v10, /device:TPU:1, one launch (start us, length us, event | category | flops | bytes accessed | tf_op | source)
XLA Modules:
  0.0 226.2 jit_solution(11221968337156385858)
XLA Ops:
  1.8 8.4 %all_gather.19 = bf16[256,256]{1,0:T(8,128)(2,1)S(1)} all-gather(bf16[128,256]{1,0:T(8,128)(2,1)S(1)} %compare_select_fusion), channel_id=1, replica_groups=mesh['y'=8,'zl'=4,'core'=2,'x'=4,'zh'=2] {'core'}, dimensions={0}, use_global_device_ids=true | all-gather | bytes 196608 | tf_op jit(solution)/shard_map/pair_inputs/all_gather | solution.py:166
  16.6 5.1 %all-to-all-done = bf16[4,256,128]{2,1,0:T(8,128)(2,1)S(1)} async-done(((bf16[4,256,128]{2,1,0:T(8,128)(2,1)}), bf16[4,256,128]{2,1,0:T(8,128)(2,1)S(1)}, u32[]{:S(2)}, u32[]{:S(2)}) %all-to-all-start) | async-done | bytes 262176 | tf_op jit(solution)/shard_map/section_top/all_to_all | solution.py:18
  21.7 4.3 %collective-permute-start.5 = (bf16[8,12,128,128]{3,2,1,0:T(8,128)(2,1)}, bf16[8,12,128,128]{3,2,1,0:T(8,128)(2,1)S(1)}, u32[]{:S(2)}, u32[]{:S(2)}) collective-permute-start(bf16[8,12,128,128]{3,2,1,0:T(8,128)(2,1)} %bitcast.54), channel_id=1, source_target_pairs={{0,8},{8,0},{1,9},{9,1},{2,10},{10,2},{3,11},{11,3},{4,12},{12,4},... | collective-permute-start | bytes 9437192 | tf_op jit(solution)/shard_map/section_top/ppermute | solution.py:177
  31.3 3.8 %collective-permute-done.refs_1_ = bf16[8,128,128]{2,1,0:T(8,128)(2,1)} collective-permute-done((bf16[8,128,128]{2,1,0:T(8,128)(2,1)S(1)}, bf16[8,128,128]{2,1,0:T(8,128)(2,1)}, u32[]{:S(2)}, u32[]{:S(2)}) %collective-permute-start) | collective-permute-done | bytes 262176 | tf_op jit(solution)/shard_map/section_top/ppermute | solution.py:48
  43.6 3.4 %collective-permute-start.4 = (bf16[8,128,128]{2,1,0:T(8,128)(2,1)}, bf16[8,128,128]{2,1,0:T(8,128)(2,1)}, u32[]{:S(2)}, u32[]{:S(2)}) collective-permute-start(bf16[8,128,128]{2,1,0:T(8,128)(2,1)} %collective-permute-done.1.refs_3_), channel_id=1, source_target_pairs={{0,64},{8,456},{64,0},{72,136},{128,192},{136,72},{192,128},{200,2... | collective-permute-start | bytes 786440 | tf_op jit(solution)/shard_map/section_top/ppermute | solution.py:48
  48.8 8.5 %collective-permute-start.6 = (bf16[256,256]{1,0:T(8,128)(2,1)S(1)}, bf16[256,256]{1,0:T(8,128)(2,1)S(1)}, u32[]{:S(2)}, u32[]{:S(2)}) collective-permute-start(bf16[256,256]{1,0:T(8,128)(2,1)S(1)} %get-tuple-element.29), channel_id=1, source_target_pairs={{0,1},{1,0},{2,3},{3,2},{4,5},{5,4},{6,7},{7,6},{8,9},{9,8},{10,11... | collective-permute-start | bytes 393224 | tf_op jit(solution)/shard_map/section_top/ppermute | solution.py:178
  59.2 4.3 %collective-permute-done.6 = bf16[256,256]{1,0:T(8,128)(2,1)S(1)} collective-permute-done((bf16[256,256]{1,0:T(8,128)(2,1)S(1)}, bf16[256,256]{1,0:T(8,128)(2,1)S(1)}, u32[]{:S(2)}, u32[]{:S(2)}) %collective-permute-start.6) | collective-permute-done | bytes 131104 | tf_op jit(solution)/shard_map/section_top/ppermute | solution.py:178
  66.8 4.9 %collective-permute-done.8.refs_7_ = bf16[8,128,128]{2,1,0:T(8,128)(2,1)} collective-permute-done((bf16[8,128,128]{2,1,0:T(8,128)(2,1)}, bf16[8,128,128]{2,1,0:T(8,128)(2,1)}, u32[]{:S(2)}, u32[]{:S(2)}) %collective-permute-start.8) | collective-permute-done | bytes 262176 | tf_op jit(solution)/shard_map/section_top/ppermute | solution.py:48
  71.6 6.6 %section_top.1 = bf16[8,2,128,128]{3,2,1,0:T(8,128)(2,1)} custom-call(s32[256]{0:T(256)} %reshape.69.meta_ref, s32[128]{0:T(128)} %constant.34.clone.table_ref, s32[2]{0:T(128)} %pad_add_fusion.place_ref, bf16[8,128,128]{2,1,0:T(8,128)(2,1)} %bitcast.68, bf16[8,128,128]{2,1,0:T(8,128)(2,1)} %collective-permute-done.refs_1_, ...), custom_call_target="tpu_custom_call" | custom-call | tf_op jit(solution)/shard_map/section_top/pallas_call | solution.py:121
  78.3 18.9 %all_to_all.35 = bf16[8,256,128]{2,1,0:T(8,128)(2,1)S(1)} all-to-all(bf16[8,256,128]{2,1,0:T(8,128)(2,1)} %bitcast.61), channel_id=1, replica_groups=mesh['y'=8,'zl'=4,'core'=2,'x'=4,'zh'=2] {'x','zh'}, dimensions={0} | all-to-all | bytes 1048576 | tf_op jit(solution)/shard_map/section_top/all_to_all | solution.py:181
  97.3 5.8 %all_gather.21 = bf16[256,256]{1,0:T(8,128)(2,1)S(1)} all-gather(bf16[256,128]{1,0:T(8,128)(2,1)S(1)} %reduce_sum.42), channel_id=1, replica_groups=mesh['y'=8,'zl'=4,'core'=2,'x'=4,'zh'=2] {'core'}, dimensions={1}, use_global_device_ids=true | all-gather | bytes 196608 | tf_op jit(solution)/shard_map/section_top/all_gather | solution.py:185
  104.0 8.1 %all-to-all-start.2 = ((bf16[4,256,128]{2,1,0:T(8,128)(2,1)}), bf16[4,256,128]{2,1,0:T(8,128)(2,1)S(1)}, u32[]{:S(2)}, u32[]{:S(2)}) async-start(bf16[4,256,128]{2,1,0:T(8,128)(2,1)} %broadcast_in_dim.17), calls=%async_computation.2 | async-start | bytes 524288 | tf_op jit(solution)/shard_map/section_mid/all_to_all | solution.py:18
  113.3 6.3 %all-to-all-done.2 = bf16[4,256,128]{2,1,0:T(8,128)(2,1)S(1)} async-done(((bf16[4,256,128]{2,1,0:T(8,128)(2,1)}), bf16[4,256,128]{2,1,0:T(8,128)(2,1)S(1)}, u32[]{:S(2)}, u32[]{:S(2)}) %all-to-all-start.2) | async-done | bytes 262176 | tf_op jit(solution)/shard_map/section_mid/all_to_all | solution.py:18
  122.7 3.5 %all-to-all-start.3 = ((bf16[4,512,256]{1,2,0:T(8,128)(2,1)}), bf16[4,512,256]{1,2,0:T(8,128)(2,1)S(1)}, u32[]{:S(2)}, u32[]{:S(2)}) async-start(bf16[4,512,256]{1,2,0:T(8,128)(2,1)} %broadcast_in_dim.18), calls=%async_computation.3 | async-start | bytes 2097152 | tf_op jit(solution)/shard_map/section_mid/all_to_all | solution.py:195
  126.2 3.5 %collective-permute-start.10 = (bf16[8,128,128]{2,1,0:T(8,128)(2,1)S(1)}, bf16[8,128,128]{2,1,0:T(8,128)(2,1)S(1)}, u32[]{:S(2)}, u32[]{:S(2)}) collective-permute-start(bf16[8,128,128]{2,1,0:T(8,128)(2,1)S(1)} %bitcast.64), channel_id=1, source_target_pairs={{0,448},{8,72},{64,128},{72,8},{128,64},{136,200},{192,256},{200,1... | collective-permute-start | bytes 786440 | tf_op jit(solution)/shard_map/section_mid/ppermute | solution.py:48
  133.9 4.3 %collective-permute-start.12 = (bf16[8,128,128]{2,1,0:T(8,128)(2,1)S(1)}, bf16[8,128,128]{2,1,0:T(8,128)(2,1)S(1)}, u32[]{:S(2)}, u32[]{:S(2)}) collective-permute-start(bf16[8,128,128]{2,1,0:T(8,128)(2,1)S(1)} %collective-permute-done.10.refs_2_), channel_id=1, source_target_pairs={{0,64},{8,456},{64,0},{72,136},{128,192},{136,72},{192,128},{200,2... | collective-permute-start | bytes 786440 | tf_op jit(solution)/shard_map/section_mid/ppermute | solution.py:48
  143.1 4.2 %collective-permute-start.14 = (bf16[8,128,128]{2,1,0:T(8,128)(2,1)S(1)}, bf16[8,128,128]{2,1,0:T(8,128)(2,1)}, u32[]{:S(2)}, u32[]{:S(2)}) collective-permute-start(bf16[8,128,128]{2,1,0:T(8,128)(2,1)S(1)} %collective-permute-done.12.refs_4_), channel_id=1, source_target_pairs={{0,448},{8,72},{64,128},{72,8},{128,64},{136,200},{192,256},{200,1... | collective-permute-start | bytes 786440 | tf_op jit(solution)/shard_map/section_mid/ppermute | solution.py:48
  153.4 3.7 %collective-permute-done.15.refs_7_ = bf16[8,128,128]{2,1,0:T(8,128)(2,1)} collective-permute-done((bf16[8,128,128]{2,1,0:T(8,128)(2,1)S(1)}, bf16[8,128,128]{2,1,0:T(8,128)(2,1)}, u32[]{:S(2)}, u32[]{:S(2)}) %collective-permute-start.15) | collective-permute-done | bytes 262176 | tf_op jit(solution)/shard_map/section_mid/ppermute | solution.py:48
  157.0 6.6 %section_mid.1 = bf16[8,2,128,128]{3,2,1,0:T(8,128)(2,1)} custom-call(s32[256]{0:T(256)} %reshape.69.meta_ref, s32[128]{0:T(128)} %constant.34.clone.table_ref, s32[2]{0:T(128)} %pad_add_fusion.place_ref, bf16[8,128,128]{2,1,0:T(8,128)(2,1)} %bitcast.65, bf16[8,128,128]{2,1,0:T(8,128)(2,1)} %copy-done.7, bf16[8,128,128]{2,1,0:T(8,128)(2,1)} %copy-done.8, ...), custom_call_target="tpu_custom_call" | custom-call | tf_op jit(solution)/shard_map/section_mid/pallas_call | solution.py:121
  165.3 17.4 %all_to_all.36 = bf16[8,320,128]{2,1,0:T(8,128)(2,1)S(1)} all-to-all(bf16[8,320,128]{2,1,0:T(8,128)(2,1)S(1)} %pad_maximum_fusion), channel_id=1, replica_groups=mesh['y'=8,'zl'=4,'core'=2,'x'=4,'zh'=2] {'x','zh'}, dimensions={0} | all-to-all | bytes 1310720 | tf_op jit(solution)/shard_map/section_mid/all_to_all | solution.py:203
  182.9 14.3 %all_to_all.37 = bf16[8,64,128]{2,1,0:T(8,128)(2,1)S(1)} all-to-all(bf16[8,64,128]{2,1,0:T(8,128)(2,1)S(1)} %broadcast_in_dim.19), channel_id=1, replica_groups=mesh['y'=8,'zl'=4,'core'=2,'x'=4,'zh'=2] {'y'}, dimensions={0} | all-to-all | bytes 262144 | tf_op jit(solution)/shard_map/weight_sums/all_to_all | solution.py:18
  198.1 3.9 %all-to-all-start.6 = ((bf16[32,64,128]{2,1,0:T(8,128)(2,1)}), bf16[32,64,128]{2,1,0:T(8,128)(2,1)S(1)}, u32[]{:S(2)}, u32[]{:S(2)}) async-start(bf16[32,64,128]{2,1,0:T(8,128)(2,1)} %broadcast_in_dim.20), calls=%async_computation.6 | async-start | bytes 1048576 | tf_op jit(solution)/shard_map/weight_sums/all_to_all | solution.py:18
  202.0 10.4 %all_gather.22 = bf16[256,256]{1,0:T(8,128)(2,1)S(1)} all-gather(bf16[256,128]{1,0:T(8,128)(2,1)S(1)} %slice.32), channel_id=1, replica_groups=mesh['y'=8,'zl'=4,'core'=2,'x'=4,'zh'=2] {'core'}, dimensions={1}, use_global_device_ids=true | all-gather | bytes 196608 | tf_op jit(solution)/shard_map/section_mid/all_gather | solution.py:206
  213.5 11.8 %all_gather.23 = f32[8,2,32,256]{3,2,1,0:T(8,128)S(1)} all-gather(f32[8,2,32,128]{3,2,1,0:T(8,128)S(1)} %bitcast.69), channel_id=1, replica_groups=mesh['y'=8,'zl'=4,'core'=2,'x'=4,'zh'=2] {'core'}, dimensions={3}, use_global_device_ids=true | all-gather | bytes 786432 | tf_op jit(solution)/shard_map/weight_sums/all_gather | solution.py:216
  (106 shorter events, 52.8 us)
Async XLA Ops:
  0.6 102.4 %copy-start = (bf16[256,256]{1,0:T(8,128)(2,1)S(1)}, bf16[256,256]{1,0:T(8,128)(2,1)}, u32[]{:S(2)}) copy-start(bf16[256,256]{1,0:T(8,128)(2,1)} %param.18) | copy-start | bytes 393220
  0.7 36.4 %copy-start.20 = (s32[8,1]{0,1:T(1,128)S(1)}, s32[8,1]{0,1:T(1,128)}, u32[]{:S(2)}) copy-start(s32[8,1]{0,1:T(1,128)} %param.21) | copy-start | bytes 100
  0.7 36.5 %copy-start.19 = (s32[8,1,12]{2,1,0:T(1,128)S(1)}, s32[8,1,12]{2,1,0:T(1,128)}, u32[]{:S(2)}) copy-start(s32[8,1,12]{2,1,0:T(1,128)} %param.20) | copy-start | bytes 1156
  10.9 10.8 %all-to-all-start = ((bf16[4,256,128]{2,1,0:T(8,128)(2,1)}), bf16[4,256,128]{2,1,0:T(8,128)(2,1)S(1)}, u32[]{:S(2)}, u32[]{:S(2)}) async-start(bf16[4,256,128]{2,1,0:T(8,128)(2,1)} %broadcast_in_dim.15), calls=%async_computation | async-start | bytes 524288 | tf_op jit(solution)/shard_map/section_top/all_to_all | solution.py:18
  21.7 49.9 %copy-start.4 = (bf16[4,256,128]{2,1,0:T(8,128)(2,1)}, bf16[4,256,128]{2,1,0:T(8,128)(2,1)S(1)}, u32[]{:S(2)}) copy-start(bf16[4,256,128]{2,1,0:T(8,128)(2,1)S(1)} %all-to-all-done) | copy-start | bytes 786436
  21.7 41.8 %collective-permute-start.5 = (bf16[8,12,128,128]{3,2,1,0:T(8,128)(2,1)}, bf16[8,12,128,128]{3,2,1,0:T(8,128)(2,1)S(1)}, u32[]{:S(2)}, u32[]{:S(2)}) collective-permute-start(bf16[8,12,128,128]{3,2,1,0:T(8,128)(2,1)} %bitcast.54), channel_id=1, source_target_pairs={{0,8},{8,0},{1,9},{9,1},{2,10},{10,2},{3,11},{11,3},{4,12},{12,4},... | collective-permute-start | bytes 9437192 | tf_op jit(solution)/shard_map/section_top/ppermute | solution.py:177
  26.0 9.1 %collective-permute-start = (bf16[8,128,128]{2,1,0:T(8,128)(2,1)S(1)}, bf16[8,128,128]{2,1,0:T(8,128)(2,1)}, u32[]{:S(2)}, u32[]{:S(2)}) collective-permute-start(bf16[8,128,128]{2,1,0:T(8,128)(2,1)S(1)} %bitcast.66), channel_id=1, source_target_pairs={{0,64},{8,456},{64,0},{72,136},{128,192},{136,72},{192,128},{200,2... | collective-permute-start | bytes 786440 | tf_op jit(solution)/shard_map/section_top/ppermute | solution.py:48
  29.4 11.1 %collective-permute-start.2 = (bf16[8,128,128]{2,1,0:T(8,128)(2,1)S(1)}, bf16[8,128,128]{2,1,0:T(8,128)(2,1)}, u32[]{:S(2)}, u32[]{:S(2)}) collective-permute-start(bf16[8,128,128]{2,1,0:T(8,128)(2,1)S(1)} %bitcast.67), channel_id=1, source_target_pairs={{0,448},{8,72},{64,128},{72,8},{128,64},{136,200},{192,256},{200,1... | collective-permute-start | bytes 786440 | tf_op jit(solution)/shard_map/section_top/ppermute | solution.py:48
  35.1 8.5 %collective-permute-start.1 = (bf16[8,128,128]{2,1,0:T(8,128)(2,1)}, bf16[8,128,128]{2,1,0:T(8,128)(2,1)}, u32[]{:S(2)}, u32[]{:S(2)}) collective-permute-start(bf16[8,128,128]{2,1,0:T(8,128)(2,1)} %collective-permute-done.refs_1_), channel_id=1, source_target_pairs={{0,448},{8,72},{64,128},{72,8},{128,64},{136,200},{192,256},{200,1... | collective-permute-start | bytes 786440 | tf_op jit(solution)/shard_map/section_top/ppermute | solution.py:48
  40.5 16.7 %collective-permute-start.3 = (bf16[8,128,128]{2,1,0:T(8,128)(2,1)}, bf16[8,128,128]{2,1,0:T(8,128)(2,1)}, u32[]{:S(2)}, u32[]{:S(2)}) collective-permute-start(bf16[8,128,128]{2,1,0:T(8,128)(2,1)} %collective-permute-done.2.refs_2_), channel_id=1, source_target_pairs={{0,64},{8,456},{64,0},{72,136},{128,192},{136,72},{192,128},{200,2... | collective-permute-start | bytes 786440 | tf_op jit(solution)/shard_map/section_top/ppermute | solution.py:48
  43.6 20.0 %collective-permute-start.4 = (bf16[8,128,128]{2,1,0:T(8,128)(2,1)}, bf16[8,128,128]{2,1,0:T(8,128)(2,1)}, u32[]{:S(2)}, u32[]{:S(2)}) collective-permute-start(bf16[8,128,128]{2,1,0:T(8,128)(2,1)} %collective-permute-done.1.refs_3_), channel_id=1, source_target_pairs={{0,64},{8,456},{64,0},{72,136},{128,192},{136,72},{192,128},{200,2... | collective-permute-start | bytes 786440 | tf_op jit(solution)/shard_map/section_top/ppermute | solution.py:48
  48.8 14.8 %collective-permute-start.6 = (bf16[256,256]{1,0:T(8,128)(2,1)S(1)}, bf16[256,256]{1,0:T(8,128)(2,1)S(1)}, u32[]{:S(2)}, u32[]{:S(2)}) collective-permute-start(bf16[256,256]{1,0:T(8,128)(2,1)S(1)} %get-tuple-element.29), channel_id=1, source_target_pairs={{0,1},{1,0},{2,3},{3,2},{4,5},{5,4},{6,7},{7,6},{8,9},{9,8},{10,11... | collective-permute-start | bytes 393224 | tf_op jit(solution)/shard_map/section_top/ppermute | solution.py:178
  57.3 9.5 %collective-permute-start.7 = (bf16[8,128,128]{2,1,0:T(8,128)(2,1)}, bf16[8,128,128]{2,1,0:T(8,128)(2,1)}, u32[]{:S(2)}, u32[]{:S(2)}) collective-permute-start(bf16[8,128,128]{2,1,0:T(8,128)(2,1)} %collective-permute-done.3.refs_4_), channel_id=1, source_target_pairs={{0,448},{8,72},{64,128},{72,8},{128,64},{136,200},{192,256},{200,1... | collective-permute-start | bytes 786440 | tf_op jit(solution)/shard_map/section_top/ppermute | solution.py:48
  64.2 7.4 %collective-permute-start.8 = (bf16[8,128,128]{2,1,0:T(8,128)(2,1)}, bf16[8,128,128]{2,1,0:T(8,128)(2,1)}, u32[]{:S(2)}, u32[]{:S(2)}) collective-permute-start(bf16[8,128,128]{2,1,0:T(8,128)(2,1)} %collective-permute-done.4.refs_5_), channel_id=1, source_target_pairs={{0,448},{8,72},{64,128},{72,8},{128,64},{136,200},{192,256},{200,1... | collective-permute-start | bytes 786440 | tf_op jit(solution)/shard_map/section_top/ppermute | solution.py:48
  104.0 15.6 %all-to-all-start.2 = ((bf16[4,256,128]{2,1,0:T(8,128)(2,1)}), bf16[4,256,128]{2,1,0:T(8,128)(2,1)S(1)}, u32[]{:S(2)}, u32[]{:S(2)}) async-start(bf16[4,256,128]{2,1,0:T(8,128)(2,1)} %broadcast_in_dim.17), calls=%async_computation.2 | async-start | bytes 524288 | tf_op jit(solution)/shard_map/section_mid/all_to_all | solution.py:18
  120.6 9.1 %collective-permute-start.9 = (bf16[8,128,128]{2,1,0:T(8,128)(2,1)S(1)}, bf16[8,128,128]{2,1,0:T(8,128)(2,1)S(1)}, u32[]{:S(2)}, u32[]{:S(2)}) collective-permute-start(bf16[8,128,128]{2,1,0:T(8,128)(2,1)S(1)} %bitcast.63), channel_id=1, source_target_pairs={{0,64},{8,456},{64,0},{72,136},{128,192},{136,72},{192,128},{200,2... | collective-permute-start | bytes 786440 | tf_op jit(solution)/shard_map/section_mid/ppermute | solution.py:48
  122.7 28.1 %all-to-all-start.3 = ((bf16[4,512,256]{1,2,0:T(8,128)(2,1)}), bf16[4,512,256]{1,2,0:T(8,128)(2,1)S(1)}, u32[]{:S(2)}, u32[]{:S(2)}) async-start(bf16[4,512,256]{1,2,0:T(8,128)(2,1)} %broadcast_in_dim.18), calls=%async_computation.3 | async-start | bytes 2097152 | tf_op jit(solution)/shard_map/section_mid/all_to_all | solution.py:195
  126.2 7.7 %collective-permute-start.10 = (bf16[8,128,128]{2,1,0:T(8,128)(2,1)S(1)}, bf16[8,128,128]{2,1,0:T(8,128)(2,1)S(1)}, u32[]{:S(2)}, u32[]{:S(2)}) collective-permute-start(bf16[8,128,128]{2,1,0:T(8,128)(2,1)S(1)} %bitcast.64), channel_id=1, source_target_pairs={{0,448},{8,72},{64,128},{72,8},{128,64},{136,200},{192,256},{200,1... | collective-permute-start | bytes 786440 | tf_op jit(solution)/shard_map/section_mid/ppermute | solution.py:48
  129.8 8.4 %collective-permute-start.11 = (bf16[8,128,128]{2,1,0:T(8,128)(2,1)S(1)}, bf16[8,128,128]{2,1,0:T(8,128)(2,1)S(1)}, u32[]{:S(2)}, u32[]{:S(2)}) collective-permute-start(bf16[8,128,128]{2,1,0:T(8,128)(2,1)S(1)} %collective-permute-done.9.refs_1_), channel_id=1, source_target_pairs={{0,448},{8,72},{64,128},{72,8},{128,64},{136,200},{192,256},{200,1... | collective-permute-start | bytes 786440 | tf_op jit(solution)/shard_map/section_mid/ppermute | solution.py:48
  133.9 9.2 %collective-permute-start.12 = (bf16[8,128,128]{2,1,0:T(8,128)(2,1)S(1)}, bf16[8,128,128]{2,1,0:T(8,128)(2,1)S(1)}, u32[]{:S(2)}, u32[]{:S(2)}) collective-permute-start(bf16[8,128,128]{2,1,0:T(8,128)(2,1)S(1)} %collective-permute-done.10.refs_2_), channel_id=1, source_target_pairs={{0,64},{8,456},{64,0},{72,136},{128,192},{136,72},{192,128},{200,2... | collective-permute-start | bytes 786440 | tf_op jit(solution)/shard_map/section_mid/ppermute | solution.py:48
  138.2 9.0 %collective-permute-start.13 = (bf16[8,128,128]{2,1,0:T(8,128)(2,1)S(1)}, bf16[8,128,128]{2,1,0:T(8,128)(2,1)S(1)}, u32[]{:S(2)}, u32[]{:S(2)}) collective-permute-start(bf16[8,128,128]{2,1,0:T(8,128)(2,1)S(1)} %collective-permute-done.11.refs_3_), channel_id=1, source_target_pairs={{0,64},{8,456},{64,0},{72,136},{128,192},{136,72},{192,128},{200,2... | collective-permute-start | bytes 786440 | tf_op jit(solution)/shard_map/section_mid/ppermute | solution.py:48
  143.1 10.3 %collective-permute-start.14 = (bf16[8,128,128]{2,1,0:T(8,128)(2,1)S(1)}, bf16[8,128,128]{2,1,0:T(8,128)(2,1)}, u32[]{:S(2)}, u32[]{:S(2)}) collective-permute-start(bf16[8,128,128]{2,1,0:T(8,128)(2,1)S(1)} %collective-permute-done.12.refs_4_), channel_id=1, source_target_pairs={{0,448},{8,72},{64,128},{72,8},{128,64},{136,200},{192,256},{200,1... | collective-permute-start | bytes 786440 | tf_op jit(solution)/shard_map/section_mid/ppermute | solution.py:48
  147.3 9.7 %collective-permute-start.15 = (bf16[8,128,128]{2,1,0:T(8,128)(2,1)S(1)}, bf16[8,128,128]{2,1,0:T(8,128)(2,1)}, u32[]{:S(2)}, u32[]{:S(2)}) collective-permute-start(bf16[8,128,128]{2,1,0:T(8,128)(2,1)S(1)} %collective-permute-done.13.refs_5_), channel_id=1, source_target_pairs={{0,448},{8,72},{64,128},{72,8},{128,64},{136,200},{192,256},{200,1... | collective-permute-start | bytes 786440 | tf_op jit(solution)/shard_map/section_mid/ppermute | solution.py:48
  198.1 15.3 %all-to-all-start.6 = ((bf16[32,64,128]{2,1,0:T(8,128)(2,1)}), bf16[32,64,128]{2,1,0:T(8,128)(2,1)S(1)}, u32[]{:S(2)}, u32[]{:S(2)}) async-start(bf16[32,64,128]{2,1,0:T(8,128)(2,1)} %broadcast_in_dim.20), calls=%async_computation.6 | async-start | bytes 1048576 | tf_op jit(solution)/shard_map/weight_sums/all_to_all | solution.py:18
  (17 other events, 241.2 us)

commit v11 on v9

--- a/solution.py
+++ b/solution.py
@@ -173,10 +173,11 @@
         return everyone(unit, "zl", ZL).reshape(-1, bs, half)
 
     with jax.named_scope("section_top"):
+        adj, unit_top = lax.optimization_barrier((adj, unit_top))
+        other_adj = lax.ppermute(adj, "core", [(0, 1), (1, 0)])
         units = gather_z(unit_top)
         mine = lax.all_gather(feats_in, "core", axis=0, tiled=True)
-        adj, mine, units = lax.optimization_barrier((adj, mine, units))
-        other_adj = lax.ppermute(adj, "core", [(0, 1), (1, 0)])
+        mine, units = lax.optimization_barrier((mine, units))
         other = lax.ppermute(mine, "zh", [(0, 1), (1, 0)])
         pieces, meta, (other_adj, other) = gather_y(units, meta, (other_adj, other))
         partial_top = spmm(meta, place, pieces, adj, other_adj)

time: 226 us -> 228 us (level)
  blocking collectives: 75 us -> 80.7 us
  waiting for transfers between devices: 42 us -> 39.3 us
    all_gather x1, blocking collectives: 2.6 us -> 6.95 us  [local(): meta = lax.all_gather(meta, 'core', axis=0, tiled=True).reshape(-1)]
    ppermute x1, waiting for transfers between devices: 4.55 us -> 1.97 us  [local(): other = lax.ppermute(mine, 'zh', [(0, 1), (1, 0)])]
    all_to_all x1, starting transfers between devices: 7.21 us -> 9.63 us  [local(): lax.all_to_all(partial_top.reshape(NCOL, CORE * bs, half), COLS, 0, 0, ti...]
  transfers between devices with their start and end apart: 21 -> 21, of which waited for: 11 -> 12; matrix products, arithmetic and copies ran while one was open for 3% -> 3% of each run, Pallas kernels for 0% -> 0%
where the time goes in v11:
time: 228 us; the launch traced here: 227 us
  blocking collectives  80.7 us (35%)
  starting transfers between devices  77.7 us (34%)
  waiting for transfers between devices  39.3 us (17%)
  Pallas kernels  13.3 us (6%)
  local copies, waits for them, and re-layouts  7.98 us (4%)
  other arithmetic  3.82 us (2%)
  matrix products  2.72 us (1%)
    ppermute x14, starting transfers between devices, swap(): return lax.ppermute(value, ('y', 'core'), y_pairs(which))  37.6 us
    ppermute x14, waiting for transfers between devices, swap(): return lax.ppermute(value, ('y', 'core'), y_pairs(which))  19.2 us
    all_to_all x1, blocking collectives, local(): parts = lax.all_to_all(sent, COLS, 0, 0, tiled=True)  17 us
    all_to_all x3, starting transfers between devices, everyone(): lax.all_to_all(jnp.broadcast_to(value[None], (count,) + value.shape), axe...  16.3 us
    all_to_all x1, blocking collectives, everyone(): lax.all_to_all(jnp.broadcast_to(value[None], (count,) + value.shape), axe...  14.5 us
    pallas_call x2, Pallas kernels, spmm(): pl.pallas_call(spmm_kernel, out_shape=jax.ShapeDtypeStruct((NCOL, CORE, b...  13.3 us
    all_to_all x3, waiting for transfers between devices, everyone(): lax.all_to_all(jnp.broadcast_to(value[None], (count,) + value.shape), axe...  12.9 us
    all_gather x1, blocking collectives, local(): whole = lax.all_gather(over_x * norm_scale, 'core', axis=3, tiled=True)  10.8 us
  transfers between devices with their start and end apart: 21, of which 12 were waited for; matrix products, arithmetic and copies ran while one was open for 3% of the time, Pallas kernels for 0%

profile of v11, /device:TPU:1, one launch (start us, length us, event | category | flops | bytes accessed | tf_op | source)
XLA Modules:
  0.0 226.6 jit_solution(10289690755981003257)
XLA Ops:
  1.7 8.4 %all_gather.22 = bf16[256,256]{1,0:T(8,128)(2,1)S(1)} all-gather(bf16[128,256]{1,0:T(8,128)(2,1)S(1)} %compare_select_fusion), channel_id=1, replica_groups=mesh['y'=8,'zl'=4,'core'=2,'x'=4,'zh'=2] {'core'}, dimensions={0}, use_global_device_ids=true | all-gather | bytes 196608 | tf_op jit(solution)/shard_map/pair_inputs/all_gather | solution.py:166
  13.1 3.4 %all-to-all-start = ((bf16[4,256,128]{2,1,0:T(8,128)(2,1)}), bf16[4,256,128]{2,1,0:T(8,128)(2,1)S(1)}, u32[]{:S(2)}, u32[]{:S(2)}) async-start(bf16[4,256,128]{2,1,0:T(8,128)(2,1)} %broadcast_in_dim.15), calls=%async_computation | async-start | bytes 524288 | tf_op jit(solution)/shard_map/section_top/all_to_all | solution.py:18
  19.9 4.6 %all-to-all-done = bf16[4,256,128]{2,1,0:T(8,128)(2,1)S(1)} async-done(((bf16[4,256,128]{2,1,0:T(8,128)(2,1)}), bf16[4,256,128]{2,1,0:T(8,128)(2,1)S(1)}, u32[]{:S(2)}, u32[]{:S(2)}) %all-to-all-start) | async-done | bytes 262176 | tf_op jit(solution)/shard_map/section_top/all_to_all | solution.py:18
  29.1 3.8 %collective-permute-done.refs_1_ = bf16[8,128,128]{2,1,0:T(8,128)(2,1)} collective-permute-done((bf16[8,128,128]{2,1,0:T(8,128)(2,1)S(1)}, bf16[8,128,128]{2,1,0:T(8,128)(2,1)}, u32[]{:S(2)}, u32[]{:S(2)}) %collective-permute-start) | collective-permute-done | bytes 262176 | tf_op jit(solution)/shard_map/section_top/ppermute | solution.py:48
  35.0 7.0 %all_gather.23 = s32[16,16]{1,0:T(8,128)S(1)} all-gather(s32[8,16]{1,0:T(8,128)S(1)} %add_add_fusion), channel_id=1, replica_groups=mesh['y'=8,'zl'=4,'core'=2,'x'=4,'zh'=2] {'core'}, dimensions={0}, use_global_device_ids=true | all-gather | bytes 1536 | tf_op jit(solution)/shard_map/all_gather | solution.py:161
  42.6 3.7 %collective-permute-start.3 = (bf16[8,128,128]{2,1,0:T(8,128)(2,1)}, bf16[8,128,128]{2,1,0:T(8,128)(2,1)}, u32[]{:S(2)}, u32[]{:S(2)}) collective-permute-start(bf16[8,128,128]{2,1,0:T(8,128)(2,1)} %collective-permute-done.2.refs_2_), channel_id=1, source_target_pairs={{0,64},{8,456},{64,0},{72,136},{128,192},{136,72},{192,128},{200,2... | collective-permute-start | bytes 786440 | tf_op jit(solution)/shard_map/section_top/ppermute | solution.py:48
  49.1 8.4 %collective-permute-start.6 = (bf16[256,256]{1,0:T(8,128)(2,1)}, bf16[256,256]{1,0:T(8,128)(2,1)S(1)}, u32[]{:S(2)}, u32[]{:S(2)}) collective-permute-start(bf16[256,256]{1,0:T(8,128)(2,1)} %all_gather.21), channel_id=1, source_target_pairs={{0,1},{1,0},{2,3},{3,2},{4,5},{5,4},{6,7},{7,6},{8,9},{9,8},{10,11... | collective-permute-start | bytes 393224 | tf_op jit(solution)/shard_map/section_top/ppermute | solution.py:181
  65.3 4.5 %collective-permute-done.8.refs_7_ = bf16[8,128,128]{2,1,0:T(8,128)(2,1)} collective-permute-done((bf16[8,128,128]{2,1,0:T(8,128)(2,1)}, bf16[8,128,128]{2,1,0:T(8,128)(2,1)}, u32[]{:S(2)}, u32[]{:S(2)}) %collective-permute-start.8) | collective-permute-done | bytes 262176 | tf_op jit(solution)/shard_map/section_top/ppermute | solution.py:48
  69.9 6.6 %section_top.1 = bf16[8,2,128,128]{3,2,1,0:T(8,128)(2,1)} custom-call(s32[256]{0:T(256)} %reshape.69.meta_ref, s32[128]{0:T(128)} %constant.34.clone.table_ref, s32[2]{0:T(128)} %pad_add_fusion.place_ref, bf16[8,128,128]{2,1,0:T(8,128)(2,1)} %bitcast.65, bf16[8,128,128]{2,1,0:T(8,128)(2,1)} %collective-permute-done.refs_1_, ...), custom_call_target="tpu_custom_call" | custom-call | tf_op jit(solution)/shard_map/section_top/pallas_call | solution.py:121
  76.5 9.6 %all-to-all-start.1 = ((bf16[8,256,128]{2,1,0:T(8,128)(2,1)}), bf16[8,256,128]{2,1,0:T(8,128)(2,1)S(1)}, u32[]{:S(2)}, u32[]{:S(2)}) async-start(bf16[8,256,128]{2,1,0:T(8,128)(2,1)} %bitcast.58), calls=%async_computation.1 | async-start | bytes 1048576 | tf_op jit(solution)/shard_map/section_top/all_to_all | solution.py:184
  87.9 4.5 %all_gather.24 = bf16[2,256,256]{2,1,0:T(8,128)(2,1)S(1)} all-gather(bf16[2,128,256]{2,1,0:T(8,128)(2,1)S(1)} %pad_maximum_fusion.2), channel_id=1, replica_groups=mesh['y'=8,'zl'=4,'core'=2,'x'=4,'zh'=2] {'core'}, dimensions={1}, use_global_device_ids=true | all-gather | bytes 393216 | tf_op jit(solution)/shard_map/pair_inputs/all_gather | solution.py:167
  92.5 5.2 %all-to-all-done.1 = bf16[8,256,128]{2,1,0:T(8,128)(2,1)S(1)} async-done(((bf16[8,256,128]{2,1,0:T(8,128)(2,1)}), bf16[8,256,128]{2,1,0:T(8,128)(2,1)S(1)}, u32[]{:S(2)}, u32[]{:S(2)}) %all-to-all-start.1) | async-done | bytes 524320 | tf_op jit(solution)/shard_map/section_top/all_to_all | solution.py:184
  97.8 5.8 %all_gather.25 = bf16[256,256]{1,0:T(8,128)(2,1)S(1)} all-gather(bf16[256,128]{1,0:T(8,128)(2,1)S(1)} %reduce_sum.42), channel_id=1, replica_groups=mesh['y'=8,'zl'=4,'core'=2,'x'=4,'zh'=2] {'core'}, dimensions={1}, use_global_device_ids=true | all-gather | bytes 196608 | tf_op jit(solution)/shard_map/section_top/all_gather | solution.py:188
  104.5 8.0 %all-to-all-start.2 = ((bf16[4,256,128]{2,1,0:T(8,128)(2,1)}), bf16[4,256,128]{2,1,0:T(8,128)(2,1)S(1)}, u32[]{:S(2)}, u32[]{:S(2)}) async-start(bf16[4,256,128]{2,1,0:T(8,128)(2,1)} %broadcast_in_dim.17), calls=%async_computation.2 | async-start | bytes 524288 | tf_op jit(solution)/shard_map/section_mid/all_to_all | solution.py:18
  112.7 7.2 %all-to-all-done.2 = bf16[4,256,128]{2,1,0:T(8,128)(2,1)S(1)} async-done(((bf16[4,256,128]{2,1,0:T(8,128)(2,1)}), bf16[4,256,128]{2,1,0:T(8,128)(2,1)S(1)}, u32[]{:S(2)}, u32[]{:S(2)}) %all-to-all-start.2) | async-done | bytes 262176 | tf_op jit(solution)/shard_map/section_mid/all_to_all | solution.py:18
  123.3 3.5 %all-to-all-start.3 = ((bf16[4,2,256,256]{2,1,3,0:T(2,128)(2,1)}), bf16[4,2,256,256]{2,1,3,0:T(2,128)(2,1)S(1)}, u32[]{:S(2)}, u32[]{:S(2)}) async-start(bf16[4,2,256,256]{2,1,3,0:T(2,128)(2,1)} %broadcast_in_dim.18), calls=%async_computation.3 | async-start | bytes 2097152 | tf_op jit(solution)/shard_map/section_mid/all_to_all | solution.py:198
  134.5 4.3 %collective-permute-start.12 = (bf16[8,128,128]{2,1,0:T(8,128)(2,1)S(1)}, bf16[8,128,128]{2,1,0:T(8,128)(2,1)}, u32[]{:S(2)}, u32[]{:S(2)}) collective-permute-start(bf16[8,128,128]{2,1,0:T(8,128)(2,1)S(1)} %collective-permute-done.10.refs_2_), channel_id=1, source_target_pairs={{0,64},{8,456},{64,0},{72,136},{128,192},{136,72},{192,128},{200,2... | collective-permute-start | bytes 786440 | tf_op jit(solution)/shard_map/section_mid/ppermute | solution.py:48
  144.0 3.8 %collective-permute-start.14 = (bf16[8,128,128]{2,1,0:T(8,128)(2,1)}, bf16[8,128,128]{2,1,0:T(8,128)(2,1)}, u32[]{:S(2)}, u32[]{:S(2)}) collective-permute-start(bf16[8,128,128]{2,1,0:T(8,128)(2,1)} %collective-permute-done.12.refs_4_), channel_id=1, source_target_pairs={{0,448},{8,72},{64,128},{72,8},{128,64},{136,200},{192,256},{200,1... | collective-permute-start | bytes 786440 | tf_op jit(solution)/shard_map/section_mid/ppermute | solution.py:48
  157.7 6.6 %section_mid.1 = bf16[8,2,128,128]{3,2,1,0:T(8,128)(2,1)} custom-call(s32[256]{0:T(256)} %reshape.69.meta_ref, s32[128]{0:T(128)} %constant.34.clone.table_ref, s32[2]{0:T(128)} %pad_add_fusion.place_ref, bf16[8,128,128]{2,1,0:T(8,128)(2,1)} %bitcast.62, bf16[8,128,128]{2,1,0:T(8,128)(2,1)} %copy-done.6, bf16[8,128,128]{2,1,0:T(8,128)(2,1)} %copy-done.7, ...), custom_call_target="tpu_custom_call" | custom-call | tf_op jit(solution)/shard_map/section_mid/pallas_call | solution.py:121
  166.0 17.0 %all_to_all.35 = bf16[8,320,128]{2,1,0:T(8,128)(2,1)S(1)} all-to-all(bf16[8,320,128]{2,1,0:T(8,128)(2,1)S(1)} %pad_maximum_fusion), channel_id=1, replica_groups=mesh['y'=8,'zl'=4,'core'=2,'x'=4,'zh'=2] {'x','zh'}, dimensions={0} | all-to-all | bytes 1310720 | tf_op jit(solution)/shard_map/section_mid/all_to_all | solution.py:206
  183.2 14.5 %all_to_all.36 = bf16[8,64,128]{2,1,0:T(8,128)(2,1)S(1)} all-to-all(bf16[8,64,128]{2,1,0:T(8,128)(2,1)S(1)} %broadcast_in_dim.19), channel_id=1, replica_groups=mesh['y'=8,'zl'=4,'core'=2,'x'=4,'zh'=2] {'y'}, dimensions={0} | all-to-all | bytes 262144 | tf_op jit(solution)/shard_map/weight_sums/all_to_all | solution.py:18
  198.7 4.9 %all-to-all-start.6 = ((bf16[32,64,128]{2,1,0:T(8,128)(2,1)}), bf16[32,64,128]{2,1,0:T(8,128)(2,1)S(1)}, u32[]{:S(2)}, u32[]{:S(2)}) async-start(bf16[32,64,128]{2,1,0:T(8,128)(2,1)} %broadcast_in_dim.20), calls=%async_computation.6 | async-start | bytes 1048576 | tf_op jit(solution)/shard_map/weight_sums/all_to_all | solution.py:18
  203.6 9.4 %all_gather.26 = bf16[256,256]{1,0:T(8,128)(2,1)S(1)} all-gather(bf16[256,128]{1,0:T(8,128)(2,1)S(1)} %slice.30), channel_id=1, replica_groups=mesh['y'=8,'zl'=4,'core'=2,'x'=4,'zh'=2] {'core'}, dimensions={1}, use_global_device_ids=true | all-gather | bytes 196608 | tf_op jit(solution)/shard_map/section_mid/all_gather | solution.py:209
  215.0 10.8 %all_gather.27 = f32[8,2,32,256]{3,2,1,0:T(8,128)S(1)} all-gather(f32[8,2,32,128]{3,2,1,0:T(8,128)S(1)} %bitcast.66), channel_id=1, replica_groups=mesh['y'=8,'zl'=4,'core'=2,'x'=4,'zh'=2] {'core'}, dimensions={3}, use_global_device_ids=true | all-gather | bytes 786432 | tf_op jit(solution)/shard_map/weight_sums/all_gather | solution.py:219
  (94 shorter events, 60.0 us)
Async XLA Ops:
  0.6 102.9 %copy-start = (bf16[256,256]{1,0:T(8,128)(2,1)S(1)}, bf16[256,256]{1,0:T(8,128)(2,1)}, u32[]{:S(2)}) copy-start(bf16[256,256]{1,0:T(8,128)(2,1)} %param.18) | copy-start | bytes 393220
  0.7 34.3 %copy-start.12 = (s32[8,1,12]{2,1,0:T(1,128)S(1)}, s32[8,1,12]{2,1,0:T(1,128)}, u32[]{:S(2)}) copy-start(s32[8,1,12]{2,1,0:T(1,128)} %param.20) | copy-start | bytes 1156
  10.1 51.4 %collective-permute-start.5 = (bf16[8,12,128,128]{3,2,1,0:T(8,128)(2,1)}, bf16[8,12,128,128]{3,2,1,0:T(8,128)(2,1)S(1)}, u32[]{:S(2)}, u32[]{:S(2)}) collective-permute-start(bf16[8,12,128,128]{3,2,1,0:T(8,128)(2,1)} %bitcast.51), channel_id=1, source_target_pairs={{0,8},{8,0},{1,9},{9,1},{2,10},{10,2},{3,11},{11,3},{4,12},{12,4},... | collective-permute-start | bytes 9437192 | tf_op jit(solution)/shard_map/section_top/ppermute | solution.py:177
  13.1 11.3 %all-to-all-start = ((bf16[4,256,128]{2,1,0:T(8,128)(2,1)}), bf16[4,256,128]{2,1,0:T(8,128)(2,1)S(1)}, u32[]{:S(2)}, u32[]{:S(2)}) async-start(bf16[4,256,128]{2,1,0:T(8,128)(2,1)} %broadcast_in_dim.15), calls=%async_computation | async-start | bytes 524288 | tf_op jit(solution)/shard_map/section_top/all_to_all | solution.py:18
  24.4 45.4 %copy-start.4 = (bf16[4,256,128]{2,1,0:T(8,128)(2,1)}, bf16[4,256,128]{2,1,0:T(8,128)(2,1)S(1)}, u32[]{:S(2)}) copy-start(bf16[4,256,128]{2,1,0:T(8,128)(2,1)S(1)} %all-to-all-done) | copy-start | bytes 786436
  24.4 8.4 %collective-permute-start = (bf16[8,128,128]{2,1,0:T(8,128)(2,1)S(1)}, bf16[8,128,128]{2,1,0:T(8,128)(2,1)}, u32[]{:S(2)}, u32[]{:S(2)}) collective-permute-start(bf16[8,128,128]{2,1,0:T(8,128)(2,1)S(1)} %bitcast.63), channel_id=1, source_target_pairs={{0,64},{8,456},{64,0},{72,136},{128,192},{136,72},{192,128},{200,2... | collective-permute-start | bytes 786440 | tf_op jit(solution)/shard_map/section_top/ppermute | solution.py:48
  27.1 15.5 %collective-permute-start.2 = (bf16[8,128,128]{2,1,0:T(8,128)(2,1)S(1)}, bf16[8,128,128]{2,1,0:T(8,128)(2,1)}, u32[]{:S(2)}, u32[]{:S(2)}) collective-permute-start(bf16[8,128,128]{2,1,0:T(8,128)(2,1)S(1)} %bitcast.64), channel_id=1, source_target_pairs={{0,448},{8,72},{64,128},{72,8},{128,64},{136,200},{192,256},{200,1... | collective-permute-start | bytes 786440 | tf_op jit(solution)/shard_map/section_top/ppermute | solution.py:48
  32.9 13.5 %collective-permute-start.1 = (bf16[8,128,128]{2,1,0:T(8,128)(2,1)}, bf16[8,128,128]{2,1,0:T(8,128)(2,1)}, u32[]{:S(2)}, u32[]{:S(2)}) collective-permute-start(bf16[8,128,128]{2,1,0:T(8,128)(2,1)} %collective-permute-done.refs_1_), channel_id=1, source_target_pairs={{0,448},{8,72},{64,128},{72,8},{128,64},{136,200},{192,256},{200,1... | collective-permute-start | bytes 786440 | tf_op jit(solution)/shard_map/section_top/ppermute | solution.py:48
  42.6 15.0 %collective-permute-start.3 = (bf16[8,128,128]{2,1,0:T(8,128)(2,1)}, bf16[8,128,128]{2,1,0:T(8,128)(2,1)}, u32[]{:S(2)}, u32[]{:S(2)}) collective-permute-start(bf16[8,128,128]{2,1,0:T(8,128)(2,1)} %collective-permute-done.2.refs_2_), channel_id=1, source_target_pairs={{0,64},{8,456},{64,0},{72,136},{128,192},{136,72},{192,128},{200,2... | collective-permute-start | bytes 786440 | tf_op jit(solution)/shard_map/section_top/ppermute | solution.py:48
  46.3 15.2 %collective-permute-start.4 = (bf16[8,128,128]{2,1,0:T(8,128)(2,1)}, bf16[8,128,128]{2,1,0:T(8,128)(2,1)}, u32[]{:S(2)}, u32[]{:S(2)}) collective-permute-start(bf16[8,128,128]{2,1,0:T(8,128)(2,1)} %collective-permute-done.1.refs_3_), channel_id=1, source_target_pairs={{0,64},{8,456},{64,0},{72,136},{128,192},{136,72},{192,128},{200,2... | collective-permute-start | bytes 786440 | tf_op jit(solution)/shard_map/section_top/ppermute | solution.py:48
  49.1 12.4 %collective-permute-start.6 = (bf16[256,256]{1,0:T(8,128)(2,1)}, bf16[256,256]{1,0:T(8,128)(2,1)S(1)}, u32[]{:S(2)}, u32[]{:S(2)}) collective-permute-start(bf16[256,256]{1,0:T(8,128)(2,1)} %all_gather.21), channel_id=1, source_target_pairs={{0,1},{1,0},{2,3},{3,2},{4,5},{5,4},{6,7},{7,6},{8,9},{9,8},{10,11... | collective-permute-start | bytes 393224 | tf_op jit(solution)/shard_map/section_top/ppermute | solution.py:181
  57.6 7.7 %collective-permute-start.7 = (bf16[8,128,128]{2,1,0:T(8,128)(2,1)}, bf16[8,128,128]{2,1,0:T(8,128)(2,1)}, u32[]{:S(2)}, u32[]{:S(2)}) collective-permute-start(bf16[8,128,128]{2,1,0:T(8,128)(2,1)} %collective-permute-done.3.refs_4_), channel_id=1, source_target_pairs={{0,448},{8,72},{64,128},{72,8},{128,64},{136,200},{192,256},{200,1... | collective-permute-start | bytes 786440 | tf_op jit(solution)/shard_map/section_top/ppermute | solution.py:48
  62.1 7.7 %collective-permute-start.8 = (bf16[8,128,128]{2,1,0:T(8,128)(2,1)}, bf16[8,128,128]{2,1,0:T(8,128)(2,1)}, u32[]{:S(2)}, u32[]{:S(2)}) collective-permute-start(bf16[8,128,128]{2,1,0:T(8,128)(2,1)} %collective-permute-done.4.refs_5_), channel_id=1, source_target_pairs={{0,448},{8,72},{64,128},{72,8},{128,64},{136,200},{192,256},{200,1... | collective-permute-start | bytes 786440 | tf_op jit(solution)/shard_map/section_top/ppermute | solution.py:48
  76.5 21.2 %all-to-all-start.1 = ((bf16[8,256,128]{2,1,0:T(8,128)(2,1)}), bf16[8,256,128]{2,1,0:T(8,128)(2,1)S(1)}, u32[]{:S(2)}, u32[]{:S(2)}) async-start(bf16[8,256,128]{2,1,0:T(8,128)(2,1)} %bitcast.58), calls=%async_computation.1 | async-start | bytes 1048576 | tf_op jit(solution)/shard_map/section_top/all_to_all | solution.py:184
  104.5 15.4 %all-to-all-start.2 = ((bf16[4,256,128]{2,1,0:T(8,128)(2,1)}), bf16[4,256,128]{2,1,0:T(8,128)(2,1)S(1)}, u32[]{:S(2)}, u32[]{:S(2)}) async-start(bf16[4,256,128]{2,1,0:T(8,128)(2,1)} %broadcast_in_dim.17), calls=%async_computation.2 | async-start | bytes 524288 | tf_op jit(solution)/shard_map/section_mid/all_to_all | solution.py:18
  121.4 8.8 %collective-permute-start.9 = (bf16[8,128,128]{2,1,0:T(8,128)(2,1)S(1)}, bf16[8,128,128]{2,1,0:T(8,128)(2,1)S(1)}, u32[]{:S(2)}, u32[]{:S(2)}) collective-permute-start(bf16[8,128,128]{2,1,0:T(8,128)(2,1)S(1)} %bitcast.60), channel_id=1, source_target_pairs={{0,64},{8,456},{64,0},{72,136},{128,192},{136,72},{192,128},{200,2... | collective-permute-start | bytes 786440 | tf_op jit(solution)/shard_map/section_mid/ppermute | solution.py:48
  123.3 27.4 %all-to-all-start.3 = ((bf16[4,2,256,256]{2,1,3,0:T(2,128)(2,1)}), bf16[4,2,256,256]{2,1,3,0:T(2,128)(2,1)S(1)}, u32[]{:S(2)}, u32[]{:S(2)}) async-start(bf16[4,2,256,256]{2,1,3,0:T(2,128)(2,1)} %broadcast_in_dim.18), calls=%async_computation.3 | async-start | bytes 2097152 | tf_op jit(solution)/shard_map/section_mid/all_to_all | solution.py:198
  126.9 7.7 %collective-permute-start.10 = (bf16[8,128,128]{2,1,0:T(8,128)(2,1)S(1)}, bf16[8,128,128]{2,1,0:T(8,128)(2,1)S(1)}, u32[]{:S(2)}, u32[]{:S(2)}) collective-permute-start(bf16[8,128,128]{2,1,0:T(8,128)(2,1)S(1)} %bitcast.61), channel_id=1, source_target_pairs={{0,448},{8,72},{64,128},{72,8},{128,64},{136,200},{192,256},{200,1... | collective-permute-start | bytes 786440 | tf_op jit(solution)/shard_map/section_mid/ppermute | solution.py:48
  130.2 8.6 %collective-permute-start.11 = (bf16[8,128,128]{2,1,0:T(8,128)(2,1)S(1)}, bf16[8,128,128]{2,1,0:T(8,128)(2,1)S(1)}, u32[]{:S(2)}, u32[]{:S(2)}) collective-permute-start(bf16[8,128,128]{2,1,0:T(8,128)(2,1)S(1)} %collective-permute-done.9.refs_1_), channel_id=1, source_target_pairs={{0,448},{8,72},{64,128},{72,8},{128,64},{136,200},{192,256},{200,1... | collective-permute-start | bytes 786440 | tf_op jit(solution)/shard_map/section_mid/ppermute | solution.py:48
  134.5 9.5 %collective-permute-start.12 = (bf16[8,128,128]{2,1,0:T(8,128)(2,1)S(1)}, bf16[8,128,128]{2,1,0:T(8,128)(2,1)}, u32[]{:S(2)}, u32[]{:S(2)}) collective-permute-start(bf16[8,128,128]{2,1,0:T(8,128)(2,1)S(1)} %collective-permute-done.10.refs_2_), channel_id=1, source_target_pairs={{0,64},{8,456},{64,0},{72,136},{128,192},{136,72},{192,128},{200,2... | collective-permute-start | bytes 786440 | tf_op jit(solution)/shard_map/section_mid/ppermute | solution.py:48
  138.9 8.9 %collective-permute-start.13 = (bf16[8,128,128]{2,1,0:T(8,128)(2,1)S(1)}, bf16[8,128,128]{2,1,0:T(8,128)(2,1)}, u32[]{:S(2)}, u32[]{:S(2)}) collective-permute-start(bf16[8,128,128]{2,1,0:T(8,128)(2,1)S(1)} %collective-permute-done.11.refs_3_), channel_id=1, source_target_pairs={{0,64},{8,456},{64,0},{72,136},{128,192},{136,72},{192,128},{200,2... | collective-permute-start | bytes 786440 | tf_op jit(solution)/shard_map/section_mid/ppermute | solution.py:48
  144.0 10.4 %collective-permute-start.14 = (bf16[8,128,128]{2,1,0:T(8,128)(2,1)}, bf16[8,128,128]{2,1,0:T(8,128)(2,1)}, u32[]{:S(2)}, u32[]{:S(2)}) collective-permute-start(bf16[8,128,128]{2,1,0:T(8,128)(2,1)} %collective-permute-done.12.refs_4_), channel_id=1, source_target_pairs={{0,448},{8,72},{64,128},{72,8},{128,64},{136,200},{192,256},{200,1... | collective-permute-start | bytes 786440 | tf_op jit(solution)/shard_map/section_mid/ppermute | solution.py:48
  147.8 10.0 %collective-permute-start.15 = (bf16[8,128,128]{2,1,0:T(8,128)(2,1)}, bf16[8,128,128]{2,1,0:T(8,128)(2,1)}, u32[]{:S(2)}, u32[]{:S(2)}) collective-permute-start(bf16[8,128,128]{2,1,0:T(8,128)(2,1)} %collective-permute-done.13.refs_5_), channel_id=1, source_target_pairs={{0,448},{8,72},{64,128},{72,8},{128,64},{136,200},{192,256},{200,1... | collective-permute-start | bytes 786440 | tf_op jit(solution)/shard_map/section_mid/ppermute | solution.py:48
  198.7 16.3 %all-to-all-start.6 = ((bf16[32,64,128]{2,1,0:T(8,128)(2,1)}), bf16[32,64,128]{2,1,0:T(8,128)(2,1)S(1)}, u32[]{:S(2)}, u32[]{:S(2)}) async-start(bf16[32,64,128]{2,1,0:T(8,128)(2,1)} %broadcast_in_dim.20), calls=%async_computation.6 | async-start | bytes 1048576 | tf_op jit(solution)/shard_map/weight_sums/all_to_all | solution.py:18
  (11 other events, 172.0 us)
